TPU v7x, 32 devices: a whole 2x2x4 slice. The times are simulated.
32 devices in a mesh: groups: 2 (over y), space: 4 (over z), season: 2 (over x), var: 2 (over core).
Axes of the slice: x: 2, y: 2, z: 4, core: 2. Of those that a mesh axis runs over, the one named last changes fastest.
Arguments:
- right_side: float32 [64, 2, 32768], P('season', 'var', ('groups', 'space')), parts along dimension 2, may hold values from -60 to 60
- spatial: float32 [256, 3, 128, 128], P(('groups', 'space')), parts along dimension 0, as said below
- columns: int32 [256, 3], P(('groups', 'space')), parts along dimension 0, may hold values from 0 to 127, as said below
- counts: int32 [256], P(('groups', 'space')), parts along dimension 0, may hold values from 1 to 64, as said below
- season_cov: float32 [64, 2, 64, 2], replicated, as said below
Outputs:
- solution_field: float32 [64, 2, 32768], P('season', 'var', ('groups', 'space')), parts along dimension 2
- residual: float32 [64, 2, 32768], P('season', 'var', ('groups', 'space')), parts along dimension 2
There are 2 independent parts, one for each index of `groups`. A program takes and returns all parts, laid end to end along the dimension named above; an argument that names none is the same for every part. Nothing has to cross between parts.
Inputs may be any that keep to these rules, and one draw needn't show every extreme that they name: `columns`: each row's first entry is the row's own block; the second is the block before it and the third the block after it where the taper couples them, else the row's own block with an all-zero stored block. The observed seasons of a block are its last counts seasons. `spatial`: symmetric as a whole: the block stored for row i at column j is the transpose of the block stored for row j at column i, and each diagonal block is symmetric. `season_cov`: Symmetric.
All inputs are finite; a program needn't handle non-finite values.
Results may differ from a plain program's by a relative error of at most 0.015.
Values sent between devices are 32-bit elements; how exact they have to be, the bound alone decides.
No kernel may reach another device: no remote copies, remote signals or barrier semaphores. Data moves between devices by JAX's collectives and lax.ppermute only.
A program may use at most 64 MiB of HBM per device.

v0:
```python
import jax
import jax.numpy as jnp
from jax import lax
from jax.sharding import PartitionSpec as P

SEASONS = 64
VARS = 2
REACH = 1
ITERS = 2


nugget_level = 10.5


def padded_2(shard, sides, width):
    for axis, dim in sides:
        size, length = (lax.axis_size(axis), shard.shape[dim])
        up = [(i, (i + 1) % size) for i in range(size - 1)]
        down = [(j, i) for i, j in up]
        last = lax.slice_in_dim(shard, length - width, length, axis=dim)
        initial = lax.slice_in_dim(shard, 0, width, axis=dim)
        before = lax.ppermute(last, axis, up)
        after = lax.ppermute(initial, axis, down)
        shard = jnp.concatenate([before, shard, after], axis=dim)
    return shard


def residual_norm(field):
    return lax.psum(jnp.sum(field * field), ("space", "season", "var"))


def body(right_side, spatial, columns, counts, season_cov):
    season_parts = lax.axis_size("season")
    local_seasons = right_side.shape[0]
    blocks = spatial.shape[0]
    width = spatial.shape[2]
    order = SEASONS * VARS
    season_ids = lax.axis_index("season") * local_seasons + jnp.arange(
        local_seasons, dtype=jnp.int32
    )
    observed = (season_ids[:, None] >= SEASONS - counts[None, :]).astype(jnp.float32)[:, :, None]
    permuted = season_cov.reshape(
        season_parts, local_seasons, VARS, season_parts, local_seasons, VARS
    )
    permuted = permuted.transpose(0, 2, 1, 3, 5, 4).reshape(order, order)
    local_cols = columns - (lax.axis_index("space") * blocks - REACH)
    target = right_side.reshape(local_seasons, blocks, width)
    solution_field = jnp.zeros_like(target)
    residual = target
    direction = target
    norm_now = residual_norm(residual)
    for step in range(ITERS):
        masked = observed * direction
        padded = padded_2(masked, (("space", 1),), REACH)
        picked = padded[:, local_cols, :]
        moved = jnp.einsum("ikac,sikc->sia", spatial, picked, precision=lax.Precision.HIGHEST)
        owner = lax.axis_index(("season", "var"))
        my_rows = lax.dynamic_slice_in_dim(permuted, owner * local_seasons, local_seasons, 0)
        flat = moved.reshape(local_seasons, blocks * width)
        mixed = jnp.dot(
            my_rows,
            lax.all_gather(flat, ("season", "var"), axis=0, tiled=True),
            precision=lax.Precision.HIGHEST,
        )
        mixed = mixed.reshape(local_seasons, blocks, width)
        image = nugget_level * direction + observed * mixed
        alpha = norm_now / lax.psum(jnp.sum(direction * image), ("space", "season", "var"))
        solution_field = solution_field + alpha * direction
        residual = residual - alpha * image
        norm_next = residual_norm(residual)
        direction = residual + norm_next / norm_now * direction
        norm_now = norm_next
    shape_out = right_side.shape
    return (solution_field.reshape(shape_out), residual.reshape(shape_out))


def solution(mesh):
    placed = (
        P("season", "var", ("groups", "space")),
        P(("groups", "space"), None, None, None),
        P(("groups", "space"), None),
        P(("groups", "space")),
        P(),
    )
    return jax.shard_map(
        body,
        mesh=mesh,
        in_specs=placed,
        out_specs=(
            P("season", "var", ("groups", "space")),
            P("season", "var", ("groups", "space")),
        ),
        check_vma=False,
    )
```

profile of v0, /device:TPU:0, one launch (start us, length us, event | category | flops | bytes accessed | tf_op | source)
XLA Modules:
  0.0 211.5 jit_solution(10391695513650199790)
XLA Ops:
  7.2 0.7 iota_add_fusion
  7.9 1.4 copy_multiply_fusion
  9.4 4.9 %collective-permute-start = (f32[32,1,128]{2,0,1:T(8,128)S(1)}, f32[32,1,128]{2,0,1:T(8,128)S(1)}, u32[]{:S(2)}, u32[]{:S(2)}) collective-permute-start(f32[32,1,128]{2,0,1:T(8,128)S(1)} %get-tuple-element.16), channel_id=1, source_target_pairs={{0,4},{4,8},{8,12},{1,5},{5,9},{9,13},{2,6},{6,10},{10,14},{3,7},{... | collective-permute-start | bytes 49160 | tf_op jit(solution)/shard_map/ppermute | solution.py:22
  14.3 1.3 collective-permute-start.1
  15.6 0.7 compare_select_fusion
  16.5 3.4 %collective-permute-done.1 = f32[32,1,128]{2,0,1:T(8,128)S(1)} collective-permute-done((f32[32,1,128]{2,0,1:T(8,128)S(1)}, f32[32,1,128]{2,0,1:T(8,128)S(1)}, u32[]{:S(2)}, u32[]{:S(2)}) %collective-permute-start.1) | collective-permute-done | bytes 16416 | tf_op jit(solution)/shard_map/ppermute | solution.py:23
  20.0 0.7 gather_fusion
  20.7 8.7 %convolution_bitcast_fusion.1 = f32[32,4,8,128]{3,2,1,0:T(8,128)S(1)} fusion(f32[32,32,3,128]{3,0,2,1:T(8,128)S(1)} %bitcast.80, f32[32,3,128,128]{3,2,1,0:T(8,128)} %param.6), kind=kOutput, calls=%fused_computation.6 | convolution fusion | flops 603979776 | bytes 8388608 | tf_op jit(solution)/shard_map/ikac,sikc->sia/dot_general | solution.py:56
  29.5 0.8 copy.79
  30.4 0.2 reshape.89
  30.7 0.1 copy.80
  30.8 0.2 reshape.90
  31.1 1.7 multiply_reduce_fusion.3
  32.7 20.6 %all-gather.3.cloned.1.call-done = f32[128,4096]{1,0:T(8,128)} async-done(((f32[32,4096]{1,0:T(8,128)}), f32[128,4096]{1,0:T(8,128)}) %all-gather.3.cloned.1.call-update) | async-done | bytes 2097168 | tf_op jit(solution)/shard_map/all_gather | solution.py:62
  53.3 0.2 mul.135.clone
  53.5 3.9 %multiply_reduce_fusion.2 = (f32[]{:T(128)}, f32[32,4096]{1,0:T(8,128)S(1)}) fusion(f32[4,8,32,128]{3,2,1,0:T(8,128)S(1)} %bitcast.81, f32[32,1,4096]{2,1,0:T(1,128)S(1)} %copy-done, f32[128,4096]{1,0:T(8,128)} %all-gather.3.cloned.1.call-done, f32[128,128]{1,0:T(8,128)S(1)} %reshape.90, s32[]{:T(128)S(6)} %select_n.8), kind=kOutput, calls=%fused_computation.26 | convolution fusion | flops 201981952 | bytes 3686408 | tf_op jit(solution)/shard_map/dot_general | solution.py:60
  57.4 33.3 %all-reduce = (f32[]{:T(128)}, f32[]{:T(128)}) all-reduce(f32[]{:T(128)} %multiply_reduce_fusion.3, f32[]{:T(128)} %get-tuple-element.18), channel_id=1, replica_groups=mesh['groups'=2,'space'=4,'season'=2,'var'=2] {'space','season','var'}, use_global_device_ids=true, to_apply=%region_1.0 | all-reduce | flops 2 | bytes 16 | tf_op jit(solution)/shard_map/psum | solution.py:29
  92.0 2.1 multiply_reduce_fusion.1
  94.1 30.1 %psum.30 = f32[]{:T(128)} all-reduce(f32[]{:T(128)} %get-tuple-element.10), channel_id=1, replica_groups=mesh['groups'=2,'space'=4,'season'=2,'var'=2] {'space','season','var'}, use_global_device_ids=true, to_apply=%region_5.0 | all-reduce | flops 1 | bytes 8 | tf_op jit(solution)/shard_map/psum | solution.py:29
  125.5 0.4 fusion.8
  125.9 1.3 collective-permute-start.2
  127.2 1.5 collective-permute-start.3
  128.7 4.1 %collective-permute-done.3 = f32[32,1,128]{2,0,1:T(8,128)S(1)} collective-permute-done((f32[32,1,128]{2,0,1:T(8,128)S(1)}, f32[32,1,128]{2,0,1:T(8,128)S(1)}, u32[]{:S(2)}, u32[]{:S(2)}) %collective-permute-start.3) | collective-permute-done | bytes 16416 | tf_op jit(solution)/shard_map/ppermute | solution.py:23
  132.9 0.7 gather_fusion.1
  133.6 8.7 %convolution_bitcast_fusion = f32[32,4,8,128]{3,2,1,0:T(8,128)S(1)} fusion(f32[32,32,3,128]{3,0,2,1:T(8,128)S(1)} %bitcast.79, f32[32,3,128,128]{3,2,1,0:T(8,128)} %param.6), kind=kOutput, calls=%fused_computation.5 | convolution fusion | flops 603979776 | bytes 8388608 | tf_op jit(solution)/shard_map/ikac,sikc->sia/dot_general | solution.py:56
  142.4 0.8 copy.78
  143.2 20.0 %all-gather.5.cloned.1.call-done = f32[128,4096]{1,0:T(8,128)} async-done(((f32[32,4096]{1,0:T(8,128)}), f32[128,4096]{1,0:T(8,128)}) %all-gather.5.cloned.1.call-update) | async-done | bytes 2097168 | tf_op jit(solution)/shard_map/all_gather | solution.py:62
  163.2 3.9 %multiply_reduce_fusion = (f32[]{:T(128)}, f32[32,1,4096]{2,0,1:T(8,128)S(1)}) fusion(f32[32,1,4096]{2,0,1:T(8,128)S(1)} %copy-done.1, f32[32,1,4096]{2,1,0:T(1,128)S(1)} %copy-done, f32[]{:T(128)S(6)} %div.10, f32[128,4096]{1,0:T(8,128)} %all-gather.5.cloned.1.call-done, f32[128,128]{1,0:T(8,128)S(1)} %reshape.90, s32[]{:T(128)S(6)} %select_n.8, ...), kind=kOutput, calls=%fused_computation.22 | convolution fusion | flops 202244096 | bytes 4210700 | tf_op jit(solution)/shard_map/dot_general | solution.py:60
  167.1 33.3 %psum.31 = f32[]{:T(128)} all-reduce(f32[]{:T(128)} %get-tuple-element.20), channel_id=1, replica_groups=mesh['groups'=2,'space'=4,'season'=2,'var'=2] {'space','season','var'}, use_global_device_ids=true, to_apply=%region_7.0 | all-reduce | flops 1 | bytes 8 | tf_op jit(solution)/shard_map/psum | solution.py:67
  201.6 0.4 multiply_subtract_fusion
  202.0 1.3 copy.46
  203.4 1.3 copy.45
  (21 shorter events, 0.6 us)
Async XLA Ops:
  7.2 46.1 %all-gather.3.cloned.1.call-start = ((), (), s32[]{:S(2)}) async-start(), calls=%async_computation | async-start | bytes 2621440 | tf_op jit(solution)/shard_map/all_gather | solution.py:62
  9.4 7.1 %collective-permute-start = (f32[32,1,128]{2,0,1:T(8,128)S(1)}, f32[32,1,128]{2,0,1:T(8,128)S(1)}, u32[]{:S(2)}, u32[]{:S(2)}) collective-permute-start(f32[32,1,128]{2,0,1:T(8,128)S(1)} %get-tuple-element.16), channel_id=1, source_target_pairs={{0,4},{4,8},{8,12},{1,5},{5,9},{9,13},{2,6},{6,10},{10,14},{3,7},{... | collective-permute-start | bytes 49160 | tf_op jit(solution)/shard_map/ppermute | solution.py:22
  14.3 5.6 %collective-permute-start.1 = (f32[32,1,128]{2,0,1:T(8,128)S(1)}, f32[32,1,128]{2,0,1:T(8,128)S(1)}, u32[]{:S(2)}, u32[]{:S(2)}) collective-permute-start(f32[32,1,128]{2,0,1:T(8,128)S(1)} %get-tuple-element.17), channel_id=1, source_target_pairs={{4,0},{8,4},{12,8},{5,1},{9,5},{13,9},{6,2},{10,6},{14,10},{7,3},{... | collective-permute-start | bytes 49160 | tf_op jit(solution)/shard_map/ppermute | solution.py:23
  20.7 9.7 %copy-start.2 = (f32[64,2,64,2]{2,3,1,0:T(2,128)S(1)}, f32[64,2,64,2]{2,3,1,0:T(2,128)}, u32[]{:S(2)}) copy-start(f32[64,2,64,2]{2,3,1,0:T(2,128)} %param.9) | copy-start | bytes 196612
  29.4 1.6 copy-start
  30.3 132.9 %all-gather.5.cloned.1.call-start = ((), (), s32[]{:S(2)}) async-start(), calls=%async_computation.1 | async-start | bytes 2621440 | tf_op jit(solution)/shard_map/all_gather | solution.py:62
  125.9 2.8 %collective-permute-start.2 = (f32[32,1,128]{2,0,1:T(8,128)S(1)}, f32[32,1,128]{2,0,1:T(8,128)S(1)}, u32[]{:S(2)}, u32[]{:S(2)}) collective-permute-start(f32[32,1,128]{2,0,1:T(8,128)S(1)} %get-tuple-element.14), channel_id=1, source_target_pairs={{0,4},{4,8},{8,12},{1,5},{5,9},{9,13},{2,6},{6,10},{10,14},{3,7},{... | collective-permute-start | bytes 49160 | tf_op jit(solution)/shard_map/ppermute | solution.py:22
  127.2 5.6 %collective-permute-start.3 = (f32[32,1,128]{2,0,1:T(8,128)S(1)}, f32[32,1,128]{2,0,1:T(8,128)S(1)}, u32[]{:S(2)}, u32[]{:S(2)}) collective-permute-start(f32[32,1,128]{2,0,1:T(8,128)S(1)} %get-tuple-element.15), channel_id=1, source_target_pairs={{4,0},{8,4},{12,8},{5,1},{9,5},{13,9},{6,2},{10,6},{14,10},{7,3},{... | collective-permute-start | bytes 49160 | tf_op jit(solution)/shard_map/ppermute | solution.py:23
  133.6 29.6 %copy-start.1 = (f32[32,1,4096]{2,0,1:T(8,128)S(1)}, f32[32,1,4096]{2,0,1:T(8,128)}, u32[]{:S(2)}) copy-start(f32[32,1,4096]{2,0,1:T(8,128)} %get-tuple-element.11) | copy-start | bytes 1572868
Sparse Core Ops, SparseCore 0:
  30.4 22.8 all-gather.2
  143.3 19.8 all-gather.4
where the time goes:
time: 212 us
  blocking collectives  96.7 us (46%)
  waiting for transfers between devices  48.1 us (23%)
  matrix products  25.2 us (12%)
  between operations  18.2 us (9%)
  starting transfers between devices  9.06 us (4%)
  other arithmetic  7.43 us (4%)
  local copies, waits for them, and re-layouts  6.86 us (3%)
    psum x2, blocking collectives, residual_norm(): return lax.psum(jnp.sum(field * field), ('space', 'season', 'var'))  63.4 us
    all_gather x2, waiting for transfers between devices, body(): lax.all_gather(flat, ('season', 'var'), axis=0, tiled=True)  40.5 us
    psum x1, blocking collectives, body(): lax.psum(jnp.sum(direction * image), ('space', 'season', 'var'))  33.3 us
    dot_general x2, matrix products, body(): jnp.einsum('ikac,sikc->sia', spatial, picked, precision=lax.Precision.HIG...  17.5 us
    dot_general x2, matrix products, body(): jnp.dot(my_rows, lax.all_gather(flat, ('season', 'var'), axis=0, tiled=Tr...  7.76 us
    ppermute x2, waiting for transfers between devices, padded_2(): after = lax.ppermute(initial, axis, down)  7.56 us
    ppermute x2, starting transfers between devices, padded_2(): before = lax.ppermute(last, axis, up)  6.22 us
  transfers between devices with their start and end apart: 6, of which 4 were waited for; matrix products, arithmetic and copies ran while one was open for 2% of the time, Pallas kernels for 0%

commit v1 on v0

v1 whole, which is shorter than its diff:
```python
import functools

import jax
import jax.numpy as jnp
from jax import lax
from jax.experimental import pallas as pl
from jax.experimental.pallas import tpu as pltpu
from jax.sharding import PartitionSpec as P

SEASONS = 64
VARS = 2
ORDER = SEASONS * VARS
REACH = 1
NUGGET = 10.5
CUTS = (12, 24)

F32 = jnp.float32
BF16 = jnp.bfloat16
NT = (((1,), (1,)), ((), ()))
NN = (((1,), (0,)), ((), ()))
VMEM = pltpu.VMEM


def dot(a, b, dims):
    return lax.dot_general(a, b, dims, preferred_element_type=F32)


def halves(x):
    high = x.astype(BF16)
    return high, (x - high.astype(F32)).astype(BF16)


def fold(x):
    return jnp.sum(x.reshape(x.shape[0] // 8, 8, x.shape[1]), axis=0)


def pack_kernel(cuts, x_ref, *out_refs):
    blocks = cuts[-1]
    seasons = x_ref.shape[0] // blocks
    for ref, first, last in zip(out_refs, cuts[:-1], cuts[1:]):
        for j in range(first, last):
            ref[j - first] = x_ref[pl.ds(j, seasons, stride=blocks), :]


def pack(x, cuts):
    blocks = cuts[-1]
    seasons, width = x.shape[0] // blocks, x.shape[1]
    return pl.pallas_call(
        functools.partial(pack_kernel, cuts),
        out_shape=[
            jax.ShapeDtypeStruct((last - first, seasons, width), F32)
            for first, last in zip(cuts[:-1], cuts[1:])
        ],
        name="pack",
    )(x)


def prepare_kernel(w_ref, r_ref, w2_ref, rh_ref, rl_ref, scale_ref, top_ref):
    step = pl.program_id(0)

    @pl.when(step == 0)
    def _():
        top_ref[...] = jnp.zeros_like(top_ref)

    width = w_ref.shape[2]
    top = top_ref[...]
    for i in range(w_ref.shape[0]):
        for place, slot in enumerate((1, 0, 2)):
            w = w_ref[i, slot]
            high, low = halves(w)
            lanes = slice(place * width, (place + 1) * width)
            w2_ref[i, :width, lanes] = high
            w2_ref[i, width:, lanes] = low
            top = jnp.maximum(top, jnp.max(jnp.abs(w).reshape(-1, 8, width), axis=0))
    top_ref[...] = top

    @pl.when(step == pl.num_programs(0) - 1)
    def _():
        space_top = jnp.max(jnp.max(top, axis=0, keepdims=True), axis=1, keepdims=True)
        r = r_ref[...]
        season_top = jnp.max(jnp.max(jnp.abs(r), axis=0, keepdims=True), axis=1, keepdims=True)
        space_top = jnp.where(space_top > 0, space_top, 1.0)
        season_top = jnp.where(season_top > 0, season_top, 1.0)
        high, low = halves(r / season_top / space_top)
        rh_ref[...] = high
        rl_ref[...] = low
        rows = lax.broadcasted_iota(jnp.int32, scale_ref.shape, 0)
        scale_ref[...] = jnp.where(rows == 4, space_top, jnp.where(rows == 5, season_top, 0.0))


def prepare(spatial, season):
    blocks, slots, width, _ = spatial.shape
    rows = 4
    return pl.pallas_call(
        prepare_kernel,
        grid=(blocks // rows,),
        in_specs=[
            pl.BlockSpec((rows, slots, width, width), lambda i: (i, 0, 0, 0)),
            pl.BlockSpec((ORDER, ORDER), lambda i: (0, 0)),
        ],
        out_specs=[
            pl.BlockSpec((rows, 2 * width, slots * width), lambda i: (i, 0, 0)),
            pl.BlockSpec((ORDER, ORDER), lambda i: (0, 0)),
            pl.BlockSpec((ORDER, ORDER), lambda i: (0, 0)),
            pl.BlockSpec((8, 128), lambda i: (0, 0)),
        ],
        out_shape=[
            jax.ShapeDtypeStruct((blocks, 2 * width, slots * width), BF16),
            jax.ShapeDtypeStruct((ORDER, ORDER), BF16),
            jax.ShapeDtypeStruct((ORDER, ORDER), BF16),
            jax.ShapeDtypeStruct((8, 128), F32),
        ],
        scratch_shapes=[VMEM((8, width), F32)],
        name="prepare",
    )(spatial, season)


def make_plan(cuts):
    blocks = cuts[-1]
    stages = []
    have_x, have_1, have_2 = set(), set(), set()
    count = len(cuts) - 1
    for m in range(count):
        new = list(range(cuts[m], cuts[m + 1]))
        if m == count - 1:
            new = new + [-2, -1, blocks, blocks + 1]
        have_x |= set(new)
        ones = [
            i for i in range(-1, blocks + 1)
            if i not in have_1 and {i - 1, i, i + 1} <= have_x
        ]
        have_1 |= set(ones)
        twos = [
            i for i in range(blocks) if i not in have_2 and {i - 1, i, i + 1} <= have_1
        ]
        have_2 |= set(twos)
        later_1 = [i for i in range(-1, blocks + 1) if i not in have_1]
        later_2 = [i for i in range(blocks) if i not in have_2]
        keep_x = sorted({i + d for i in later_1 for d in (-1, 0, 1)} & have_x)
        keep_1 = sorted({i + d for i in later_2 for d in (-1, 0, 1)} & have_1)
        stages.append((new, ones, twos, keep_x, keep_1))
    return stages


def runs(ids, most):
    groups = []
    for i in ids:
        if groups and len(groups[-1]) < most:
            groups[-1].append(i)
        else:
            groups.append([i])
    return groups


def make_stage(plan, m, blocks, seasons, width, slots):
    new, ones, twos, keep_x, keep_1 = plan[m]
    first, last = m == 0, m == len(plan) - 1
    old_x, old_1 = ([], []) if first else (plan[m - 1][3], plan[m - 1][4])
    x_at = {i: n for n, i in enumerate(list(old_x) + list(new))}
    one_at = {i: n for n, i in enumerate(list(old_1) + list(ones))}
    inner_ones = [i for i in ones if 0 <= i < blocks]

    def kernel(*refs):
        refs = list(refs)

        def take(n):
            out = refs[:n]
            del refs[:n]
            return out

        (place_ref,) = take(1)
        field_refs = take(slots)
        w2_ref, rh_ref, rl_ref, count_ref, sums_in = take(5)
        if not first:
            old_xh, old_xl, old_1h, old_1l = take(4)
        if last:
            wide_ref, edge_ref = take(2)
        sums_out, own_1, own_2 = take(3)
        if not last:
            keep_xh, keep_xl, keep_1h, keep_1l = take(4)
        xh, xl, oh, ol, pick = take(5)

        def count_row(i):
            if 0 <= i < blocks:
                return count_ref[i : i + 1, :]
            at = i + 2 if i < 0 else i - blocks + 2
            return edge_ref[at : at + 1, :]

        def iota(rows):
            return lax.broadcasted_iota(jnp.int32, (rows, width), 0)

        season = lax.rem(iota(ORDER), SEASONS).astype(F32)

        def masked(i, value):
            return jnp.where(season >= SEASONS - count_row(i), value, 0.0)

        for n in range(len(old_x)):
            xh[n] = old_xh[n]
            xl[n] = old_xl[n]
        for n in range(len(old_1)):
            oh[n] = old_1h[n]
            ol[n] = old_1l[n]

        total_0 = sums_in[0]
        for k in range(slots):
            at = pl.multiple_of(place_ref[k], seasons)
            piece_season = (iota(seasons) + lax.rem(at, SEASONS)).astype(F32)
            for n, i in enumerate(new):
                piece = field_refs[k][n]
                if 0 <= i < blocks:
                    total_0 += fold(piece * piece)
                seen = piece_season >= SEASONS - count_row(i)
                high, low = halves(jnp.where(seen, piece, 0.0))
                xh[x_at[i], pl.ds(at, seasons), :] = high
                xl[x_at[i], pl.ds(at, seasons), :] = low
        sums_out[0] = total_0

        def space(i, high, low, at):
            if 0 <= i < blocks:
                hs = jnp.concatenate([high[at[i + d]] for d in (-1, 0, 1)], axis=1)
                ls = jnp.concatenate([low[at[i + d]] for d in (-1, 0, 1)], axis=1)
                both = dot(hs, w2_ref[i], NT)
                return both[:, :width] + both[:, width:] + dot(ls, w2_ref[i, :width, :], NT)
            e, inner, far = (0, 0, -2) if i < 0 else (1, blocks - 1, blocks + 1)
            lanes = slice(0, width) if i < 0 else slice(2 * width, 3 * width)
            near_high = w2_ref[inner, :width, lanes]
            total = dot(high[at[inner]], near_high, NN)
            total += dot(high[at[inner]], w2_ref[inner, width:, lanes], NN)
            total += dot(low[at[inner]], near_high, NN)
            for slot, j in enumerate((i, far)):
                wh, wl = halves(wide_ref[e, slot * width : (slot + 1) * width, :])
                total += dot(high[at[j]], wh, NT) + dot(high[at[j]], wl, NT)
                total += dot(low[at[j]], wh, NT)
            return total

        def mix(parts):
            zh, zl = halves(jnp.concatenate(parts, axis=1))
            lhs = jnp.concatenate([rh_ref[...], rh_ref[...], rl_ref[...]], axis=1)
            return dot(lhs, jnp.concatenate([zh, zl, zh], axis=0), NN)

        own = pl.multiple_of(place_ref[slots], seasons)
        total_1, total_2, total_3 = sums_in[1], sums_in[2], sums_in[3]
        for group in runs(ones, 4):
            mixed = mix([space(i, xh, xl, x_at) for i in group])
            for n, i in enumerate(group):
                one = masked(i, mixed[:, n * width : (n + 1) * width])
                high, low = halves(one)
                oh[one_at[i]] = high
                ol[one_at[i]] = low
                if 0 <= i < blocks:
                    x = xh[x_at[i]].astype(F32) + xl[x_at[i]].astype(F32)
                    total_1 += fold(x * one)
                    total_2 += fold(one * one)
                    n_own = inner_ones.index(i)
                    pick[n_own] = one
                    own_1[n_own] = pick[n_own, pl.ds(own, seasons), :]
        sums_out[1] = total_1
        sums_out[2] = total_2
        for group in runs(twos, 4):
            mixed = mix([space(i, oh, ol, one_at) for i in group])
            for n, i in enumerate(group):
                two = masked(i, mixed[:, n * width : (n + 1) * width])
                one = oh[one_at[i]].astype(F32) + ol[one_at[i]].astype(F32)
                total_3 += fold(one * two)
                n_own = len(inner_ones) + twos.index(i)
                pick[n_own] = two
                own_2[twos.index(i)] = pick[n_own, pl.ds(own, seasons), :]
        sums_out[3] = total_3
        if not last:
            for n, i in enumerate(keep_x):
                keep_xh[n] = xh[x_at[i]]
                keep_xl[n] = xl[x_at[i]]
            for n, i in enumerate(keep_1):
                keep_1h[n] = oh[one_at[i]]
                keep_1l[n] = ol[one_at[i]]

    tile = (ORDER, width)
    outs = [
        jax.ShapeDtypeStruct((4, 8, width), F32),
        jax.ShapeDtypeStruct((len(inner_ones), seasons, width), F32),
        jax.ShapeDtypeStruct((len(twos), seasons, width), F32),
    ]
    if not last:
        outs += [jax.ShapeDtypeStruct((len(keep_x),) + tile, BF16)] * 2
        outs += [jax.ShapeDtypeStruct((len(keep_1),) + tile, BF16)] * 2
    scratch = [VMEM((len(x_at),) + tile, BF16)] * 2 + [VMEM((len(one_at),) + tile, BF16)] * 2
    scratch += [VMEM((len(inner_ones) + len(twos),) + tile, F32)]
    return kernel, outs, scratch


def run_stage(plan, m, blocks, seasons, width, fields, *operands):
    kernel, outs, scratch = make_stage(plan, m, blocks, seasons, width, len(fields))
    place, rest = operands[0], operands[1:]
    count = len(fields) + len(rest)
    return pl.pallas_call(
        kernel,
        in_specs=[pl.BlockSpec(memory_space=pltpu.SMEM)]
        + [pl.BlockSpec(memory_space=VMEM)] * count,
        out_shape=outs,
        scratch_shapes=scratch,
        compiler_params=pltpu.CompilerParams(vmem_limit_bytes=40 << 20),
        name="stage",
    )(place, *fields, *rest)


def finish_kernel(plan, blocks, gathered_ref, x_ref, *refs):
    count = len(plan)
    ones, twos = refs[:count], refs[count : 2 * count]
    x_out, r_out = refs[2 * count :]
    seasons = x_ref.shape[0] // blocks

    def total(v):
        return jnp.sum(v, axis=1, keepdims=True)

    tuples = [gathered_ref[j] for j in range(gathered_ref.shape[0])]
    top = functools.reduce(jnp.maximum, [t[4:5] for t in tuples])
    sums = [0.0, 0.0, 0.0, 0.0]
    for t in tuples:
        ratio = t[4:5] / top
        factor = jnp.ones_like(ratio)
        for n in range(4):
            sums[n] = sums[n] + t[n : n + 1] * factor
            factor = factor * ratio
    m0, m1, m2, m3 = [total(v) for v in sums]
    scale = (top * tuples[0][5:6])[:, :1]
    mine = (tuples[0][4:5] / top)[:, :1]

    first = NUGGET * m0 + scale * m1
    alpha = m0 / first
    lead = alpha * scale
    mean = m1 / m0
    fresh = lead * lead * (m2 - mean * m1)
    c = lead * mean + fresh / m0
    dd = c * c * m0 - 2.0 * c * lead * m1 + lead * lead * m2
    dkd = c * c * m1 - 2.0 * c * lead * m2 + lead * lead * m3
    alpha_2 = fresh / (NUGGET * dd + scale * dkd)
    x_0 = alpha + alpha_2 * c
    x_1 = -alpha_2 * lead * mine
    r_0 = lead * mean - NUGGET * alpha_2 * c
    r_1 = (NUGGET * alpha_2 * lead - lead - alpha_2 * scale * c) * mine
    r_2 = alpha_2 * scale * lead * mine * mine

    where_1, where_2 = {}, {}
    for m, (_, one_ids, two_ids, _, _) in enumerate(plan):
        inner = [i for i in one_ids if 0 <= i < blocks]
        where_1.update({i: (m, n) for n, i in enumerate(inner)})
        where_2.update({i: (m, n) for n, i in enumerate(two_ids)})
    for i in range(blocks):
        rows = pl.ds(i, seasons, stride=blocks)
        x = x_ref[rows, :]
        m, n = where_1[i]
        one = ones[m][n]
        m, n = where_2[i]
        two = twos[m][n]
        x_out[rows, :] = x_0 * x + x_1 * one
        r_out[rows, :] = r_0 * x + r_1 * one + r_2 * two


def finish(plan, blocks, gathered, x, ones, twos):
    return pl.pallas_call(
        functools.partial(finish_kernel, plan, blocks),
        out_shape=[jax.ShapeDtypeStruct(x.shape, F32)] * 2,
        name="finish",
    )(gathered, x, *ones, *twos)


def from_season(value, step):
    size = lax.axis_size("season")
    return lax.ppermute(value, "season", [((i + step) % size, i) for i in range(size)])


def from_var(value):
    return lax.ppermute(value, "var", [(0, 1), (1, 0)])


def gather_space(value):
    size = lax.axis_size("space")
    if size & (size - 1):
        me = lax.axis_index("space")
        return jnp.roll(lax.all_gather(value, "space", axis=0, tiled=True), -me, axis=0)
    have = value
    hop = 1
    while hop < size:
        other = lax.ppermute(have, "space", [(i, i ^ hop) for i in range(size)])
        have = jnp.concatenate([have, other], axis=0)
        hop *= 2
    return have


def body(right_side, spatial, columns, counts, season_cov):
    del columns
    seasons = right_side.shape[0]
    blocks, _, width, _ = spatial.shape
    parts = lax.axis_size("season")
    cuts = (0,) + tuple(c for c in CUTS if c < blocks) + (blocks,)
    plan = make_plan(cuts)

    x = right_side.reshape(seasons * blocks, width)
    packs = list(pack(x, cuts))

    count_rows = jnp.broadcast_to(counts.astype(F32)[:, None], (blocks, width))
    size = lax.axis_size("space")

    def message(own, slots, ids):
        slab = x.reshape(seasons, blocks, width)[:, ids[0] : ids[1] + 1].transpose(1, 0, 2)
        tail = jnp.concatenate(
            [count_rows[ids[0] : ids[1] + 1], jnp.zeros((6, width), F32)], axis=0
        )
        wide = jnp.concatenate([spatial[own, slot] for slot in slots], axis=0)
        return jnp.concatenate([slab.reshape(2 * seasons, width), wide, tail], axis=0)

    up = [(i, i + 1) for i in range(size - 1)]
    down = [(i + 1, i) for i in range(size - 1)]
    below = lax.ppermute(message(blocks - 1, (0, 1), (blocks - 2, blocks - 1)), "space", up)
    above = lax.ppermute(message(0, (0, 2), (0, 1)), "space", down)
    halo = jnp.concatenate([below[: 2 * seasons], above[: 2 * seasons]], axis=0)
    halo = halo.reshape(4, seasons, width)
    wide_rows = slice(2 * seasons, 2 * seasons + 2 * width)
    wide = jnp.stack([below[wide_rows], above[wide_rows]])
    last_rows = 2 * seasons + 2 * width
    edge = jnp.concatenate(
        [
            below[last_rows : last_rows + 2],
            above[last_rows : last_rows + 2],
            jnp.zeros((4, width), F32),
        ],
        axis=0,
    )
    packs[-1] = jnp.concatenate([packs[-1], halo], axis=0)

    fields = []
    for part in packs:
        held = [part] + [from_season(part, d) for d in range(1, parts)]
        fields.append([v for h in held for v in (h, from_var(h))])
    me_season, me_var = lax.axis_index("season"), lax.axis_index("var")
    places = [
        (me_var ^ w) * SEASONS + lax.rem(me_season + d, parts) * seasons
        for d in range(parts)
        for w in range(VARS)
    ]
    place = jnp.stack(places + [places[0]]).astype(jnp.int32)

    season = season_cov.transpose(1, 0, 3, 2).reshape(ORDER, ORDER)
    w2, rh, rl, scale = prepare(spatial, season)

    sums = jnp.zeros((4, 8, width), F32)
    ones, twos, kept = [], [], []
    for m in range(len(plan)):
        extra = [wide, edge] if m == len(plan) - 1 else []
        out = run_stage(
            plan, m, blocks, seasons, width, fields[m],
            place, w2, rh, rl, count_rows, sums, *kept, *extra,
        )
        sums, one, two, kept = out[0], out[1], out[2], list(out[3:])
        ones.append(one)
        twos.append(two)
    tile = jnp.concatenate([jnp.sum(sums, axis=1), scale[4:]], axis=0)[None]
    gathered = gather_space(tile)
    x_out, r_out = finish(plan, blocks, gathered, x, ones, twos)
    return x_out.reshape(right_side.shape), r_out.reshape(right_side.shape)


def solution(mesh):
    field = P("season", "var", ("groups", "space"))
    return jax.shard_map(
        body,
        mesh=mesh,
        in_specs=(
            field,
            P(("groups", "space"), None, None, None),
            P(("groups", "space"), None),
            P(("groups", "space")),
            P(),
        ),
        out_specs=(field, field),
        check_vma=False,
    )
```

time: 212 us -> 65.3 us (0.31)
  blocking collectives: 96.7 us -> 0 us
  waiting for transfers between devices: 48.1 us -> 8.08 us
  Pallas kernels: 0 us -> 26.5 us
  matrix products: 25.2 us -> 0 us
  between operations: 18.2 us -> 0.88 us
  starting transfers between devices: 9.06 us -> 16.5 us
  other arithmetic: 7.43 us -> 1.4 us
  local copies, waits for them, and re-layouts: 6.86 us -> 11.2 us
    psum x3 -> x0, blocking collectives: 96.7 us -> none  [the longest x2 63.4 us: residual_norm(): return lax.psum(jnp.sum(field * field), ('space', 'season', 'var'))]
    all_gather x2 -> x0, waiting for transfers between devices: 40.5 us -> none  [body(): lax.all_gather(flat, ('season', 'var'), axis=0, tiled=True)]
    pallas_call x0 -> x6, Pallas kernels: none -> 26.5 us  [the longest x3 12.5 us: run_stage(): pl.pallas_call(kernel, in_specs=[pl.BlockSpec(memory_space=pltpu.SMEM)] +...]
    dot_general x4 -> x0, matrix products: 25.2 us -> none  [the longest x2 17.5 us: body(): jnp.einsum('ikac,sikc->sia', spatial, picked, precision=lax.Precision.HIG...]
    ppermute x4 -> x13, starting transfers between devices: 8.98 us -> 16.5 us  [the longest x2 5.74 us: gather_space(): other = lax.ppermute(have, 'space', [(i, i ^ hop) for i in range(size)])]
    reduce_sum x2 -> x1, other arithmetic: 3.77 us -> 0.02 us  [body(): tile = jnp.concatenate([jnp.sum(sums, axis=1), scale[4:]], axis=0)[None]]
    unnamed x9 -> x26, local copies, waits for them, and re-layouts: 2.76 us -> 6.33 us
    ppermute x4 -> x13, waiting for transfers between devices: 7.57 us -> 8.08 us  [the longest x3 4.84 us: from_season(): lax.ppermute(value, 'season', [((i + step) % size, i) for i in range(size)])]
  transfers between devices with their start and end apart: 6 -> 13, of which waited for: 4 -> 3; matrix products, arithmetic and copies ran while one was open for 2% -> 4% of each run, Pallas kernels for 0% -> 28%
where the time goes in v1:
time: 65.3 us; the launch traced here: 64.6 us
  Pallas kernels  26.5 us (41%)
  starting transfers between devices  16.5 us (25%)
  local copies, waits for them, and re-layouts  11.2 us (17%)
  waiting for transfers between devices  8.08 us (12%)
  other arithmetic  1.4 us (2%)
  between operations  0.88 us (1%)
    pallas_call x3, Pallas kernels, run_stage(): pl.pallas_call(kernel, in_specs=[pl.BlockSpec(memory_space=pltpu.SMEM)] +...  12.5 us
    pallas_call x1, Pallas kernels, prepare(): pl.pallas_call(prepare_kernel, grid=(blocks // rows,), in_specs=[pl.Block...  8.32 us
    unnamed x26, local copies, waits for them, and re-layouts  6.33 us
    ppermute x2, starting transfers between devices, gather_space(): other = lax.ppermute(have, 'space', [(i, i ^ hop) for i in range(size)])  5.74 us
    ppermute x1, starting transfers between devices, body(): lax.ppermute(message(blocks - 1, (0, 1), (blocks - 2, blocks - 1)), 'spac...  4.93 us
    ppermute x3, waiting for transfers between devices, from_season(): lax.ppermute(value, 'season', [((i + step) % size, i) for i in range(size)])  4.84 us
    pallas_call x1, Pallas kernels, finish(): pl.pallas_call(functools.partial(finish_kernel, plan, blocks), out_shape=...  3.67 us
    ppermute x3, starting transfers between devices, from_season(): lax.ppermute(value, 'season', [((i + step) % size, i) for i in range(size)])  3.63 us
  transfers between devices with their start and end apart: 13, of which 3 were waited for; matrix products, arithmetic and copies ran while one was open for 4% of the time, Pallas kernels for 28%

profile of v1, /device:TPU:0, one launch (start us, length us, event | category | flops | bytes accessed | tf_op | source)
XLA Modules:
  0.0 64.6 jit_solution(16534388835930082733)
XLA Ops:
  0.6 0.7 %convert_element_type.3 = f32[32]{0:T(128)S(1)} convert(s32[32]{0:T(128)} %param.7) | non-fusion elementwise | flops 32 | bytes 256 | tf_op jit(solution)/shard_map/convert_element_type | solution.py:401
  1.3 1.0 %slice_bitcast_fusion.4 = (f32[128,128]{1,0:T(8,128)S(1)}, f32[128,128]{1,0:T(8,128)S(1)}, f32[128,128]{1,0:T(8,128)S(1)}, f32[128,128]{1,0:T(8,128)S(1)}) fusion(f32[32,3,128,128]{3,2,1,0:T(8,128)} %w_ref.1), kind=kLoop, calls=%fused_computation.7 | loop fusion | bytes 524288 | tf_op jit(solution)/shard_map/squeeze | solution.py:409
  2.3 1.0 %fusion = (f32[32,2,128]{2,1,0:T(2,128)S(1)}, f32[32,2,128]{2,1,0:T(2,128)S(1)}) fusion(f32[32,32,128]{2,1,0:T(8,128)} %bitcast.30), kind=kLoop, calls=%fused_computation.13 | loop fusion | bytes 131072 | tf_op jit(solution)/shard_map/slice | solution.py:405
  3.4 4.9 %collective-permute-start = (f32[328,128]{1,0:T(8,128)S(1)}, f32[328,128]{1,0:T(8,128)S(1)}, u32[]{:S(2)}, u32[]{:S(2)}) collective-permute-start(f32[328,128]{1,0:T(8,128)S(1)} %concatenate.25), channel_id=1, source_target_pairs={{0,4},{4,8},{8,12},{1,5},{5,9},{9,13},{2,6},{6,10},{10,14},{3,7},{... | collective-permute-start | bytes 503816 | tf_op jit(solution)/shard_map/ppermute | solution.py:414
  8.5 1.3 %collective-permute-start.1 = (f32[328,128]{1,0:T(8,128)S(1)}, f32[328,128]{1,0:T(8,128)S(1)}, u32[]{:S(2)}, u32[]{:S(2)}) collective-permute-start(f32[328,128]{1,0:T(8,128)S(1)} %concatenate.26), channel_id=1, source_target_pairs={{4,0},{8,4},{12,8},{5,1},{9,5},{13,9},{6,2},{10,6},{14,10},{7,3},{... | collective-permute-start | bytes 503816 | tf_op jit(solution)/shard_map/ppermute | solution.py:415
  9.8 2.0 %pack.1 = (f32[12,32,128]{2,1,0:T(8,128)}, f32[12,32,128]{2,1,0:T(8,128)}, f32[8,32,128]{2,1,0:T(8,128)}) custom-call(f32[1024,128]{1,0:T(8,128)} %bitcast.31), custom_call_target="tpu_custom_call" | custom-call | tf_op jit(solution)/shard_map/pack/pallas_call | solution.py:48
  11.8 1.5 %collective-permute-start.9 = (f32[12,32,128]{2,1,0:T(8,128)}, f32[12,32,128]{2,1,0:T(8,128)S(1)}, u32[]{:S(2)}, u32[]{:S(2)}) collective-permute-start(f32[12,32,128]{2,1,0:T(8,128)} %get-tuple-element.33.refs_1_), channel_id=1, source_target_pairs={{2,0},{0,2},{3,1},{1,3},{6,4},{4,6},{7,5},{5,7},{10,8},{8,10},{11,... | collective-permute-start | bytes 589832 | tf_op jit(solution)/shard_map/ppermute | solution.py:369
  13.3 0.5 collective-permute-start.6
  13.9 0.9 %copy.8 = f32[2,64,2,64]{3,2,1,0:T(2,128)S(1)} copy(f32[2,64,2,64]{3,2,0,1:T(2,128)} %bitcast.34) | data formatting | bytes 131072 | tf_op jit(solution)/shard_map/transpose | solution.py:443
  14.8 0.7 %reshape.31.r_ref = f32[128,128]{1,0:T(8,128)} reshape(f32[2,64,2,64]{3,2,1,0:T(2,128)S(1)} %copy.8) | data formatting | bytes 131072 | tf_op jit(solution)/shard_map/reshape | solution.py:443
  15.6 8.3 %prepare.1 = (bf16[32,256,384]{2,1,0:T(8,128)(2,1)}, bf16[128,128]{1,0:T(8,128)(2,1)}, bf16[128,128]{1,0:T(8,128)(2,1)}, f32[8,128]{1,0:T(8,128)}) custom-call(f32[32,3,128,128]{3,2,1,0:T(8,128)} %w_ref.1, f32[128,128]{1,0:T(8,128)} %reshape.31.r_ref), custom_call_target="tpu_custom_call" | custom-call | tf_op jit(solution)/shard_map/prepare/pallas_call | solution.py:94
  23.9 0.7 %slice.62 = f32[4,128]{1,0:T(4,128)S(1)} slice(f32[8,128]{1,0:T(8,128)} %get-tuple-element.45), slice={[4:8], [0:128]} | slice | bytes 4096 | tf_op jit(solution)/shard_map/slice | solution.py:457
  24.7 0.3 collective-permute-start.5
  25.1 1.6 %collective-permute-start.3 = (f32[12,32,128]{2,1,0:T(8,128)S(1)}, f32[12,32,128]{2,1,0:T(8,128)S(1)}, u32[]{:S(2)}, u32[]{:S(2)}) collective-permute-start(f32[12,32,128]{2,1,0:T(8,128)S(1)} %pad_maximum_fusion.1.refs_1_), channel_id=1, source_target_pairs={{2,0},{0,2},{3,1},{1,3},{6,4},{4,6},{7,5},{5,7},{10,8},{8,10},{11,... | collective-permute-start | bytes 589832 | tf_op jit(solution)/shard_map/ppermute | solution.py:369
  26.8 0.5 collective-permute-start.10
  27.3 0.1 collective-permute-start.7
  27.4 4.8 %collective-permute-done.3.refs_3_ = f32[12,32,128]{2,1,0:T(8,128)S(1)} collective-permute-done((f32[12,32,128]{2,1,0:T(8,128)S(1)}, f32[12,32,128]{2,1,0:T(8,128)S(1)}, u32[]{:S(2)}, u32[]{:S(2)}) %collective-permute-start.3) | collective-permute-done | bytes 196640 | tf_op jit(solution)/shard_map/ppermute | solution.py:369
  32.4 2.8 %copy-done = bf16[32,256,384]{2,1,0:T(8,128)(2,1)S(1)} copy-done((bf16[32,256,384]{2,1,0:T(8,128)(2,1)S(1)}, bf16[32,256,384]{2,1,0:T(8,128)(2,1)}, u32[]{:S(2)}) %copy-start) | copy-done | bytes 6291480
  35.2 0.8 %copy-done.1 = bf16[128,128]{1,0:T(8,128)(2,1)S(1)} copy-done((bf16[128,128]{1,0:T(8,128)(2,1)S(1)}, bf16[128,128]{1,0:T(8,128)(2,1)}, u32[]{:S(2)}) %copy-start.1) | copy-done | bytes 32792
  35.9 0.8 %copy-done.2 = bf16[128,128]{1,0:T(8,128)(2,1)S(1)} copy-done((bf16[128,128]{1,0:T(8,128)(2,1)S(1)}, bf16[128,128]{1,0:T(8,128)(2,1)}, u32[]{:S(2)}) %copy-start.2) | copy-done | bytes 32792
  36.7 3.5 %stage.3 = (f32[4,8,128]{2,1,0:T(8,128)S(1)}, f32[10,32,128]{2,1,0:T(8,128)S(1)}, f32[8,32,128]{2,1,0:T(8,128)S(1)}, bf16[4,128,128]{2,1,0:T(8,128)(2,1)S(1)}, b...) custom-call(s32[5]{0:T(128)S(1)} %stack.29.refs_0_, ...), custom_call_target="tpu_custom_call" | custom-call | tf_op jit(solution)/shard_map/stage/pallas_call | solution.py:295
  40.3 4.4 %stage.4 = (f32[4,8,128]{2,1,0:T(8,128)S(1)}, f32[12,32,128]{2,1,0:T(8,128)S(1)}, f32[12,32,128]{2,1,0:T(8,128)S(1)}, bf16[4,128,128]{2,1,0:T(8,128)(2,1)S(1)}, ...) custom-call(s32[5]{0:T(128)S(1)} %stack.29.refs_0_, ...), custom_call_target="tpu_custom_call" | custom-call | tf_op jit(solution)/shard_map/stage/pallas_call | solution.py:295
  44.7 0.7 %copy-done.5 = f32[12,32,128]{2,1,0:T(8,128)} copy-done((f32[12,32,128]{2,1,0:T(8,128)}, f32[12,32,128]{2,1,0:T(8,128)S(1)}, u32[]{:S(2)}) %copy-start.5) | copy-done | bytes 196632
  45.4 4.6 %stage.5 = (f32[4,8,128]{2,1,0:T(8,128)S(1)}, f32[10,32,128]{2,1,0:T(8,128)S(1)}, f32[12,32,128]{2,1,0:T(8,128)S(1)}) custom-call(s32[5]{0:T(128)S(1)} %stack.29.refs_0_, f32[12,32,128]{2,1,0:T(8,128)S(1)} %pad_maximum_fusion.1.refs_1_, f32[12,32,128]{2,1,0:T(8,128)S(1)} %collective-permute-done.2.refs_2_, ...), custom_call_target="tpu_custom_call" | custom-call | tf_op jit(solution)/shard_map/stage/pallas_call | solution.py:295
  50.0 0.7 %copy-done.6 = f32[12,32,128]{2,1,0:T(8,128)} copy-done((f32[12,32,128]{2,1,0:T(8,128)}, f32[12,32,128]{2,1,0:T(8,128)S(1)}, u32[]{:S(2)}) %copy-start.6) | copy-done | bytes 196632
  50.7 0.7 %copy-done.9 = f32[10,32,128]{2,1,0:T(8,128)} copy-done((f32[10,32,128]{2,1,0:T(8,128)}, f32[10,32,128]{2,1,0:T(8,128)S(1)}, u32[]{:S(2)}) %copy-start.9) | copy-done | bytes 163864
  51.4 2.7 %collective-permute-start.11 = (f32[1,8,128]{2,1,0:T(8,128)S(1)}, f32[1,8,128]{2,1,0:T(8,128)S(1)}, u32[]{:S(2)}, u32[]{:S(2)}) collective-permute-start(f32[1,8,128]{2,1,0:T(8,128)S(1)} %maximum_bitcast_fusion), channel_id=1, source_target_pairs={{0,4},{4,0},{8,12},{12,8},{1,5},{5,1},{9,13},{13,9},{2,6},{6,2},{1... | collective-permute-start | bytes 12296 | tf_op jit(solution)/shard_map/ppermute | solution.py:384
  54.1 1.6 %collective-permute-done.11 = f32[1,8,128]{2,1,0:T(8,128)S(1)} collective-permute-done((f32[1,8,128]{2,1,0:T(8,128)S(1)}, f32[1,8,128]{2,1,0:T(8,128)S(1)}, u32[]{:S(2)}, u32[]{:S(2)}) %collective-permute-start.11) | collective-permute-done | bytes 4128 | tf_op jit(solution)/shard_map/ppermute | solution.py:384
  55.7 3.0 %collective-permute-start.12 = (f32[2,8,128]{2,1,0:T(8,128)S(1)}, f32[2,8,128]{2,1,0:T(8,128)S(1)}, u32[]{:S(2)}, u32[]{:S(2)}) collective-permute-start(f32[2,8,128]{2,1,0:T(8,128)S(1)} %pad_maximum_fusion.4), channel_id=1, source_target_pairs={{0,8},{4,12},{8,0},{12,4},{1,9},{5,13},{9,1},{13,5},{2,10},{6,14},... | collective-permute-start | bytes 24584 | tf_op jit(solution)/shard_map/ppermute | solution.py:384
  58.7 1.6 %collective-permute-done.12 = f32[2,8,128]{2,1,0:T(8,128)S(1)} collective-permute-done((f32[2,8,128]{2,1,0:T(8,128)S(1)}, f32[2,8,128]{2,1,0:T(8,128)S(1)}, u32[]{:S(2)}, u32[]{:S(2)}) %collective-permute-start.12) | collective-permute-done | bytes 8224 | tf_op jit(solution)/shard_map/ppermute | solution.py:384
  60.3 0.6 pad_maximum_fusion.3.gathered_ref
  60.9 3.7 %finish.1 = (f32[1024,128]{1,0:T(8,128)}, f32[1024,128]{1,0:T(8,128)}) custom-call(f32[4,8,128]{2,1,0:T(8,128)} %pad_maximum_fusion.3.gathered_ref, f32[1024,128]{1,0:T(8,128)} %bitcast.32, f32[10,32,128]{2,1,0:T(8,128)} %copy-done.8, f32[12,32,128]{2,1,0:T(8,128)} %copy-done.4, f32[10,32,128]{2,1,0:T(8,128)} %copy-done.9, f32[8,32,128]{2,1,0:T(8,128)} %copy-done.10, ...), custom_call_target="tpu_custom_call" | custom-call | tf_op jit(solution)/shard_map/finish/pallas_call | solution.py:360
  (57 shorter events, 0.8 us)
Async XLA Ops:
  3.4 21.3 %collective-permute-start = (f32[328,128]{1,0:T(8,128)S(1)}, f32[328,128]{1,0:T(8,128)S(1)}, u32[]{:S(2)}, u32[]{:S(2)}) collective-permute-start(f32[328,128]{1,0:T(8,128)S(1)} %concatenate.25), channel_id=1, source_target_pairs={{0,4},{4,8},{8,12},{1,5},{5,9},{9,13},{2,6},{6,10},{10,14},{3,7},{... | collective-permute-start | bytes 503816 | tf_op jit(solution)/shard_map/ppermute | solution.py:414
  8.5 16.5 %collective-permute-start.1 = (f32[328,128]{1,0:T(8,128)S(1)}, f32[328,128]{1,0:T(8,128)S(1)}, u32[]{:S(2)}, u32[]{:S(2)}) collective-permute-start(f32[328,128]{1,0:T(8,128)S(1)} %concatenate.26), channel_id=1, source_target_pairs={{4,0},{8,4},{12,8},{5,1},{9,5},{13,9},{6,2},{10,6},{14,10},{7,3},{... | collective-permute-start | bytes 503816 | tf_op jit(solution)/shard_map/ppermute | solution.py:415
  11.8 13.0 %copy-start.7 = (f32[12,32,128]{2,1,0:T(8,128)S(1)}, f32[12,32,128]{2,1,0:T(8,128)}, u32[]{:S(2)}) copy-start(f32[12,32,128]{2,1,0:T(8,128)} %get-tuple-element.32.refs_1_) | copy-start | bytes 589828
  11.8 13.3 %copy-start.11 = (f32[8,32,128]{2,1,0:T(8,128)S(1)}, f32[8,32,128]{2,1,0:T(8,128)}, u32[]{:S(2)}) copy-start(f32[8,32,128]{2,1,0:T(8,128)} %get-tuple-element.28) | copy-start | bytes 393220
  11.8 20.6 %copy-start.3 = (f32[12,32,128]{2,1,0:T(8,128)S(1)}, f32[12,32,128]{2,1,0:T(8,128)}, u32[]{:S(2)}) copy-start(f32[12,32,128]{2,1,0:T(8,128)} %get-tuple-element.33.refs_1_) | copy-start | bytes 589828
  11.8 15.0 %collective-permute-start.9 = (f32[12,32,128]{2,1,0:T(8,128)}, f32[12,32,128]{2,1,0:T(8,128)S(1)}, u32[]{:S(2)}, u32[]{:S(2)}) collective-permute-start(f32[12,32,128]{2,1,0:T(8,128)} %get-tuple-element.33.refs_1_), channel_id=1, source_target_pairs={{2,0},{0,2},{3,1},{1,3},{6,4},{4,6},{7,5},{5,7},{10,8},{8,10},{11,... | collective-permute-start | bytes 589832 | tf_op jit(solution)/shard_map/ppermute | solution.py:369
  13.3 13.5 %collective-permute-start.8 = (f32[12,32,128]{2,1,0:T(8,128)}, f32[12,32,128]{2,1,0:T(8,128)S(1)}, u32[]{:S(2)}, u32[]{:S(2)}) collective-permute-start(f32[12,32,128]{2,1,0:T(8,128)} %get-tuple-element.33.refs_1_), channel_id=1, source_target_pairs={{0,1},{1,0},{2,3},{3,2},{4,5},{5,4},{6,7},{7,6},{8,9},{9,8},{10,11... | collective-permute-start | bytes 589832 | tf_op jit(solution)/shard_map/ppermute | solution.py:373
  13.3 14.0 %collective-permute-start.6 = (f32[12,32,128]{2,1,0:T(8,128)}, f32[12,32,128]{2,1,0:T(8,128)S(1)}, u32[]{:S(2)}, u32[]{:S(2)}) collective-permute-start(f32[12,32,128]{2,1,0:T(8,128)} %get-tuple-element.32.refs_1_), channel_id=1, source_target_pairs={{2,0},{0,2},{3,1},{1,3},{6,4},{4,6},{7,5},{5,7},{10,8},{8,10},{11,... | collective-permute-start | bytes 589832 | tf_op jit(solution)/shard_map/ppermute | solution.py:369
  24.7 15.5 %collective-permute-start.5 = (f32[12,32,128]{2,1,0:T(8,128)S(1)}, f32[12,32,128]{2,1,0:T(8,128)S(1)}, u32[]{:S(2)}, u32[]{:S(2)}) collective-permute-start(f32[12,32,128]{2,1,0:T(8,128)S(1)} %copy-done.7), channel_id=1, source_target_pairs={{0,1},{1,0},{2,3},{3,2},{4,5},{5,4},{6,7},{7,6},{8,9},{9,8},{10,11... | collective-permute-start | bytes 589832 | tf_op jit(solution)/shard_map/ppermute | solution.py:373
  25.1 7.2 %collective-permute-start.3 = (f32[12,32,128]{2,1,0:T(8,128)S(1)}, f32[12,32,128]{2,1,0:T(8,128)S(1)}, u32[]{:S(2)}, u32[]{:S(2)}) collective-permute-start(f32[12,32,128]{2,1,0:T(8,128)S(1)} %pad_maximum_fusion.1.refs_1_), channel_id=1, source_target_pairs={{2,0},{0,2},{3,1},{1,3},{6,4},{4,6},{7,5},{5,7},{10,8},{8,10},{11,... | collective-permute-start | bytes 589832 | tf_op jit(solution)/shard_map/ppermute | solution.py:369
  26.7 18.6 %collective-permute-start.2 = (f32[12,32,128]{2,1,0:T(8,128)S(1)}, f32[12,32,128]{2,1,0:T(8,128)S(1)}, u32[]{:S(2)}, u32[]{:S(2)}) collective-permute-start(f32[12,32,128]{2,1,0:T(8,128)S(1)} %pad_maximum_fusion.1.refs_1_), channel_id=1, source_target_pairs={{0,1},{1,0},{2,3},{3,2},{4,5},{5,4},{6,7},{7,6},{8,9},{9,8},{10,11... | collective-permute-start | bytes 589832 | tf_op jit(solution)/shard_map/ppermute | solution.py:373
  26.8 5.5 %collective-permute-start.10 = (f32[12,32,128]{2,1,0:T(8,128)S(1)}, f32[12,32,128]{2,1,0:T(8,128)S(1)}, u32[]{:S(2)}, u32[]{:S(2)}) collective-permute-start(f32[12,32,128]{2,1,0:T(8,128)S(1)} %collective-permute-done.9.refs_3_), channel_id=1, source_target_pairs={{0,1},{1,0},{2,3},{3,2},{4,5},{5,4},{6,7},{7,6},{8,9},{9,8},{10,11... | collective-permute-start | bytes 589832 | tf_op jit(solution)/shard_map/ppermute | solution.py:373
  27.3 13.0 %collective-permute-start.7 = (f32[12,32,128]{2,1,0:T(8,128)S(1)}, f32[12,32,128]{2,1,0:T(8,128)S(1)}, u32[]{:S(2)}, u32[]{:S(2)}) collective-permute-start(f32[12,32,128]{2,1,0:T(8,128)S(1)} %collective-permute-done.6.refs_3_), channel_id=1, source_target_pairs={{0,1},{1,0},{2,3},{3,2},{4,5},{5,4},{6,7},{7,6},{8,9},{9,8},{10,11... | collective-permute-start | bytes 589832 | tf_op jit(solution)/shard_map/ppermute | solution.py:373
  32.2 13.1 %collective-permute-start.4 = (f32[12,32,128]{2,1,0:T(8,128)S(1)}, f32[12,32,128]{2,1,0:T(8,128)S(1)}, u32[]{:S(2)}, u32[]{:S(2)}) collective-permute-start(f32[12,32,128]{2,1,0:T(8,128)S(1)} %collective-permute-done.3.refs_3_), channel_id=1, source_target_pairs={{0,1},{1,0},{2,3},{3,2},{4,5},{5,4},{6,7},{7,6},{8,9},{9,8},{10,11... | collective-permute-start | bytes 589832 | tf_op jit(solution)/shard_map/ppermute | solution.py:373
  32.4 2.8 %copy-start = (bf16[32,256,384]{2,1,0:T(8,128)(2,1)S(1)}, bf16[32,256,384]{2,1,0:T(8,128)(2,1)}, u32[]{:S(2)}) copy-start(bf16[32,256,384]{2,1,0:T(8,128)(2,1)} %get-tuple-element.29.refs_5_) | copy-start | bytes 18874372
  35.2 0.8 %copy-start.1 = (bf16[128,128]{1,0:T(8,128)(2,1)S(1)}, bf16[128,128]{1,0:T(8,128)(2,1)}, u32[]{:S(2)}) copy-start(bf16[128,128]{1,0:T(8,128)(2,1)} %get-tuple-element.30.refs_6_) | copy-start | bytes 98308
  35.9 0.8 %copy-start.2 = (bf16[128,128]{1,0:T(8,128)(2,1)S(1)}, bf16[128,128]{1,0:T(8,128)(2,1)}, u32[]{:S(2)}) copy-start(bf16[128,128]{1,0:T(8,128)(2,1)} %get-tuple-element.31.refs_7_) | copy-start | bytes 98308
  40.2 5.1 %copy-start.10 = (f32[8,32,128]{2,1,0:T(8,128)}, f32[8,32,128]{2,1,0:T(8,128)S(1)}, u32[]{:S(2)}) copy-start(f32[8,32,128]{2,1,0:T(8,128)S(1)} %get-tuple-element.49.refs_3_) | copy-start | bytes 393220
  40.3 9.7 %copy-start.8 = (f32[10,32,128]{2,1,0:T(8,128)}, f32[10,32,128]{2,1,0:T(8,128)S(1)}, u32[]{:S(2)}) copy-start(f32[10,32,128]{2,1,0:T(8,128)S(1)} %get-tuple-element.46.refs_0_) | copy-start | bytes 491524
  44.7 0.7 %copy-start.5 = (f32[12,32,128]{2,1,0:T(8,128)}, f32[12,32,128]{2,1,0:T(8,128)S(1)}, u32[]{:S(2)}) copy-start(f32[12,32,128]{2,1,0:T(8,128)S(1)} %get-tuple-element.50.refs_4_) | copy-start | bytes 589828
  45.3 4.6 %copy-start.4 = (f32[12,32,128]{2,1,0:T(8,128)}, f32[12,32,128]{2,1,0:T(8,128)S(1)}, u32[]{:S(2)}) copy-start(f32[12,32,128]{2,1,0:T(8,128)S(1)} %get-tuple-element.47.refs_1_) | copy-start | bytes 589828
  50.0 0.7 %copy-start.6 = (f32[12,32,128]{2,1,0:T(8,128)}, f32[12,32,128]{2,1,0:T(8,128)S(1)}, u32[]{:S(2)}) copy-start(f32[12,32,128]{2,1,0:T(8,128)S(1)} %get-tuple-element.51.refs_5_) | copy-start | bytes 589828
  50.7 0.7 %copy-start.9 = (f32[10,32,128]{2,1,0:T(8,128)}, f32[10,32,128]{2,1,0:T(8,128)S(1)}, u32[]{:S(2)}) copy-start(f32[10,32,128]{2,1,0:T(8,128)S(1)} %get-tuple-element.48.refs_2_) | copy-start | bytes 491524
  51.4 4.3 %collective-permute-start.11 = (f32[1,8,128]{2,1,0:T(8,128)S(1)}, f32[1,8,128]{2,1,0:T(8,128)S(1)}, u32[]{:S(2)}, u32[]{:S(2)}) collective-permute-start(f32[1,8,128]{2,1,0:T(8,128)S(1)} %maximum_bitcast_fusion), channel_id=1, source_target_pairs={{0,4},{4,0},{8,12},{12,8},{1,5},{5,1},{9,13},{13,9},{2,6},{6,2},{1... | collective-permute-start | bytes 12296 | tf_op jit(solution)/shard_map/ppermute | solution.py:384
  55.7 4.7 %collective-permute-start.12 = (f32[2,8,128]{2,1,0:T(8,128)S(1)}, f32[2,8,128]{2,1,0:T(8,128)S(1)}, u32[]{:S(2)}, u32[]{:S(2)}) collective-permute-start(f32[2,8,128]{2,1,0:T(8,128)S(1)} %pad_maximum_fusion.4), channel_id=1, source_target_pairs={{0,8},{4,12},{8,0},{12,4},{1,9},{5,13},{9,1},{13,5},{2,10},{6,14},... | collective-permute-start | bytes 24584 | tf_op jit(solution)/shard_map/ppermute | solution.py:384

commit v2 on v1

v2 whole, which is shorter than its diff:
```python
import functools

import jax
import jax.numpy as jnp
from jax import lax
from jax.experimental import pallas as pl
from jax.experimental.pallas import tpu as pltpu
from jax.sharding import PartitionSpec as P

SEASONS = 64
VARS = 2
ORDER = SEASONS * VARS
REACH = 1
NUGGET = 10.5
CUTS = (4, 10)
STAGES = ((0, 1), (-1,), (2,))

F32 = jnp.float32
BF16 = jnp.bfloat16
NT = (((1,), (1,)), ((), ()))
NN = (((1,), (0,)), ((), ()))
VMEM = pltpu.VMEM


def dot(a, b, dims):
    return lax.dot_general(a, b, dims, preferred_element_type=F32)


def halves(x):
    high = x.astype(BF16)
    return high, (x - high.astype(F32)).astype(BF16)


def fold(x):
    return jnp.sum(x.reshape(x.shape[0] // 8, 8, x.shape[1]), axis=0)


def block_at(half_id, m, blocks):
    return m + half_id * (blocks - 1 - 2 * m)


def pack_kernel(first, last, blocks, x_ref, same_ref, other_ref):
    me = lax.axis_index("var")
    seasons = x_ref.shape[0] // blocks
    for m in range(first, last):
        for half_id, ref in ((me, same_ref), (1 - me, other_ref)):
            rows = pl.ds(block_at(half_id, m, blocks), seasons, stride=blocks)
            ref[m - first] = x_ref[rows, :]


def pack(x, first, last, blocks):
    seasons, width = x.shape[0] // blocks, x.shape[1]
    return pl.pallas_call(
        functools.partial(pack_kernel, first, last, blocks),
        out_shape=[jax.ShapeDtypeStruct((last - first, seasons, width), F32)] * 2,
        name="pack",
    )(x)


def prepare_kernel(blocks, w_ref, r_ref, w2_ref, rh_ref, rl_ref, scale_ref, held, sems):
    me = lax.axis_index("var")
    count, width = held.shape[0], held.shape[2]
    copies = []
    for m in range(count):
        row = block_at(me, m, blocks)
        group = [
            pltpu.make_async_copy(w_ref.at[row, slot], held.at[m, place], sems.at[m, place])
            for place, slot in enumerate((1 + me, 0, 2 - me))
        ]
        for copy in group:
            copy.start()
        copies.append(group)
    top = jnp.zeros((8, width), F32)
    for m in range(count):
        for place, copy in enumerate(copies[m]):
            copy.wait()
            w = held[m, place]
            high, low = halves(w)
            lanes = slice(place * width, (place + 1) * width)
            w2_ref[m, :width, lanes] = high
            w2_ref[m, width:, lanes] = low
            top = jnp.maximum(top, jnp.max(jnp.abs(w).reshape(-1, 8, width), axis=0))
    r = jnp.concatenate(
        [
            jnp.concatenate(
                [r_ref[pl.ds(VARS * v + w, SEASONS, stride=VARS * VARS), :] for w in range(VARS)],
                axis=1,
            )
            for v in range(VARS)
        ],
        axis=0,
    )
    space_top = jnp.max(jnp.max(top, axis=0, keepdims=True), axis=1, keepdims=True)
    season_top = jnp.max(jnp.max(jnp.abs(r), axis=0, keepdims=True), axis=1, keepdims=True)
    space_top = jnp.where(space_top > 0, space_top, 1.0)
    season_top = jnp.where(season_top > 0, season_top, 1.0)
    high, low = halves(r / season_top / space_top)
    rh_ref[...] = high
    rl_ref[...] = low
    rows = lax.broadcasted_iota(jnp.int32, scale_ref.shape, 0)
    scale_ref[...] = jnp.where(rows == 4, space_top, jnp.where(rows == 5, season_top, 0.0))


def prepare(spatial, season):
    blocks, slots, width, _ = spatial.shape
    count = blocks // 2 + 1
    return pl.pallas_call(
        functools.partial(prepare_kernel, blocks),
        in_specs=[pl.BlockSpec(memory_space=pl.ANY), pl.BlockSpec(memory_space=VMEM)],
        out_specs=[pl.BlockSpec(memory_space=VMEM)] * 4,
        out_shape=[
            jax.ShapeDtypeStruct((count, 2 * width, slots * width), BF16),
            jax.ShapeDtypeStruct((ORDER, ORDER), BF16),
            jax.ShapeDtypeStruct((ORDER, ORDER), BF16),
            jax.ShapeDtypeStruct((8, width), F32),
        ],
        scratch_shapes=[
            VMEM((count, slots, width, width), F32),
            pltpu.SemaphoreType.DMA((count, slots)),
        ],
        compiler_params=pltpu.CompilerParams(vmem_limit_bytes=20 << 20),
        name="prepare",
    )(spatial, season)


def row_starts(seasons, parts):
    me_season, me_var = lax.axis_index("season"), lax.axis_index("var")
    return [
        pl.multiple_of(
            lax.rem(me_var + w, VARS) * SEASONS + lax.rem(me_season + d, parts) * seasons, seasons
        )
        for d in range(parts)
        for w in range(VARS)
    ]


def iota(rows, width):
    return lax.broadcasted_iota(jnp.int32, (rows, width), 0)


def edge_kernel(blocks, parts, *refs):
    w_ref, count_ref, *fields, out_ref, sems = refs
    me = lax.axis_index("var")
    seasons, width = fields[0].shape[1:]
    row = block_at(me, 0, blocks)
    copies = [
        pltpu.make_async_copy(
            w_ref.at[row, slot],
            out_ref.at[pl.ds(2 * ORDER + place * width, width)],
            sems.at[place],
        )
        for place, slot in enumerate((0, 2 - me))
    ]
    for copy in copies:
        copy.start()
    for start, field in zip(row_starts(seasons, parts), fields):
        season = (iota(seasons, width) + lax.rem(start, SEASONS)).astype(F32)
        for m in range(2):
            seen = season >= SEASONS - count_ref[pl.ds(block_at(me, m, blocks), 1), :]
            out_ref[pl.ds(m * ORDER + start, seasons), :] = jnp.where(seen, field[m], 0.0)
    last = 2 * ORDER + 2 * width
    out_ref[last:, :] = jnp.broadcast_to(count_ref[pl.ds(row, 1), :], (8, width))
    for copy in copies:
        copy.wait()


def edge(spatial, count_rows, fields, parts):
    blocks, _, width, _ = spatial.shape
    return pl.pallas_call(
        functools.partial(edge_kernel, blocks, parts),
        in_specs=[pl.BlockSpec(memory_space=pl.ANY)]
        + [pl.BlockSpec(memory_space=VMEM)] * (1 + len(fields)),
        out_specs=pl.BlockSpec(memory_space=VMEM),
        out_shape=jax.ShapeDtypeStruct((2 * ORDER + 2 * width + 8, width), F32),
        scratch_shapes=[pltpu.SemaphoreType.DMA((2,))],
        name="edge",
    )(spatial, count_rows, *fields)


def make_plan(cuts, half):
    plan = []
    have_x, have_1, have_2 = set(), set(), set()
    for chunks in STAGES:
        new = []
        for c in chunks:
            new += [-2, -1] if c < 0 else list(range(cuts[c], cuts[c + 1]))
        have_x |= set(new)
        ones = [
            i for i in range(-1, half + 1) if i not in have_1 and {i - 1, i, i + 1} <= have_x
        ]
        have_1 |= set(ones)
        twos = [i for i in range(half) if i not in have_2 and {i - 1, i, i + 1} <= have_1]
        have_2 |= set(twos)
        later_1 = [i for i in range(-1, half + 1) if i not in have_1]
        later_2 = [i for i in range(half) if i not in have_2]
        keep_x = sorted({i + d for i in later_1 for d in (-1, 0, 1)} & have_x)
        keep_1 = sorted({i + d for i in later_2 for d in (-1, 0, 1)} & have_1)
        plan.append((new, ones, twos, keep_x, keep_1))
    return plan


def in_half(ids, half):
    return [i for i in ids if 0 <= i < half]


def runs(ids, most):
    groups = []
    for i in ids:
        if groups and len(groups[-1]) < most:
            groups[-1].append(i)
        else:
            groups.append([i])
    return groups


def make_stage(plan, cuts, m, blocks, parts, seasons, width):
    half = blocks // 2
    slots = parts * VARS
    new, ones, twos, keep_x, keep_1 = plan[m]
    first, last = m == 0, m == len(plan) - 1
    chunks = [c for c in STAGES[m] if c >= 0]
    outer = -1 in STAGES[m]
    old_x, old_1 = ([], []) if first else (plan[m - 1][3], plan[m - 1][4])
    x_at = {i: n for n, i in enumerate(list(old_x) + list(new))}
    one_at = {i: n for n, i in enumerate(list(old_1) + list(ones))}
    inner_ones = in_half(ones, half)

    def kernel(*refs):
        refs = list(refs)

        def take(n):
            out = refs[:n]
            del refs[:n]
            return out

        field_refs = [take(slots) for _ in chunks]
        w2_ref, rh_ref, rl_ref, count_ref, sums_in = take(5)
        if not first:
            old_xh, old_xl, old_1h, old_1l = take(4)
        if outer:
            (edge_ref,) = take(1)
        sums_out, mine, theirs = take(3)
        if not last:
            keep_xh, keep_xl, keep_1h, keep_1l = take(4)
        xh, xl, oh, ol, pick = take(5)
        me = lax.axis_index("var")

        def count_row(i):
            if i == -1:
                return edge_ref[2 * ORDER + 2 * width : 2 * ORDER + 2 * width + 1, :]
            return count_ref[pl.ds(block_at(me, i, blocks), 1), :]

        season = lax.rem(iota(ORDER, width), SEASONS).astype(F32)

        def masked(i, value):
            return jnp.where(season >= SEASONS - count_row(i), value, 0.0)

        for n in range(len(old_x)):
            xh[n] = old_xh[n]
            xl[n] = old_xl[n]
        for n in range(len(old_1)):
            oh[n] = old_1h[n]
            ol[n] = old_1l[n]

        starts = row_starts(seasons, parts)
        total_0 = sums_in[0]
        for c, fields in zip(chunks, field_refs):
            places = [i for i in new if cuts[c] <= i < cuts[c + 1]]
            for start, field in zip(starts, fields):
                piece_season = (iota(seasons, width) + lax.rem(start, SEASONS)).astype(F32)
                for n, i in enumerate(places):
                    piece = field[n]
                    if 0 <= i < half:
                        total_0 += fold(piece * piece)
                    seen = piece_season >= SEASONS - count_row(i)
                    high, low = halves(jnp.where(seen, piece, 0.0))
                    xh[x_at[i], pl.ds(start, seasons), :] = high
                    xl[x_at[i], pl.ds(start, seasons), :] = low
        if outer:
            for i, n in ((-1, 0), (-2, 1)):
                xh[x_at[i]], xl[x_at[i]] = halves(edge_ref[n * ORDER : (n + 1) * ORDER, :])
        sums_out[0] = total_0

        def space(i, high, low, at):
            if i >= 0:
                hs = jnp.concatenate([high[at[i + d]] for d in (-1, 0, 1)], axis=1)
                ls = jnp.concatenate([low[at[i + d]] for d in (-1, 0, 1)], axis=1)
                both = dot(hs, w2_ref[i], NT)
                return both[:, :width] + both[:, width:] + dot(ls, w2_ref[i, :width, :], NT)
            near = w2_ref[0, :width, :width]
            total = dot(high[at[0]], near, NN)
            total += dot(high[at[0]], w2_ref[0, width:, :width], NN)
            total += dot(low[at[0]], near, NN)
            for n, j in enumerate((-1, -2)):
                begin = 2 * ORDER + n * width
                wh, wl = halves(edge_ref[begin : begin + width, :])
                total += dot(high[at[j]], wh, NT) + dot(high[at[j]], wl, NT)
                total += dot(low[at[j]], wh, NT)
            return total

        def mix(parts_of):
            zh, zl = halves(jnp.concatenate(parts_of, axis=1))
            lhs = jnp.concatenate([rh_ref[...], rh_ref[...], rl_ref[...]], axis=1)
            return dot(lhs, jnp.concatenate([zh, zl, zh], axis=0), NN)

        def hand_out(n, value):
            pick[n] = value
            mine[n] = pick[n, pl.ds(starts[0], seasons), :]
            theirs[n] = pick[n, pl.ds(starts[1], seasons), :]

        total_1, total_2, total_3 = sums_in[1], sums_in[2], sums_in[3]
        for group in runs(ones, 4):
            mixed = mix([space(i, xh, xl, x_at) for i in group])
            for n, i in enumerate(group):
                one = masked(i, mixed[:, n * width : (n + 1) * width])
                oh[one_at[i]], ol[one_at[i]] = halves(one)
                if 0 <= i < half:
                    x = xh[x_at[i]].astype(F32) + xl[x_at[i]].astype(F32)
                    total_1 += fold(x * one)
                    total_2 += fold(one * one)
                    hand_out(inner_ones.index(i), one)
        sums_out[1] = total_1
        sums_out[2] = total_2
        for group in runs(twos, 4):
            mixed = mix([space(i, oh, ol, one_at) for i in group])
            for n, i in enumerate(group):
                two = masked(i, mixed[:, n * width : (n + 1) * width])
                one = oh[one_at[i]].astype(F32) + ol[one_at[i]].astype(F32)
                total_3 += fold(one * two)
                hand_out(len(inner_ones) + twos.index(i), two)
        sums_out[3] = total_3
        if not last:
            for n, i in enumerate(keep_x):
                keep_xh[n] = xh[x_at[i]]
                keep_xl[n] = xl[x_at[i]]
            for n, i in enumerate(keep_1):
                keep_1h[n] = oh[one_at[i]]
                keep_1l[n] = ol[one_at[i]]

    tile = (ORDER, width)
    count = len(inner_ones) + len(twos)
    outs = [jax.ShapeDtypeStruct((4, 8, width), F32)]
    outs += [jax.ShapeDtypeStruct((count, seasons, width), F32)] * 2
    if not last:
        outs += [jax.ShapeDtypeStruct((len(keep_x),) + tile, BF16)] * 2
        outs += [jax.ShapeDtypeStruct((len(keep_1),) + tile, BF16)] * 2
    scratch = [VMEM((len(x_at),) + tile, BF16)] * 2 + [VMEM((len(one_at),) + tile, BF16)] * 2
    scratch += [VMEM((count,) + tile, F32)]
    return kernel, outs, scratch


def run_stage(plan, cuts, m, blocks, parts, seasons, width, operands):
    kernel, outs, scratch = make_stage(plan, cuts, m, blocks, parts, seasons, width)
    return pl.pallas_call(
        kernel,
        in_specs=[pl.BlockSpec(memory_space=VMEM)] * len(operands),
        out_shape=outs,
        scratch_shapes=scratch,
        compiler_params=pltpu.CompilerParams(vmem_limit_bytes=24 << 20),
        name="stage",
    )(*operands)


def finish_kernel(plan, blocks, gathered_ref, x_ref, *refs):
    count = len(plan)
    mine, theirs = refs[:count], refs[count : 2 * count]
    x_out, r_out = refs[2 * count :]
    seasons = x_ref.shape[0] // blocks
    half = blocks // 2
    me = lax.axis_index("var")

    def total(v):
        return jnp.sum(v, axis=1, keepdims=True)

    tuples = [gathered_ref[j] for j in range(gathered_ref.shape[0])]
    top = functools.reduce(jnp.maximum, [t[4:5] for t in tuples])
    sums = [0.0, 0.0, 0.0, 0.0]
    for t in tuples:
        ratio = t[4:5] / top
        factor = jnp.ones_like(ratio)
        for n in range(4):
            sums[n] = sums[n] + t[n : n + 1] * factor
            factor = factor * ratio
    m0, m1, m2, m3 = [total(v) for v in sums]
    scale = (top * tuples[0][5:6])[:, :1]

    first = NUGGET * m0 + scale * m1
    alpha = m0 / first
    lead = alpha * scale
    mean = m1 / m0
    fresh = lead * lead * (m2 - mean * m1)
    c = lead * mean + fresh / m0
    dd = c * c * m0 - 2.0 * c * lead * m1 + lead * lead * m2
    dkd = c * c * m1 - 2.0 * c * lead * m2 + lead * lead * m3
    alpha_2 = fresh / (NUGGET * dd + scale * dkd)
    x_0 = alpha + alpha_2 * c
    r_0 = lead * mean - NUGGET * alpha_2 * c
    x_1 = -alpha_2 * lead
    r_1 = NUGGET * alpha_2 * lead - lead - alpha_2 * scale * c
    r_2 = alpha_2 * scale * lead

    one_at, two_at = {}, {}
    for m, (_, ones, twos, _, _) in enumerate(plan):
        inner = in_half(ones, half)
        one_at.update({i: (m, n) for n, i in enumerate(inner)})
        two_at.update({i: (m, len(inner) + n) for n, i in enumerate(twos)})
    for half_id, held, t in ((me, mine, tuples[0]), (1 - me, theirs, tuples[1])):
        ratio = (t[4:5] / top)[:, :1]
        x_1h, r_1h, r_2h = x_1 * ratio, r_1 * ratio, r_2 * ratio * ratio
        for i in range(half):
            rows = pl.ds(block_at(half_id, i, blocks), seasons, stride=blocks)
            x = x_ref[rows, :]
            m, n = one_at[i]
            one = held[m][n]
            m, n = two_at[i]
            two = held[m][n]
            x_out[rows, :] = x_0 * x + x_1h * one
            r_out[rows, :] = r_0 * x + r_1h * one + r_2h * two


def finish(plan, blocks, gathered, x, mine, theirs):
    return pl.pallas_call(
        functools.partial(finish_kernel, plan, blocks),
        out_shape=[jax.ShapeDtypeStruct(x.shape, F32)] * 2,
        name="finish",
    )(gathered, x, *mine, *theirs)


def from_group(value, step, swap):
    size = lax.axis_size("season")
    pairs = [
        (((p + step) % size) * VARS + (v + swap) % VARS, p * VARS + v)
        for p in range(size)
        for v in range(VARS)
    ]
    return lax.ppermute(value, ("season", "var"), pairs)


def across_edge(value):
    size = lax.axis_size("space")
    pairs = []
    for i in range(1, size * VARS - 1, 2):
        pairs += [(i, i + 1), (i + 1, i)]
    return lax.ppermute(value, ("space", "var"), pairs)


def gather_tiles(value):
    have = jnp.concatenate([value, from_group(value, 0, 1)], axis=0)
    size = lax.axis_size("space")
    if size & (size - 1):
        me = lax.axis_index("space")
        all_tiles = lax.all_gather(have, "space", axis=0, tiled=True)
        return jnp.roll(all_tiles, -me * VARS, axis=0)
    hop = 1
    while hop < size:
        other = lax.ppermute(have, "space", [(i, i ^ hop) for i in range(size)])
        have = jnp.concatenate([have, other], axis=0)
        hop *= 2
    return have


def body(right_side, spatial, columns, counts, season_cov):
    del columns
    seasons = right_side.shape[0]
    blocks, _, width, _ = spatial.shape
    parts = lax.axis_size("season")
    half = blocks // 2
    cuts = (0,) + CUTS + (half + 2,)
    plan = make_plan(cuts, half)

    x = right_side.reshape(seasons * blocks, width)
    count_rows = jnp.broadcast_to(counts.astype(F32)[:, None], (blocks, width))

    chunks = []
    for first, last in zip(cuts[:-1], cuts[1:]):
        same, other = pack(x, first, last, blocks)
        chunks.append(
            [
                from_group(other if w else same, d, w) if d or w else same
                for d in range(parts)
                for w in range(VARS)
            ]
        )
    w2, rh, rl, scale = prepare(
        spatial, season_cov.transpose(0, 1, 3, 2).reshape(SEASONS * VARS * VARS, SEASONS)
    )
    outer = across_edge(edge(spatial, count_rows, chunks[0], parts))

    sums = jnp.zeros((4, 8, width), F32)
    mine, theirs, kept = [], [], []
    for m, stage in enumerate(STAGES):
        operands = [f for c in stage if c >= 0 for f in chunks[c]]
        operands += [w2, rh, rl, count_rows, sums] + kept + [outer] * (-1 in stage)
        out = run_stage(plan, cuts, m, blocks, parts, seasons, width, operands)
        sums, kept = out[0], list(out[3:])
        mine.append(out[1])
        theirs.append(from_group(out[2], 0, 1))
    tile = jnp.concatenate([jnp.sum(sums, axis=1), scale[4:]], axis=0)[None]
    gathered = gather_tiles(tile)
    x_out, r_out = finish(plan, blocks, gathered, x, mine, theirs)
    return x_out.reshape(right_side.shape), r_out.reshape(right_side.shape)


def solution(mesh):
    field = P("season", "var", ("groups", "space"))
    return jax.shard_map(
        body,
        mesh=mesh,
        in_specs=(
            field,
            P(("groups", "space"), None, None, None),
            P(("groups", "space"), None),
            P(("groups", "space")),
            P(),
        ),
        out_specs=(field, field),
        check_vma=False,
    )
```

time: 65.3 us -> 56 us (0.86)
  local copies, waits for them, and re-layouts: 11.2 us -> 6.23 us
  Pallas kernels: 26.5 us -> 23.6 us
    pallas_call x5 -> x8, Pallas kernels: 22.8 us -> 19.9 us  [the longest x3 6 us: run_stage(): pl.pallas_call(kernel, in_specs=[pl.BlockSpec(memory_space=VMEM)] * len(o...]
    slice x6 -> x0, local copies, waits for them, and re-layouts: 1.08 us -> none  [the longest x1 0.99 us: message(): x.reshape(seasons, blocks, width)[:, ids[0]:ids[1] + 1].transpose(1, 0, 2)]
    squeeze x1 -> x0, local copies, waits for them, and re-layouts: 0.95 us -> none  [message(): wide = jnp.concatenate([spatial[own, slot] for slot in slots], axis=0)]
    transpose x1 -> x0, local copies, waits for them, and re-layouts: 0.95 us -> none  [body(): season = season_cov.transpose(1, 0, 3, 2).reshape(ORDER, ORDER)]
    unnamed x26 -> x36, local copies, waits for them, and re-layouts: 6.33 us -> 5.56 us
    reshape x1 -> x0, local copies, waits for them, and re-layouts: 0.75 us -> none  [body(): season = season_cov.transpose(1, 0, 3, 2).reshape(ORDER, ORDER)]
    slice x1, local copies, waits for them, and re-layouts: 0.69 us -> 0.01 us  [body(): tile = jnp.concatenate([jnp.sum(sums, axis=1), scale[4:]], axis=0)[None]]
    ppermute x13 -> x16, starting transfers between devices: 16.5 us -> 15.9 us  [the longest x13 10.9 us: from_group(): return lax.ppermute(value, ('season', 'var'), pairs)]
  transfers between devices with their start and end apart: 13 -> 16, of which waited for: 3 -> 5; matrix products, arithmetic and copies ran while one was open for 4% -> 2% of each run, Pallas kernels for 28% -> 23%
where the time goes in v2:
time: 56 us; the launch traced here: 55.6 us
  Pallas kernels  23.6 us (42%)
  starting transfers between devices  15.9 us (28%)
  waiting for transfers between devices  7.63 us (14%)
  local copies, waits for them, and re-layouts  6.23 us (11%)
  other arithmetic  1.29 us (2%)
  between operations  0.88 us (2%)
    ppermute x13, starting transfers between devices, from_group(): return lax.ppermute(value, ('season', 'var'), pairs)  10.9 us
    pallas_call x3, Pallas kernels, run_stage(): pl.pallas_call(kernel, in_specs=[pl.BlockSpec(memory_space=VMEM)] * len(o...  6 us
    pallas_call x1, Pallas kernels, prepare(): pl.pallas_call(functools.partial(prepare_kernel, blocks), in_specs=[pl.Bl...  5.76 us
    unnamed x36, local copies, waits for them, and re-layouts  5.56 us
    pallas_call x3, Pallas kernels, pack(): pl.pallas_call(functools.partial(pack_kernel, first, last, blocks), out_s...  5.53 us
    ppermute x2, starting transfers between devices, gather_tiles(): other = lax.ppermute(have, 'space', [(i, i ^ hop) for i in range(size)])  4.17 us
    ppermute x13, waiting for transfers between devices, from_group(): return lax.ppermute(value, ('season', 'var'), pairs)  4.03 us
    pallas_call x1, Pallas kernels, finish(): pl.pallas_call(functools.partial(finish_kernel, plan, blocks), out_shape=...  3.75 us
  transfers between devices with their start and end apart: 16, of which 5 were waited for; matrix products, arithmetic and copies ran while one was open for 2% of the time, Pallas kernels for 23%

profile of v2, /device:TPU:0, one launch (start us, length us, event | category | flops | bytes accessed | tf_op | source)
XLA Modules:
  0.0 55.6 jit_solution(4167395139366155760)
XLA Ops:
  0.6 1.8 %pack.4 = (f32[4,32,128]{2,1,0:T(8,128)}, f32[4,32,128]{2,1,0:T(8,128)}) custom-call(f32[1024,128]{1,0:T(8,128)} %bitcast.9), custom_call_target="tpu_custom_call" | custom-call | tf_op jit(solution)/shard_map/pack/pallas_call | solution.py:53
  2.5 2.9 %collective-permute-start.4 = (f32[4,32,128]{2,1,0:T(8,128)}, f32[4,32,128]{2,1,0:T(8,128)S(1)}, u32[]{:S(2)}, u32[]{:S(2)}) collective-permute-start(f32[4,32,128]{2,1,0:T(8,128)} %get-tuple-element.36.refs_0_.refs_2_), channel_id=1, source_target_pairs={{2,0},{3,1},{0,2},{1,3},{6,4},{7,5},{4,6},{5,7},{10,8},{11,9},{8,1... | collective-permute-start | bytes 196616 | tf_op jit(solution)/shard_map/ppermute | solution.py:436
  5.5 0.7 %convert_element_type.3 = f32[32]{0:T(128)S(1)} convert(s32[32]{0:T(128)} %param.7) | non-fusion elementwise | flops 32 | bytes 256 | tf_op jit(solution)/shard_map/convert_element_type | solution.py:472
  6.2 1.9 %collective-permute-done.4.refs_2_.refs_4_ = f32[4,32,128]{2,1,0:T(8,128)S(1)} collective-permute-done((f32[4,32,128]{2,1,0:T(8,128)}, f32[4,32,128]{2,1,0:T(8,128)S(1)}, u32[]{:S(2)}, u32[]{:S(2)}) %collective-permute-start.4) | collective-permute-done | bytes 65568 | tf_op jit(solution)/shard_map/ppermute | solution.py:436
  8.0 1.3 %collective-permute-done.5.refs_3_.refs_5_ = f32[4,32,128]{2,1,0:T(8,128)S(1)} collective-permute-done((f32[4,32,128]{2,1,0:T(8,128)}, f32[4,32,128]{2,1,0:T(8,128)S(1)}, u32[]{:S(2)}, u32[]{:S(2)}) %collective-permute-start.5) | collective-permute-done | bytes 65568 | tf_op jit(solution)/shard_map/ppermute | solution.py:436
  9.4 0.7 %broadcast_in_dim.12.refs_11_.refs_1_.refs_3_.refs_7_ = f32[32,128]{1,0:T(8,128)} broadcast(f32[32]{0:T(128)S(1)} %convert_element_type.3), dimensions={0} | broadcast | bytes 16512 | tf_op jit(solution)/shard_map/broadcast_in_dim | solution.py:472
  10.0 2.6 %edge.1 = f32[520,128]{1,0:T(8,128)} custom-call(f32[32,3,128,128]{3,2,1,0:T(8,128)} %refs_0_.1, f32[32,128]{1,0:T(8,128)} %broadcast_in_dim.12.refs_11_.refs_1_.refs_3_.refs_7_, f32[4,32,128]{2,1,0:T(8,128)} %get-tuple-element.36.refs_0_.refs_2_, f32[4,32,128]{2,1,0:T(8,128)} %copy-done.5, f32[4,32,128]{2,1,0:T(8,128)} %copy-done.3, f32[4,32,128]{2,1,0:T(8,128)} %copy-done.7), custom_call_target="tpu_custom_call" | custom-call | tf_op jit(solution)/shard_map/edge/pallas_call | solution.py:169
  12.7 0.8 %collective-permute-start.9 = (f32[520,128]{1,0:T(8,128)}, f32[520,128]{1,0:T(8,128)S(1)}, u32[]{:S(2)}, u32[]{:S(2)}) collective-permute-start(f32[520,128]{1,0:T(8,128)} %edge.1), channel_id=1, source_target_pairs={{1,4},{4,1},{5,8},{8,5},{9,12},{12,9},{3,6},{6,3},{7,10},{10,7},{1... | collective-permute-start | bytes 798728 | tf_op jit(solution)/shard_map/ppermute | solution.py:444
  13.5 1.8 %pack.5 = (f32[6,32,128]{2,1,0:T(8,128)}, f32[6,32,128]{2,1,0:T(8,128)}) custom-call(f32[1024,128]{1,0:T(8,128)} %bitcast.10), custom_call_target="tpu_custom_call" | custom-call | tf_op jit(solution)/shard_map/pack/pallas_call | solution.py:53
  15.3 2.9 %collective-permute-start.6 = (f32[6,32,128]{2,1,0:T(8,128)}, f32[6,32,128]{2,1,0:T(8,128)S(1)}, u32[]{:S(2)}, u32[]{:S(2)}) collective-permute-start(f32[6,32,128]{2,1,0:T(8,128)} %get-tuple-element.39), channel_id=1, source_target_pairs={{1,0},{0,1},{3,2},{2,3},{5,4},{4,5},{7,6},{6,7},{9,8},{8,9},{11,10... | collective-permute-start | bytes 294920 | tf_op jit(solution)/shard_map/ppermute | solution.py:436
  18.3 1.2 %collective-permute-start.7 = (f32[6,32,128]{2,1,0:T(8,128)}, f32[6,32,128]{2,1,0:T(8,128)S(1)}, u32[]{:S(2)}, u32[]{:S(2)}) collective-permute-start(f32[6,32,128]{2,1,0:T(8,128)} %get-tuple-element.38.refs_4_), channel_id=1, source_target_pairs={{2,0},{3,1},{0,2},{1,3},{6,4},{7,5},{4,6},{5,7},{10,8},{11,9},{8,1... | collective-permute-start | bytes 294920 | tf_op jit(solution)/shard_map/ppermute | solution.py:436
  19.5 1.9 %pack.3 = (f32[8,32,128]{2,1,0:T(8,128)}, f32[8,32,128]{2,1,0:T(8,128)}) custom-call(f32[1024,128]{1,0:T(8,128)} %bitcast.11), custom_call_target="tpu_custom_call" | custom-call | tf_op jit(solution)/shard_map/pack/pallas_call | solution.py:53
  21.3 0.8 %collective-permute-start.1 = (f32[8,32,128]{2,1,0:T(8,128)}, f32[8,32,128]{2,1,0:T(8,128)S(1)}, u32[]{:S(2)}, u32[]{:S(2)}) collective-permute-start(f32[8,32,128]{2,1,0:T(8,128)} %get-tuple-element.31.refs_0_), channel_id=1, source_target_pairs={{2,0},{3,1},{0,2},{1,3},{6,4},{7,5},{4,6},{5,7},{10,8},{11,9},{8,1... | collective-permute-start | bytes 393224 | tf_op jit(solution)/shard_map/ppermute | solution.py:436
  22.2 1.0 %collective-permute-start.2 = (f32[8,32,128]{2,1,0:T(8,128)}, f32[8,32,128]{2,1,0:T(8,128)S(1)}, u32[]{:S(2)}, u32[]{:S(2)}) collective-permute-start(f32[8,32,128]{2,1,0:T(8,128)} %get-tuple-element.32), channel_id=1, source_target_pairs={{3,0},{2,1},{1,2},{0,3},{7,4},{6,5},{5,6},{4,7},{11,8},{10,9},{9,1... | collective-permute-start | bytes 393224 | tf_op jit(solution)/shard_map/ppermute | solution.py:436
  23.2 0.7 %collective-permute-start.8 = (f32[6,32,128]{2,1,0:T(8,128)}, f32[6,32,128]{2,1,0:T(8,128)S(1)}, u32[]{:S(2)}, u32[]{:S(2)}) collective-permute-start(f32[6,32,128]{2,1,0:T(8,128)} %get-tuple-element.39), channel_id=1, source_target_pairs={{3,0},{2,1},{1,2},{0,3},{7,4},{6,5},{5,6},{4,7},{11,8},{10,9},{9,1... | collective-permute-start | bytes 294920 | tf_op jit(solution)/shard_map/ppermute | solution.py:436
  23.9 2.8 %copy-done = f32[32,3,128,128]{3,2,1,0:T(8,128)S(1)} copy-done((f32[32,3,128,128]{3,2,1,0:T(8,128)S(1)}, f32[32,3,128,128]{3,2,1,0:T(8,128)}, u32[]{:S(2)}) %copy-start) | copy-done | bytes 6291480
  26.7 5.8 %prepare.1 = (bf16[17,256,384]{2,1,0:T(8,128)(2,1)S(1)}, bf16[128,128]{1,0:T(8,128)(2,1)S(1)}, bf16[128,128]{1,0:T(8,128)(2,1)S(1)}, f32[8,128]{1,0:T(8,128)S(1)}) custom-call(f32[32,3,128,128]{3,2,1,0:T(8,128)S(1)} %copy-done, f32[256,64]{1,0:T(8,128)S(1)} %bitcast.8), custom_call_target="tpu_custom_call" | custom-call | tf_op jit(solution)/shard_map/prepare/pallas_call | solution.py:107
  32.6 2.4 %stage.3 = (f32[4,8,128]{2,1,0:T(8,128)S(1)}, f32[14,32,128]{2,1,0:T(8,128)S(1)}, f32[14,32,128]{2,1,0:T(8,128)S(1)}, bf16[4,128,128]{2,1,0:T(8,128)(2,1)S(1)}, ...) custom-call(f32[4,32,128]{2,1,0:T(8,128)S(1)} %copy-done.2, ...), custom_call_target="tpu_custom_call" | custom-call | tf_op jit(solution)/shard_map/stage/pallas_call | solution.py:354
  35.0 0.7 %copy-done.10 = f32[14,32,128]{2,1,0:T(8,128)} copy-done((f32[14,32,128]{2,1,0:T(8,128)}, f32[14,32,128]{2,1,0:T(8,128)S(1)}, u32[]{:S(2)}) %copy-start.10) | copy-done | bytes 229400
  35.7 1.1 %stage.4 = (f32[4,8,128]{2,1,0:T(8,128)S(1)}, f32[3,32,128]{2,1,0:T(8,128)S(1)}, f32[3,32,128]{2,1,0:T(8,128)S(1)}, bf16[2,128,128]{2,1,0:T(8,128)(2,1)S(1)}, bf...) custom-call(bf16[17,256,384]{2,1,0:T(8,128)(2,1)S(1)} %get-tuple-element.33.refs_8, ...), custom_call_target="tpu_custom_call" | custom-call | tf_op jit(solution)/shard_map/stage/pallas_call | solution.py:354
  36.8 0.6 %copy-done.14 = f32[3,32,128]{2,1,0:T(8,128)} copy-done((f32[3,32,128]{2,1,0:T(8,128)}, f32[3,32,128]{2,1,0:T(8,128)S(1)}, u32[]{:S(2)}) %copy-start.14) | copy-done | bytes 49176
  37.4 2.5 %stage.5 = (f32[4,8,128]{2,1,0:T(8,128)S(1)}, f32[15,32,128]{2,1,0:T(8,128)S(1)}, f32[15,32,128]{2,1,0:T(8,128)S(1)}) custom-call(f32[8,32,128]{2,1,0:T(8,128)S(1)} %copy-done.12, f32[8,32,128]{2,1,0:T(8,128)S(1)} %collective-permute-done.refs_1_, f32[8,32,128]{2,1,0:T(8,128)S(1)} %collective-permute-done.1.refs_2_, ...), custom_call_target="tpu_custom_call" | custom-call | tf_op jit(solution)/shard_map/stage/pallas_call | solution.py:354
  39.9 0.7 %copy-done.9 = f32[15,32,128]{2,1,0:T(8,128)} copy-done((f32[15,32,128]{2,1,0:T(8,128)}, f32[15,32,128]{2,1,0:T(8,128)S(1)}, u32[]{:S(2)}) %copy-start.9) | copy-done | bytes 245784
  40.6 0.7 %collective-permute-start.10 = (f32[1,8,128]{2,1,0:T(8,128)S(1)}, f32[1,8,128]{2,1,0:T(8,128)S(1)}, u32[]{:S(2)}, u32[]{:S(2)}) collective-permute-start(f32[1,8,128]{2,1,0:T(8,128)S(1)} %maximum_bitcast_fusion), channel_id=1, source_target_pairs={{1,0},{0,1},{3,2},{2,3},{5,4},{4,5},{7,6},{6,7},{9,8},{8,9},{11,10... | collective-permute-start | bytes 12296 | tf_op jit(solution)/shard_map/ppermute | solution.py:436
  41.3 0.8 %collective-permute-done.10 = f32[1,8,128]{2,1,0:T(8,128)S(1)} collective-permute-done((f32[1,8,128]{2,1,0:T(8,128)S(1)}, f32[1,8,128]{2,1,0:T(8,128)S(1)}, u32[]{:S(2)}, u32[]{:S(2)}) %collective-permute-start.10) | collective-permute-done | bytes 4128 | tf_op jit(solution)/shard_map/ppermute | solution.py:436
  42.1 1.6 %collective-permute-start.11 = (f32[2,8,128]{2,1,0:T(8,128)S(1)}, f32[2,8,128]{2,1,0:T(8,128)S(1)}, u32[]{:S(2)}, u32[]{:S(2)}) collective-permute-start(f32[2,8,128]{2,1,0:T(8,128)S(1)} %pad_maximum_fusion.2), channel_id=1, source_target_pairs={{0,4},{4,0},{8,12},{12,8},{1,5},{5,1},{9,13},{13,9},{2,6},{6,2},{1... | collective-permute-start | bytes 24584 | tf_op jit(solution)/shard_map/ppermute | solution.py:456
  44.2 1.6 %collective-permute-done.11 = f32[2,8,128]{2,1,0:T(8,128)S(1)} collective-permute-done((f32[2,8,128]{2,1,0:T(8,128)S(1)}, f32[2,8,128]{2,1,0:T(8,128)S(1)}, u32[]{:S(2)}, u32[]{:S(2)}) %collective-permute-start.11) | collective-permute-done | bytes 8224 | tf_op jit(solution)/shard_map/ppermute | solution.py:456
  45.8 2.6 %collective-permute-start.12 = (f32[4,8,128]{2,1,0:T(8,128)S(1)}, f32[4,8,128]{2,1,0:T(8,128)S(1)}, u32[]{:S(2)}, u32[]{:S(2)}) collective-permute-start(f32[4,8,128]{2,1,0:T(8,128)S(1)} %pad_maximum_fusion.1), channel_id=1, source_target_pairs={{0,8},{4,12},{8,0},{12,4},{1,9},{5,13},{9,1},{13,5},{2,10},{6,14},... | collective-permute-start | bytes 49160 | tf_op jit(solution)/shard_map/ppermute | solution.py:456
  48.4 2.0 %collective-permute-done.12 = f32[4,8,128]{2,1,0:T(8,128)S(1)} collective-permute-done((f32[4,8,128]{2,1,0:T(8,128)S(1)}, f32[4,8,128]{2,1,0:T(8,128)S(1)}, u32[]{:S(2)}, u32[]{:S(2)}) %collective-permute-start.12) | collective-permute-done | bytes 16416 | tf_op jit(solution)/shard_map/ppermute | solution.py:456
  50.4 0.6 %pad_maximum_fusion.gathered_ref = f32[8,8,128]{2,1,0:T(8,128)} fusion(f32[4,8,128]{2,1,0:T(8,128)S(1)} %collective-permute-done.12, f32[2,8,128]{2,1,0:T(8,128)S(1)} %collective-permute-done.11, f32[1,8,128]{2,1,0:T(8,128)S(1)} %collective-permute-done.10, f32[1,8,128]{2,1,0:T(8,128)S(1)} %maximum_bitcast_fusion), kind=kLoop, calls=%fused_computation | loop fusion | flops 24576 | bytes 65536 | tf_op jit(solution)/shard_map/concatenate | solution.py:457
  51.1 0.7 %copy-done.16 = f32[14,32,128]{2,1,0:T(8,128)} copy-done((f32[14,32,128]{2,1,0:T(8,128)}, f32[14,32,128]{2,1,0:T(8,128)S(1)}, u32[]{:S(2)}) %copy-start.16) | copy-done | bytes 229400
  51.8 3.7 %finish.1 = (f32[1024,128]{1,0:T(8,128)}, f32[1024,128]{1,0:T(8,128)}) custom-call(f32[8,8,128]{2,1,0:T(8,128)} %pad_maximum_fusion.gathered_ref, f32[1024,128]{1,0:T(8,128)} %bitcast.12, f32[14,32,128]{2,1,0:T(8,128)} %copy-done.10, f32[3,32,128]{2,1,0:T(8,128)} %copy-done.14, f32[15,32,128]{2,1,0:T(8,128)} %copy-done.9, f32[14,32,128]{2,1,0:T(8,128)} %copy-done.16, ...), custom_call_target="tpu_custom_call" | custom-call | tf_op jit(solution)/shard_map/finish/pallas_call | solution.py:422
  (54 shorter events, 0.8 us)
Async XLA Ops:
  0.6 23.3 %copy-start.11 = (f32[64,2,64,2]{2,3,1,0:T(2,128)S(1)}, f32[64,2,64,2]{2,3,1,0:T(2,128)}, u32[]{:S(2)}) copy-start(f32[64,2,64,2]{2,3,1,0:T(2,128)} %param.8) | copy-start | bytes 196612
  2.5 5.6 %collective-permute-start.4 = (f32[4,32,128]{2,1,0:T(8,128)}, f32[4,32,128]{2,1,0:T(8,128)S(1)}, u32[]{:S(2)}, u32[]{:S(2)}) collective-permute-start(f32[4,32,128]{2,1,0:T(8,128)} %get-tuple-element.36.refs_0_.refs_2_), channel_id=1, source_target_pairs={{2,0},{3,1},{0,2},{1,3},{6,4},{7,5},{4,6},{5,7},{10,8},{11,9},{8,1... | collective-permute-start | bytes 196616 | tf_op jit(solution)/shard_map/ppermute | solution.py:436
  5.4 2.6 %collective-permute-start.3 = (f32[4,32,128]{2,1,0:T(8,128)}, f32[4,32,128]{2,1,0:T(8,128)S(1)}, u32[]{:S(2)}, u32[]{:S(2)}) collective-permute-start(f32[4,32,128]{2,1,0:T(8,128)} %get-tuple-element.37), channel_id=1, source_target_pairs={{1,0},{0,1},{3,2},{2,3},{5,4},{4,5},{7,6},{6,7},{9,8},{8,9},{11,10... | collective-permute-start | bytes 196616 | tf_op jit(solution)/shard_map/ppermute | solution.py:436
  5.4 4.0 %collective-permute-start.5 = (f32[4,32,128]{2,1,0:T(8,128)}, f32[4,32,128]{2,1,0:T(8,128)S(1)}, u32[]{:S(2)}, u32[]{:S(2)}) collective-permute-start(f32[4,32,128]{2,1,0:T(8,128)} %get-tuple-element.37), channel_id=1, source_target_pairs={{3,0},{2,1},{1,2},{0,3},{7,4},{6,5},{5,6},{4,7},{11,8},{10,9},{9,1... | collective-permute-start | bytes 196616 | tf_op jit(solution)/shard_map/ppermute | solution.py:436
  8.0 2.0 %copy-start.3 = (f32[4,32,128]{2,1,0:T(8,128)}, f32[4,32,128]{2,1,0:T(8,128)S(1)}, u32[]{:S(2)}) copy-start(f32[4,32,128]{2,1,0:T(8,128)S(1)} %collective-permute-done.4.refs_2_.refs_4_) | copy-start | bytes 196612
  8.0 2.0 %copy-start.5 = (f32[4,32,128]{2,1,0:T(8,128)}, f32[4,32,128]{2,1,0:T(8,128)S(1)}, u32[]{:S(2)}) copy-start(f32[4,32,128]{2,1,0:T(8,128)S(1)} %collective-permute-done.3.refs_1_.refs_3_) | copy-start | bytes 196612
  10.0 22.5 %copy-start.1 = (f32[32,128]{1,0:T(8,128)S(1)}, f32[32,128]{1,0:T(8,128)}, u32[]{:S(2)}) copy-start(f32[32,128]{1,0:T(8,128)} %broadcast_in_dim.12.refs_11_.refs_1_.refs_3_.refs_7_) | copy-start | bytes 49156
  10.0 22.5 %copy-start.2 = (f32[4,32,128]{2,1,0:T(8,128)S(1)}, f32[4,32,128]{2,1,0:T(8,128)}, u32[]{:S(2)}) copy-start(f32[4,32,128]{2,1,0:T(8,128)} %get-tuple-element.36.refs_0_.refs_2_) | copy-start | bytes 196612
  12.6 19.9 %copy-start.4 = (f32[4,32,128]{2,1,0:T(8,128)S(1)}, f32[4,32,128]{2,1,0:T(8,128)}, u32[]{:S(2)}) copy-start(f32[4,32,128]{2,1,0:T(8,128)} %copy-done.3) | copy-start | bytes 196612
  12.6 19.9 %copy-start.6 = (f32[4,32,128]{2,1,0:T(8,128)S(1)}, f32[4,32,128]{2,1,0:T(8,128)}, u32[]{:S(2)}) copy-start(f32[4,32,128]{2,1,0:T(8,128)} %copy-done.5) | copy-start | bytes 196612
  12.7 19.9 %copy-start.8 = (f32[4,32,128]{2,1,0:T(8,128)S(1)}, f32[4,32,128]{2,1,0:T(8,128)}, u32[]{:S(2)}) copy-start(f32[4,32,128]{2,1,0:T(8,128)} %copy-done.7) | copy-start | bytes 196612
  12.7 23.0 %collective-permute-start.9 = (f32[520,128]{1,0:T(8,128)}, f32[520,128]{1,0:T(8,128)S(1)}, u32[]{:S(2)}, u32[]{:S(2)}) collective-permute-start(f32[520,128]{1,0:T(8,128)} %edge.1), channel_id=1, source_target_pairs={{1,4},{4,1},{5,8},{8,5},{9,12},{12,9},{3,6},{6,3},{7,10},{10,7},{1... | collective-permute-start | bytes 798728 | tf_op jit(solution)/shard_map/ppermute | solution.py:444
  15.3 17.2 %copy-start.13 = (f32[6,32,128]{2,1,0:T(8,128)S(1)}, f32[6,32,128]{2,1,0:T(8,128)}, u32[]{:S(2)}) copy-start(f32[6,32,128]{2,1,0:T(8,128)} %get-tuple-element.38.refs_4_) | copy-start | bytes 294916
  15.3 6.8 %collective-permute-start.6 = (f32[6,32,128]{2,1,0:T(8,128)}, f32[6,32,128]{2,1,0:T(8,128)S(1)}, u32[]{:S(2)}, u32[]{:S(2)}) collective-permute-start(f32[6,32,128]{2,1,0:T(8,128)} %get-tuple-element.39), channel_id=1, source_target_pairs={{1,0},{0,1},{3,2},{2,3},{5,4},{4,5},{7,6},{6,7},{9,8},{8,9},{11,10... | collective-permute-start | bytes 294920 | tf_op jit(solution)/shard_map/ppermute | solution.py:436
  18.3 4.9 %collective-permute-start.7 = (f32[6,32,128]{2,1,0:T(8,128)}, f32[6,32,128]{2,1,0:T(8,128)S(1)}, u32[]{:S(2)}, u32[]{:S(2)}) collective-permute-start(f32[6,32,128]{2,1,0:T(8,128)} %get-tuple-element.38.refs_4_), channel_id=1, source_target_pairs={{2,0},{3,1},{0,2},{1,3},{6,4},{7,5},{4,6},{5,7},{10,8},{11,9},{8,1... | collective-permute-start | bytes 294920 | tf_op jit(solution)/shard_map/ppermute | solution.py:436
  21.3 16.0 %collective-permute-start = (f32[8,32,128]{2,1,0:T(8,128)}, f32[8,32,128]{2,1,0:T(8,128)S(1)}, u32[]{:S(2)}, u32[]{:S(2)}) collective-permute-start(f32[8,32,128]{2,1,0:T(8,128)} %get-tuple-element.32), channel_id=1, source_target_pairs={{1,0},{0,1},{3,2},{2,3},{5,4},{4,5},{7,6},{6,7},{9,8},{8,9},{11,10... | collective-permute-start | bytes 393224 | tf_op jit(solution)/shard_map/ppermute | solution.py:436
  21.3 16.0 %collective-permute-start.1 = (f32[8,32,128]{2,1,0:T(8,128)}, f32[8,32,128]{2,1,0:T(8,128)S(1)}, u32[]{:S(2)}, u32[]{:S(2)}) collective-permute-start(f32[8,32,128]{2,1,0:T(8,128)} %get-tuple-element.31.refs_0_), channel_id=1, source_target_pairs={{2,0},{3,1},{0,2},{1,3},{6,4},{7,5},{4,6},{5,7},{10,8},{11,9},{8,1... | collective-permute-start | bytes 393224 | tf_op jit(solution)/shard_map/ppermute | solution.py:436
  22.2 15.2 %collective-permute-start.2 = (f32[8,32,128]{2,1,0:T(8,128)}, f32[8,32,128]{2,1,0:T(8,128)S(1)}, u32[]{:S(2)}, u32[]{:S(2)}) collective-permute-start(f32[8,32,128]{2,1,0:T(8,128)} %get-tuple-element.32), channel_id=1, source_target_pairs={{3,0},{2,1},{1,2},{0,3},{7,4},{6,5},{5,6},{4,7},{11,8},{10,9},{9,1... | collective-permute-start | bytes 393224 | tf_op jit(solution)/shard_map/ppermute | solution.py:436
  23.2 9.3 %collective-permute-start.8 = (f32[6,32,128]{2,1,0:T(8,128)}, f32[6,32,128]{2,1,0:T(8,128)S(1)}, u32[]{:S(2)}, u32[]{:S(2)}) collective-permute-start(f32[6,32,128]{2,1,0:T(8,128)} %get-tuple-element.39), channel_id=1, source_target_pairs={{3,0},{2,1},{1,2},{0,3},{7,4},{6,5},{5,6},{4,7},{11,8},{10,9},{9,1... | collective-permute-start | bytes 294920 | tf_op jit(solution)/shard_map/ppermute | solution.py:436
  23.9 2.8 %copy-start = (f32[32,3,128,128]{3,2,1,0:T(8,128)S(1)}, f32[32,3,128,128]{3,2,1,0:T(8,128)}, u32[]{:S(2)}) copy-start(f32[32,3,128,128]{3,2,1,0:T(8,128)} %refs_0_.1) | copy-start | bytes 18874372
  26.7 10.7 %copy-start.12 = (f32[8,32,128]{2,1,0:T(8,128)S(1)}, f32[8,32,128]{2,1,0:T(8,128)}, u32[]{:S(2)}) copy-start(f32[8,32,128]{2,1,0:T(8,128)} %get-tuple-element.31.refs_0_) | copy-start | bytes 393220
  35.0 0.7 %copy-start.10 = (f32[14,32,128]{2,1,0:T(8,128)}, f32[14,32,128]{2,1,0:T(8,128)S(1)}, u32[]{:S(2)}) copy-start(f32[14,32,128]{2,1,0:T(8,128)S(1)} %get-tuple-element.52.refs_0_) | copy-start | bytes 688132
  39.9 0.7 %copy-start.9 = (f32[15,32,128]{2,1,0:T(8,128)}, f32[15,32,128]{2,1,0:T(8,128)S(1)}, u32[]{:S(2)}) copy-start(f32[15,32,128]{2,1,0:T(8,128)S(1)} %get-tuple-element.54.refs_2_) | copy-start | bytes 737284
  40.6 1.5 %collective-permute-start.10 = (f32[1,8,128]{2,1,0:T(8,128)S(1)}, f32[1,8,128]{2,1,0:T(8,128)S(1)}, u32[]{:S(2)}, u32[]{:S(2)}) collective-permute-start(f32[1,8,128]{2,1,0:T(8,128)S(1)} %maximum_bitcast_fusion), channel_id=1, source_target_pairs={{1,0},{0,1},{3,2},{2,3},{5,4},{4,5},{7,6},{6,7},{9,8},{8,9},{11,10... | collective-permute-start | bytes 12296 | tf_op jit(solution)/shard_map/ppermute | solution.py:436
  42.1 3.7 %collective-permute-start.11 = (f32[2,8,128]{2,1,0:T(8,128)S(1)}, f32[2,8,128]{2,1,0:T(8,128)S(1)}, u32[]{:S(2)}, u32[]{:S(2)}) collective-permute-start(f32[2,8,128]{2,1,0:T(8,128)S(1)} %pad_maximum_fusion.2), channel_id=1, source_target_pairs={{0,4},{4,0},{8,12},{12,8},{1,5},{5,1},{9,13},{13,9},{2,6},{6,2},{1... | collective-permute-start | bytes 24584 | tf_op jit(solution)/shard_map/ppermute | solution.py:456
  43.7 7.3 %collective-permute-start.15 = (f32[15,32,128]{2,1,0:T(8,128)S(1)}, f32[15,32,128]{2,1,0:T(8,128)S(1)}, u32[]{:S(2)}, u32[]{:S(2)}) collective-permute-start(f32[15,32,128]{2,1,0:T(8,128)S(1)} %get-tuple-element.57), channel_id=1, source_target_pairs={{1,0},{0,1},{3,2},{2,3},{5,4},{4,5},{7,6},{6,7},{9,8},{8,9},{11,10... | collective-permute-start | bytes 737288 | tf_op jit(solution)/shard_map/ppermute | solution.py:436
  43.8 7.3 %collective-permute-start.13 = (f32[14,32,128]{2,1,0:T(8,128)S(1)}, f32[14,32,128]{2,1,0:T(8,128)S(1)}, u32[]{:S(2)}, u32[]{:S(2)}) collective-permute-start(f32[14,32,128]{2,1,0:T(8,128)S(1)} %get-tuple-element.55), channel_id=1, source_target_pairs={{1,0},{0,1},{3,2},{2,3},{5,4},{4,5},{7,6},{6,7},{9,8},{8,9},{11,10... | collective-permute-start | bytes 688136 | tf_op jit(solution)/shard_map/ppermute | solution.py:436
  45.8 4.6 %collective-permute-start.12 = (f32[4,8,128]{2,1,0:T(8,128)S(1)}, f32[4,8,128]{2,1,0:T(8,128)S(1)}, u32[]{:S(2)}, u32[]{:S(2)}) collective-permute-start(f32[4,8,128]{2,1,0:T(8,128)S(1)} %pad_maximum_fusion.1), channel_id=1, source_target_pairs={{0,8},{4,12},{8,0},{12,4},{1,9},{5,13},{9,1},{13,5},{2,10},{6,14},... | collective-permute-start | bytes 49160 | tf_op jit(solution)/shard_map/ppermute | solution.py:456
  48.4 2.7 %collective-permute-start.14 = (f32[3,32,128]{2,1,0:T(8,128)S(1)}, f32[3,32,128]{2,1,0:T(8,128)S(1)}, u32[]{:S(2)}, u32[]{:S(2)}) collective-permute-start(f32[3,32,128]{2,1,0:T(8,128)S(1)} %get-tuple-element.56), channel_id=1, source_target_pairs={{1,0},{0,1},{3,2},{2,3},{5,4},{4,5},{7,6},{6,7},{9,8},{8,9},{11,10... | collective-permute-start | bytes 147464 | tf_op jit(solution)/shard_map/ppermute | solution.py:436
  51.0 0.7 %copy-start.16 = (f32[14,32,128]{2,1,0:T(8,128)}, f32[14,32,128]{2,1,0:T(8,128)S(1)}, u32[]{:S(2)}) copy-start(f32[14,32,128]{2,1,0:T(8,128)S(1)} %collective-permute-done.13.refs_3_) | copy-start | bytes 688132
  51.0 0.7 %copy-start.17 = (f32[3,32,128]{2,1,0:T(8,128)}, f32[3,32,128]{2,1,0:T(8,128)S(1)}, u32[]{:S(2)}) copy-start(f32[3,32,128]{2,1,0:T(8,128)S(1)} %collective-permute-done.14.refs_4_) | copy-start | bytes 147460
  51.0 0.8 %copy-start.15 = (f32[15,32,128]{2,1,0:T(8,128)}, f32[15,32,128]{2,1,0:T(8,128)S(1)}, u32[]{:S(2)}) copy-start(f32[15,32,128]{2,1,0:T(8,128)S(1)} %collective-permute-done.15.refs_5_) | copy-start | bytes 737284
  (2 other events, 1.3 us)

commit v3 on v2

--- a/solution.py
+++ b/solution.py
@@ -12,8 +12,10 @@
 ORDER = SEASONS * VARS
 REACH = 1
 NUGGET = 10.5
-CUTS = (4, 10)
-STAGES = ((0, 1), (-1,), (2,))
+LIMIT = 16 << 20
+COST = pl.CostEstimate(flops=1, bytes_accessed=1, transcendentals=0)
+CUTS = (6,)
+STAGES = ((0, -1), (1,))
 
 F32 = jnp.float32
 BF16 = jnp.bfloat16
@@ -39,42 +41,40 @@
     return m + half_id * (blocks - 1 - 2 * m)
 
 
-def pack_kernel(first, last, blocks, x_ref, same_ref, other_ref):
+def pack_kernel(cuts, blocks, x_ref, same_ref, other_ref, *chunk_refs):
     me = lax.axis_index("var")
     seasons = x_ref.shape[0] // blocks
-    for m in range(first, last):
-        for half_id, ref in ((me, same_ref), (1 - me, other_ref)):
-            rows = pl.ds(block_at(half_id, m, blocks), seasons, stride=blocks)
-            ref[m - first] = x_ref[rows, :]
-
-
-def pack(x, first, last, blocks):
+    for c in range(len(cuts) - 1):
+        for m in range(cuts[c], cuts[c + 1]):
+            for n, (half_id, ref) in enumerate(((me, same_ref), (1 - me, other_ref))):
+                value = x_ref[pl.ds(block_at(half_id, m, blocks), seasons, stride=blocks), :]
+                ref[m] = value
+                chunk_refs[2 * c + n][m - cuts[c]] = value
+
+
+def pack(x, cuts, blocks):
     seasons, width = x.shape[0] // blocks, x.shape[1]
+    counts = [cuts[-1]] + [last - first for first, last in zip(cuts[:-1], cuts[1:])]
+    shapes = [(count, seasons, width) for count in counts for _ in range(2)]
     return pl.pallas_call(
-        functools.partial(pack_kernel, first, last, blocks),
-        out_shape=[jax.ShapeDtypeStruct((last - first, seasons, width), F32)] * 2,
+        functools.partial(pack_kernel, cuts, blocks),
+        in_specs=[pl.BlockSpec(memory_space=VMEM)],
+        out_specs=[pl.BlockSpec(memory_space=VMEM)] * len(shapes),
+        out_shape=[jax.ShapeDtypeStruct(shape, F32) for shape in shapes],
+        compiler_params=pltpu.CompilerParams(vmem_limit_bytes=LIMIT),
+        cost_estimate=COST,
         name="pack",
     )(x)
 
 
-def prepare_kernel(blocks, w_ref, r_ref, w2_ref, rh_ref, rl_ref, scale_ref, held, sems):
+def prepare_kernel(blocks, w_ref, r_ref, w2_ref, rh_ref, rl_ref, scale_ref):
     me = lax.axis_index("var")
-    count, width = held.shape[0], held.shape[2]
-    copies = []
+    count, width = w2_ref.shape[0], w_ref.shape[2]
+    top = jnp.zeros((8, width), F32)
     for m in range(count):
         row = block_at(me, m, blocks)
-        group = [
-            pltpu.make_async_copy(w_ref.at[row, slot], held.at[m, place], sems.at[m, place])
-            for place, slot in enumerate((1 + me, 0, 2 - me))
-        ]
-        for copy in group:
-            copy.start()
-        copies.append(group)
-    top = jnp.zeros((8, width), F32)
-    for m in range(count):
-        for place, copy in enumerate(copies[m]):
-            copy.wait()
-            w = held[m, place]
+        for place, slot in enumerate((1 + me, 0, 2 - me)):
+            w = w_ref[row, slot]
             high, low = halves(w)
             lanes = slice(place * width, (place + 1) * width)
             w2_ref[m, :width, lanes] = high
@@ -106,7 +106,7 @@
     count = blocks // 2 + 1
     return pl.pallas_call(
         functools.partial(prepare_kernel, blocks),
-        in_specs=[pl.BlockSpec(memory_space=pl.ANY), pl.BlockSpec(memory_space=VMEM)],
+        in_specs=[pl.BlockSpec(memory_space=VMEM)] * 2,
         out_specs=[pl.BlockSpec(memory_space=VMEM)] * 4,
         out_shape=[
             jax.ShapeDtypeStruct((count, 2 * width, slots * width), BF16),
@@ -114,11 +114,8 @@
             jax.ShapeDtypeStruct((ORDER, ORDER), BF16),
             jax.ShapeDtypeStruct((8, width), F32),
         ],
-        scratch_shapes=[
-            VMEM((count, slots, width, width), F32),
-            pltpu.SemaphoreType.DMA((count, slots)),
-        ],
-        compiler_params=pltpu.CompilerParams(vmem_limit_bytes=20 << 20),
+        compiler_params=pltpu.CompilerParams(vmem_limit_bytes=LIMIT),
+        cost_estimate=COST,
         name="prepare",
     )(spatial, season)
 
@@ -138,43 +135,42 @@
     return lax.broadcasted_iota(jnp.int32, (rows, width), 0)
 
 
-def edge_kernel(blocks, parts, *refs):
-    w_ref, count_ref, *fields, out_ref, sems = refs
+def space_product(high, low, w2):
+    width = w2.shape[0] // 2
+    both = dot(high, w2, NT)
+    return both[:, :width] + both[:, width:] + dot(low, w2[:width], NT)
+
+
+def edge_kernel(blocks, parts, w2_ref, count_ref, *refs):
+    *fields, out_ref, held = refs
     me = lax.axis_index("var")
     seasons, width = fields[0].shape[1:]
-    row = block_at(me, 0, blocks)
-    copies = [
-        pltpu.make_async_copy(
-            w_ref.at[row, slot],
-            out_ref.at[pl.ds(2 * ORDER + place * width, width)],
-            sems.at[place],
-        )
-        for place, slot in enumerate((0, 2 - me))
-    ]
-    for copy in copies:
-        copy.start()
     for start, field in zip(row_starts(seasons, parts), fields):
         season = (iota(seasons, width) + lax.rem(start, SEASONS)).astype(F32)
         for m in range(2):
             seen = season >= SEASONS - count_ref[pl.ds(block_at(me, m, blocks), 1), :]
-            out_ref[pl.ds(m * ORDER + start, seasons), :] = jnp.where(seen, field[m], 0.0)
-    last = 2 * ORDER + 2 * width
-    out_ref[last:, :] = jnp.broadcast_to(count_ref[pl.ds(row, 1), :], (8, width))
-    for copy in copies:
-        copy.wait()
-
-
-def edge(spatial, count_rows, fields, parts):
-    blocks, _, width, _ = spatial.shape
+            held[m, pl.ds(start, seasons), :] = jnp.where(seen, field[m], 0.0)
+    high, low = halves(jnp.concatenate([held[0], held[1]], axis=1))
+    out_ref[:ORDER, :] = held[0]
+    out_ref[ORDER : 2 * ORDER, :] = space_product(high, low, w2_ref[0, :, width:])
+    out_ref[2 * ORDER :, :] = jnp.broadcast_to(
+        count_ref[pl.ds(block_at(me, 0, blocks), 1), :], (8, width)
+    )
+
+
+def edge(w2, count_rows, fields, parts):
+    blocks, width = count_rows.shape
+    whole = [pl.BlockSpec(memory_space=VMEM)]
     return pl.pallas_call(
         functools.partial(edge_kernel, blocks, parts),
-        in_specs=[pl.BlockSpec(memory_space=pl.ANY)]
-        + [pl.BlockSpec(memory_space=VMEM)] * (1 + len(fields)),
+        in_specs=whole * (2 + len(fields)),
         out_specs=pl.BlockSpec(memory_space=VMEM),
-        out_shape=jax.ShapeDtypeStruct((2 * ORDER + 2 * width + 8, width), F32),
-        scratch_shapes=[pltpu.SemaphoreType.DMA((2,))],
+        out_shape=jax.ShapeDtypeStruct((2 * ORDER + 8, width), F32),
+        scratch_shapes=[VMEM((2, ORDER, width), F32)],
+        compiler_params=pltpu.CompilerParams(vmem_limit_bytes=LIMIT),
+        cost_estimate=COST,
         name="edge",
-    )(spatial, count_rows, *fields)
+    )(w2, count_rows, *fields)
 
 
 def make_plan(cuts, half):
@@ -183,10 +179,10 @@
     for chunks in STAGES:
         new = []
         for c in chunks:
-            new += [-2, -1] if c < 0 else list(range(cuts[c], cuts[c + 1]))
+            new += [-1] if c < 0 else list(range(cuts[c], cuts[c + 1]))
         have_x |= set(new)
         ones = [
-            i for i in range(-1, half + 1) if i not in have_1 and {i - 1, i, i + 1} <= have_x
+            i for i in range(-1, half + 1) if i not in have_1 and {max(i - 1, -1), i, i + 1} <= have_x
         ]
         have_1 |= set(ones)
         twos = [i for i in range(half) if i not in have_2 and {i - 1, i, i + 1} <= have_1]
@@ -233,7 +229,8 @@
             del refs[:n]
             return out
 
-        field_refs = [take(slots) for _ in chunks]
+        near_refs = take(VARS)
+        far_refs = [take(slots - VARS) for _ in chunks]
         w2_ref, rh_ref, rl_ref, count_ref, sums_in = take(5)
         if not first:
             old_xh, old_xl, old_1h, old_1l = take(4)
@@ -247,7 +244,7 @@
 
         def count_row(i):
             if i == -1:
-                return edge_ref[2 * ORDER + 2 * width : 2 * ORDER + 2 * width + 1, :]
+                return edge_ref[2 * ORDER : 2 * ORDER + 1, :]
             return count_ref[pl.ds(block_at(me, i, blocks), 1), :]
 
         season = lax.rem(iota(ORDER, width), SEASONS).astype(F32)
@@ -264,12 +261,12 @@
 
         starts = row_starts(seasons, parts)
         total_0 = sums_in[0]
-        for c, fields in zip(chunks, field_refs):
+        for c, fars in zip(chunks, far_refs):
             places = [i for i in new if cuts[c] <= i < cuts[c + 1]]
-            for start, field in zip(starts, fields):
+            for k, start in enumerate(starts):
                 piece_season = (iota(seasons, width) + lax.rem(start, SEASONS)).astype(F32)
-                for n, i in enumerate(places):
-                    piece = field[n]
+                for i in places:
+                    piece = near_refs[k][i] if k < VARS else fars[k - VARS][i - cuts[c]]
                     if 0 <= i < half:
                         total_0 += fold(piece * piece)
                     seen = piece_season >= SEASONS - count_row(i)
@@ -277,26 +274,18 @@
                     xh[x_at[i], pl.ds(start, seasons), :] = high
                     xl[x_at[i], pl.ds(start, seasons), :] = low
         if outer:
-            for i, n in ((-1, 0), (-2, 1)):
-                xh[x_at[i]], xl[x_at[i]] = halves(edge_ref[n * ORDER : (n + 1) * ORDER, :])
+            xh[x_at[-1]], xl[x_at[-1]] = halves(edge_ref[:ORDER, :])
         sums_out[0] = total_0
 
         def space(i, high, low, at):
             if i >= 0:
                 hs = jnp.concatenate([high[at[i + d]] for d in (-1, 0, 1)], axis=1)
                 ls = jnp.concatenate([low[at[i + d]] for d in (-1, 0, 1)], axis=1)
-                both = dot(hs, w2_ref[i], NT)
-                return both[:, :width] + both[:, width:] + dot(ls, w2_ref[i, :width, :], NT)
+                return space_product(hs, ls, w2_ref[i])
             near = w2_ref[0, :width, :width]
-            total = dot(high[at[0]], near, NN)
+            total = edge_ref[ORDER : 2 * ORDER, :] + dot(high[at[0]], near, NN)
             total += dot(high[at[0]], w2_ref[0, width:, :width], NN)
-            total += dot(low[at[0]], near, NN)
-            for n, j in enumerate((-1, -2)):
-                begin = 2 * ORDER + n * width
-                wh, wl = halves(edge_ref[begin : begin + width, :])
-                total += dot(high[at[j]], wh, NT) + dot(high[at[j]], wl, NT)
-                total += dot(low[at[j]], wh, NT)
-            return total
+            return total + dot(low[at[0]], near, NN)
 
         def mix(parts_of):
             zh, zl = halves(jnp.concatenate(parts_of, axis=1))
@@ -356,23 +345,26 @@
         in_specs=[pl.BlockSpec(memory_space=VMEM)] * len(operands),
         out_shape=outs,
         scratch_shapes=scratch,
-        compiler_params=pltpu.CompilerParams(vmem_limit_bytes=24 << 20),
+        compiler_params=pltpu.CompilerParams(vmem_limit_bytes=LIMIT),
+        cost_estimate=COST,
         name="stage",
     )(*operands)
 
 
-def finish_kernel(plan, blocks, gathered_ref, x_ref, *refs):
+def finish_kernel(plan, blocks, tiles, *refs):
+    refs = list(refs)
     count = len(plan)
+    gathered, refs = refs[:tiles], refs[tiles:]
+    fields, refs = refs[:2], refs[2:]
     mine, theirs = refs[:count], refs[count : 2 * count]
-    x_out, r_out = refs[2 * count :]
-    seasons = x_ref.shape[0] // blocks
+    x_out, r_out, x_held, r_held, sems = refs[2 * count :]
     half = blocks // 2
     me = lax.axis_index("var")
 
     def total(v):
         return jnp.sum(v, axis=1, keepdims=True)
 
-    tuples = [gathered_ref[j] for j in range(gathered_ref.shape[0])]
+    tuples = [ref[j] for ref in gathered for j in range(ref.shape[0])]
     top = functools.reduce(jnp.maximum, [t[4:5] for t in tuples])
     sums = [0.0, 0.0, 0.0, 0.0]
     for t in tuples:
@@ -404,26 +396,44 @@
         inner = in_half(ones, half)
         one_at.update({i: (m, n) for n, i in enumerate(inner)})
         two_at.update({i: (m, len(inner) + n) for n, i in enumerate(twos)})
-    for half_id, held, t in ((me, mine, tuples[0]), (1 - me, theirs, tuples[1])):
+    copies = []
+    for side, (half_id, held, t) in enumerate(((me, mine, tuples[0]), (1 - me, theirs, tuples[1]))):
         ratio = (t[4:5] / top)[:, :1]
         x_1h, r_1h, r_2h = x_1 * ratio, r_1 * ratio, r_2 * ratio * ratio
         for i in range(half):
-            rows = pl.ds(block_at(half_id, i, blocks), seasons, stride=blocks)
-            x = x_ref[rows, :]
+            x = fields[side][i]
             m, n = one_at[i]
             one = held[m][n]
             m, n = two_at[i]
             two = held[m][n]
-            x_out[rows, :] = x_0 * x + x_1h * one
-            r_out[rows, :] = r_0 * x + r_1h * one + r_2h * two
-
-
-def finish(plan, blocks, gathered, x, mine, theirs):
+            at = side * half + i
+            x_held[at] = x_0 * x + x_1h * one
+            r_held[at] = r_0 * x + r_1h * one + r_2h * two
+            row = block_at(half_id, i, blocks)
+            for n, (source, target) in enumerate(((x_held, x_out), (r_held, r_out))):
+                copy = pltpu.make_async_copy(
+                    source.at[at], target.at[:, row, 0, :], sems.at[n, at]
+                )
+                copy.start()
+                copies.append(copy)
+    for copy in copies:
+        copy.wait()
+
+
+def finish(plan, shape, gathered, packs, mine, theirs):
+    seasons, blocks, _, width = shape
+    operands = [*gathered, *packs, *mine, *theirs]
     return pl.pallas_call(
-        functools.partial(finish_kernel, plan, blocks),
-        out_shape=[jax.ShapeDtypeStruct(x.shape, F32)] * 2,
+        functools.partial(finish_kernel, plan, blocks, len(gathered)),
+        in_specs=[pl.BlockSpec(memory_space=VMEM)] * len(operands),
+        out_specs=[pl.BlockSpec(memory_space=pltpu.HBM)] * 2,
+        out_shape=[jax.ShapeDtypeStruct(shape, F32)] * 2,
+        scratch_shapes=[VMEM((blocks, seasons, width), F32)] * 2
+        + [pltpu.SemaphoreType.DMA((2, blocks))],
+        compiler_params=pltpu.CompilerParams(vmem_limit_bytes=LIMIT),
+        cost_estimate=COST,
         name="finish",
-    )(gathered, x, *mine, *theirs)
+    )(*operands)
 
 
 def from_group(value, step, swap):
@@ -445,18 +455,18 @@
 
 
 def gather_tiles(value):
-    have = jnp.concatenate([value, from_group(value, 0, 1)], axis=0)
+    found = [value, from_group(value, 0, 1)]
     size = lax.axis_size("space")
     if size & (size - 1):
         me = lax.axis_index("space")
-        all_tiles = lax.all_gather(have, "space", axis=0, tiled=True)
-        return jnp.roll(all_tiles, -me * VARS, axis=0)
+        tiles = lax.all_gather(jnp.concatenate(found, axis=0), "space", axis=0, tiled=True)
+        return [jnp.roll(tiles, -me * VARS, axis=0)]
     hop = 1
     while hop < size:
-        other = lax.ppermute(have, "space", [(i, i ^ hop) for i in range(size)])
-        have = jnp.concatenate([have, other], axis=0)
+        have = jnp.concatenate(found, axis=0)
+        found.append(lax.ppermute(have, "space", [(i, i ^ hop) for i in range(size)]))
         hop *= 2
-    return have
+    return found
 
 
 def body(right_side, spatial, columns, counts, season_cov):
@@ -471,25 +481,21 @@
     x = right_side.reshape(seasons * blocks, width)
     count_rows = jnp.broadcast_to(counts.astype(F32)[:, None], (blocks, width))
 
-    chunks = []
-    for first, last in zip(cuts[:-1], cuts[1:]):
-        same, other = pack(x, first, last, blocks)
-        chunks.append(
-            [
-                from_group(other if w else same, d, w) if d or w else same
-                for d in range(parts)
-                for w in range(VARS)
-            ]
-        )
+    same, other, *packs = pack(x, cuts, blocks)
+    close = [same, from_group(other, 0, 1)]
+    chunks = [
+        [from_group(pair[w], d, w) for d in range(1, parts) for w in range(VARS)]
+        for pair in zip(packs[0::2], packs[1::2])
+    ]
     w2, rh, rl, scale = prepare(
         spatial, season_cov.transpose(0, 1, 3, 2).reshape(SEASONS * VARS * VARS, SEASONS)
     )
-    outer = across_edge(edge(spatial, count_rows, chunks[0], parts))
+    outer = across_edge(edge(w2, count_rows, close + chunks[0], parts))
 
     sums = jnp.zeros((4, 8, width), F32)
     mine, theirs, kept = [], [], []
     for m, stage in enumerate(STAGES):
-        operands = [f for c in stage if c >= 0 for f in chunks[c]]
+        operands = close + [f for c in stage if c >= 0 for f in chunks[c]]
         operands += [w2, rh, rl, count_rows, sums] + kept + [outer] * (-1 in stage)
         out = run_stage(plan, cuts, m, blocks, parts, seasons, width, operands)
         sums, kept = out[0], list(out[3:])
@@ -497,7 +503,7 @@
         theirs.append(from_group(out[2], 0, 1))
     tile = jnp.concatenate([jnp.sum(sums, axis=1), scale[4:]], axis=0)[None]
     gathered = gather_tiles(tile)
-    x_out, r_out = finish(plan, blocks, gathered, x, mine, theirs)
+    x_out, r_out = finish(plan, (seasons, blocks, 1, width), gathered, [same, other], mine, theirs)
     return x_out.reshape(right_side.shape), r_out.reshape(right_side.shape)
 
 

time: 56 us -> 35.7 us (0.64)
  Pallas kernels: 23.6 us -> 8.3 us
  starting transfers between devices: 15.9 us -> 12.5 us
  waiting for transfers between devices: 7.63 us -> 9.08 us
  local copies, waits for them, and re-layouts: 6.23 us -> 4.81 us
  other arithmetic: 1.29 us -> 0.04 us
    pallas_call x5 -> x3, Pallas kernels: 11.9 us -> 2.25 us  [the longest x1 1.69 us: finish(): pl.pallas_call(functools.partial(finish_kernel, plan, blocks, len(gathere...]
    pallas_call x1, Pallas kernels: 5.76 us -> 0.71 us  [prepare(): pl.pallas_call(functools.partial(prepare_kernel, blocks), in_specs=[pl.Bl...]
    ppermute x13 -> x8, starting transfers between devices: 10.9 us -> 7.17 us  [from_group(): return lax.ppermute(value, ('season', 'var'), pairs)]
    ppermute x13 -> x8, waiting for transfers between devices: 4.03 us -> 5.43 us  [from_group(): return lax.ppermute(value, ('season', 'var'), pairs)]
    unnamed x36 -> x8, local copies, waits for them, and re-layouts: 5.56 us -> 4.73 us
    pallas_call x3 -> x2, Pallas kernels: 6 us -> 5.34 us  [run_stage(): pl.pallas_call(kernel, in_specs=[pl.BlockSpec(memory_space=VMEM)] * len(o...]
    convert_element_type x1, other arithmetic: 0.66 us -> 0.01 us  [body(): count_rows = jnp.broadcast_to(counts.astype(F32)[:, None], (blocks, width))]
    concatenate x3 -> x2, other arithmetic: 0.61 us -> 0.01 us  [gather_tiles(): have = jnp.concatenate(found, axis=0)]
  transfers between devices with their start and end apart: 16 -> 11, of which waited for: 5 -> 5; matrix products, arithmetic and copies ran while one was open for 2% -> 0% of each run, Pallas kernels for 23% -> 7%
where the time goes in v3:
time: 35.7 us; the launch traced here: 35.5 us
  starting transfers between devices  12.5 us (35%)
  waiting for transfers between devices  9.08 us (25%)
  Pallas kernels  8.3 us (23%)
  local copies, waits for them, and re-layouts  4.81 us (13%)
  between operations  0.75 us (2%)
    ppermute x8, starting transfers between devices, from_group(): return lax.ppermute(value, ('season', 'var'), pairs)  7.17 us
    ppermute x8, waiting for transfers between devices, from_group(): return lax.ppermute(value, ('season', 'var'), pairs)  5.43 us
    pallas_call x2, Pallas kernels, run_stage(): pl.pallas_call(kernel, in_specs=[pl.BlockSpec(memory_space=VMEM)] * len(o...  5.34 us
    unnamed x8, local copies, waits for them, and re-layouts  4.73 us
    ppermute x2, starting transfers between devices, gather_tiles(): lax.ppermute(have, 'space', [(i, i ^ hop) for i in range(size)])  4.66 us
    ppermute x2, waiting for transfers between devices, gather_tiles(): lax.ppermute(have, 'space', [(i, i ^ hop) for i in range(size)])  3.64 us
    pallas_call x1, Pallas kernels, finish(): pl.pallas_call(functools.partial(finish_kernel, plan, blocks, len(gathere...  1.69 us
    pallas_call x1, Pallas kernels, prepare(): pl.pallas_call(functools.partial(prepare_kernel, blocks), in_specs=[pl.Bl...  0.71 us
  transfers between devices with their start and end apart: 11, of which 5 were waited for; matrix products, arithmetic and copies ran while one was open for 0% of the time, Pallas kernels for 7%

profile of v3, /device:TPU:0, one launch (start us, length us, event | category | flops | bytes accessed | tf_op | source)
XLA Modules:
  0.0 35.5 jit_solution(15779606591637640735)
XLA Ops:
  0.6 1.0 %copy-done.1 = f32[32,1,4096]{2,1,0:T(1,128)S(1)} copy-done((f32[32,1,4096]{2,1,0:T(1,128)S(1)}, f32[32,1,4096]{2,1,0:T(1,128)}, u32[]{:S(2)}) %copy-start.1) | copy-done | bytes 524312
  1.7 0.3 pack.1
  2.0 0.5 %collective-permute-start = (f32[18,32,128]{2,1,0:T(8,128)S(1)}, f32[18,32,128]{2,1,0:T(8,128)S(1)}, u32[]{:S(2)}, u32[]{:S(2)}) collective-permute-start(f32[18,32,128]{2,1,0:T(8,128)S(1)} %get-tuple-element.25.refs_5_), channel_id=1, source_target_pairs={{1,0},{0,1},{3,2},{2,3},{5,4},{4,5},{7,6},{6,7},{9,8},{8,9},{11,10... | collective-permute-start | bytes 884744 | tf_op jit(solution)/shard_map/ppermute | solution.py:446
  2.6 2.6 %collective-permute-start.3 = (f32[6,32,128]{2,1,0:T(8,128)S(1)}, f32[6,32,128]{2,1,0:T(8,128)S(1)}, u32[]{:S(2)}, u32[]{:S(2)}) collective-permute-start(f32[6,32,128]{2,1,0:T(8,128)S(1)} %get-tuple-element.31), channel_id=1, source_target_pairs={{2,0},{3,1},{0,2},{1,3},{6,4},{7,5},{4,6},{5,7},{10,8},{11,9},{8,1... | collective-permute-start | bytes 294920 | tf_op jit(solution)/shard_map/ppermute | solution.py:446
  5.1 0.1 collective-permute-start.4
  5.2 1.7 %collective-permute-start.1 = (f32[12,32,128]{2,1,0:T(8,128)S(1)}, f32[12,32,128]{2,1,0:T(8,128)S(1)}, u32[]{:S(2)}, u32[]{:S(2)}) collective-permute-start(f32[12,32,128]{2,1,0:T(8,128)S(1)} %get-tuple-element.26), channel_id=1, source_target_pairs={{2,0},{3,1},{0,2},{1,3},{6,4},{7,5},{4,6},{5,7},{10,8},{11,9},{8,1... | collective-permute-start | bytes 589832 | tf_op jit(solution)/shard_map/ppermute | solution.py:446
  6.9 0.0 collective-permute-start.2
  6.9 2.8 %copy-done = f32[32,3,128,128]{3,2,1,0:T(8,128)S(1)} copy-done((f32[32,3,128,128]{3,2,1,0:T(8,128)S(1)}, f32[32,3,128,128]{3,2,1,0:T(8,128)}, u32[]{:S(2)}) %copy-start) | copy-done | bytes 6291480
  9.7 0.9 %copy-done.2 = f32[64,2,64,2]{2,3,1,0:T(2,128)S(1)} copy-done((f32[64,2,64,2]{2,3,1,0:T(2,128)S(1)}, f32[64,2,64,2]{2,3,1,0:T(2,128)}, u32[]{:S(2)}) %copy-start.2) | copy-done | bytes 65560
  10.6 0.7 %prepare.1 = (bf16[17,256,384]{2,1,0:T(8,128)(2,1)S(1)}, bf16[128,128]{1,0:T(8,128)(2,1)S(1)}, bf16[128,128]{1,0:T(8,128)(2,1)S(1)}, f32[8,128]{1,0:T(8,128)S(1)}) custom-call(f32[32,3,128,128]{3,2,1,0:T(8,128)S(1)} %copy-done, f32[256,64]{1,0:T(8,128)S(1)} %bitcast.9), custom_call_target="tpu_custom_call" | custom-call | flops 1 | bytes 1 | tf_op jit(solution)/shard_map/prepare/pallas_call | solution.py:107
  11.4 0.0 collective-permute-done.3.refs_2_
  11.4 0.0 collective-permute-done.4.refs_3_
  11.4 0.0 collective-permute-done.refs_1_
  11.4 0.1 broadcast_in_dim.12.count_ref.refs_7_
  11.5 0.2 edge.1
  11.7 0.7 %collective-permute-start.5 = (f32[264,128]{1,0:T(8,128)S(1)}, f32[264,128]{1,0:T(8,128)S(1)}, u32[]{:S(2)}, u32[]{:S(2)}) collective-permute-start(f32[264,128]{1,0:T(8,128)S(1)} %edge.1), channel_id=1, source_target_pairs={{1,4},{4,1},{5,8},{8,5},{9,12},{12,9},{3,6},{6,3},{7,10},{10,7},{1... | collective-permute-start | bytes 405512 | tf_op jit(solution)/shard_map/ppermute | solution.py:454
  12.4 0.0 collective-permute-done.5.refs_9_
  12.4 1.7 %stage.2 = (f32[4,8,128]{2,1,0:T(8,128)S(1)}, f32[9,32,128]{2,1,0:T(8,128)S(1)}, f32[9,32,128]{2,1,0:T(8,128)S(1)}, bf16[2,128,128]{2,1,0:T(8,128)(2,1)S(1)}, bf...) custom-call(f32[18,32,128]{2,1,0:T(8,128)S(1)} %get-tuple-element.24.refs_0_.refs_, ...), custom_call_target="tpu_custom_call" | custom-call | flops 1 | bytes 1 | tf_op jit(solution)/shard_map/stage/pallas_call | solution.py:343
  14.1 1.0 %collective-permute-done.1.refs_2_ = f32[12,32,128]{2,1,0:T(8,128)S(1)} collective-permute-done((f32[12,32,128]{2,1,0:T(8,128)S(1)}, f32[12,32,128]{2,1,0:T(8,128)S(1)}, u32[]{:S(2)}, u32[]{:S(2)}) %collective-permute-start.1) | collective-permute-done | bytes 196640 | tf_op jit(solution)/shard_map/ppermute | solution.py:446
  15.1 3.7 %collective-permute-done.2.refs_3_ = f32[12,32,128]{2,1,0:T(8,128)S(1)} collective-permute-done((f32[12,32,128]{2,1,0:T(8,128)S(1)}, f32[12,32,128]{2,1,0:T(8,128)S(1)}, u32[]{:S(2)}, u32[]{:S(2)}) %collective-permute-start.2) | collective-permute-done | bytes 196640 | tf_op jit(solution)/shard_map/ppermute | solution.py:446
  18.8 3.7 %stage.3 = (f32[4,8,128]{2,1,0:T(8,128)S(1)}, f32[23,32,128]{2,1,0:T(8,128)S(1)}, f32[23,32,128]{2,1,0:T(8,128)S(1)}) custom-call(f32[18,32,128]{2,1,0:T(8,128)S(1)} %get-tuple-element.24.refs_0_.refs_4_, f32[18,32,128]{2,1,0:T(8,128)S(1)} %collective-permute-done.refs_1_, f32[12,32,128]{2,1,0:T(8,128)S(1)} %collective-permute-done.1.refs_2_, ...), custom_call_target="tpu_custom_call" | custom-call | flops 1 | bytes 1 | tf_op jit(solution)/shard_map/stage/pallas_call | solution.py:343
  22.4 1.7 %collective-permute-start.10 = (f32[23,32,128]{2,1,0:T(8,128)S(1)}, f32[23,32,128]{2,1,0:T(8,128)S(1)}, u32[]{:S(2)}, u32[]{:S(2)}) collective-permute-start(f32[23,32,128]{2,1,0:T(8,128)S(1)} %get-tuple-element.43), channel_id=1, source_target_pairs={{1,0},{0,1},{3,2},{2,3},{5,4},{4,5},{7,6},{6,7},{9,8},{8,9},{11,10... | collective-permute-start | bytes 1130504 | tf_op jit(solution)/shard_map/ppermute | solution.py:446
  24.2 0.1 collective-permute-start.6
  24.3 0.5 %collective-permute-start.9 = (f32[9,32,128]{2,1,0:T(8,128)S(1)}, f32[9,32,128]{2,1,0:T(8,128)S(1)}, u32[]{:S(2)}, u32[]{:S(2)}) collective-permute-start(f32[9,32,128]{2,1,0:T(8,128)S(1)} %get-tuple-element.42), channel_id=1, source_target_pairs={{1,0},{0,1},{3,2},{2,3},{5,4},{4,5},{7,6},{6,7},{9,8},{8,9},{11,10... | collective-permute-start | bytes 442376 | tf_op jit(solution)/shard_map/ppermute | solution.py:446
  24.8 0.7 %collective-permute-done.6.refs_1_ = f32[1,8,128]{2,1,0:T(8,128)S(1)} collective-permute-done((f32[1,8,128]{2,1,0:T(8,128)S(1)}, f32[1,8,128]{2,1,0:T(8,128)S(1)}, u32[]{:S(2)}, u32[]{:S(2)}) %collective-permute-start.6) | collective-permute-done | bytes 4128 | tf_op jit(solution)/shard_map/ppermute | solution.py:446
  25.5 1.8 %collective-permute-start.7 = (f32[2,8,128]{2,1,0:T(8,128)S(1)}, f32[2,8,128]{2,1,0:T(8,128)S(1)}, u32[]{:S(2)}, u32[]{:S(2)}) collective-permute-start(f32[2,8,128]{2,1,0:T(8,128)S(1)} %pad_maximum_fusion.1), channel_id=1, source_target_pairs={{0,4},{4,0},{8,12},{12,8},{1,5},{5,1},{9,13},{13,9},{2,6},{6,2},{1... | collective-permute-start | bytes 24584 | tf_op jit(solution)/shard_map/ppermute | solution.py:467
  27.3 1.8 %collective-permute-done.7.refs_2_ = f32[2,8,128]{2,1,0:T(8,128)S(1)} collective-permute-done((f32[2,8,128]{2,1,0:T(8,128)S(1)}, f32[2,8,128]{2,1,0:T(8,128)S(1)}, u32[]{:S(2)}, u32[]{:S(2)}) %collective-permute-start.7) | collective-permute-done | bytes 8224 | tf_op jit(solution)/shard_map/ppermute | solution.py:467
  29.2 2.8 %collective-permute-start.8 = (f32[4,8,128]{2,1,0:T(8,128)S(1)}, f32[4,8,128]{2,1,0:T(8,128)S(1)}, u32[]{:S(2)}, u32[]{:S(2)}) collective-permute-start(f32[4,8,128]{2,1,0:T(8,128)S(1)} %pad_maximum_fusion), channel_id=1, source_target_pairs={{0,8},{4,12},{8,0},{12,4},{1,9},{5,13},{9,1},{13,5},{2,10},{6,14},... | collective-permute-start | bytes 49160 | tf_op jit(solution)/shard_map/ppermute | solution.py:467
  32.0 1.8 %collective-permute-done.8.refs_3_ = f32[4,8,128]{2,1,0:T(8,128)S(1)} collective-permute-done((f32[4,8,128]{2,1,0:T(8,128)S(1)}, f32[4,8,128]{2,1,0:T(8,128)S(1)}, u32[]{:S(2)}, u32[]{:S(2)}) %collective-permute-start.8) | collective-permute-done | bytes 16416 | tf_op jit(solution)/shard_map/ppermute | solution.py:467
  33.8 0.0 collective-permute-done.9.refs_8_
  33.8 0.0 collective-permute-done.10.refs_9_
  33.8 1.7 %finish.1 = (f32[32,32,1,128]{3,2,1,0:T(1,128)}, f32[32,32,1,128]{3,2,1,0:T(1,128)}) custom-call(f32[1,8,128]{2,1,0:T(8,128)S(1)} %maximum_bitcast_fusion.refs_0_, f32[1,8,128]{2,1,0:T(8,128)S(1)} %collective-permute-done.6.refs_1_, f32[2,8,128]{2,1,0:T(8,128)S(1)} %collective-permute-done.7.refs_2_, f32[4,8,128]{2,1,0:T(8,128)S(1)} %collective-permute-done.8.refs_3_, ...), custom_call_target="tpu_custom_call" | custom-call | flops 1 | bytes 1 | tf_op jit(solution)/shard_map/finish/pallas_call | solution.py:426
  (12 shorter events, 0.1 us)
Async XLA Ops:
  0.6 10.7 %copy-start.3 = (s32[32]{0:T(128)S(1)}, s32[32]{0:T(128)}, u32[]{:S(2)}) copy-start(s32[32]{0:T(128)} %param.7) | copy-start | bytes 388
  0.6 1.0 %copy-start.1 = (f32[32,1,4096]{2,1,0:T(1,128)S(1)}, f32[32,1,4096]{2,1,0:T(1,128)}, u32[]{:S(2)}) copy-start(f32[32,1,4096]{2,1,0:T(1,128)} %param.5) | copy-start | bytes 1572868
  2.0 9.4 %collective-permute-start = (f32[18,32,128]{2,1,0:T(8,128)S(1)}, f32[18,32,128]{2,1,0:T(8,128)S(1)}, u32[]{:S(2)}, u32[]{:S(2)}) collective-permute-start(f32[18,32,128]{2,1,0:T(8,128)S(1)} %get-tuple-element.25.refs_5_), channel_id=1, source_target_pairs={{1,0},{0,1},{3,2},{2,3},{5,4},{4,5},{7,6},{6,7},{9,8},{8,9},{11,10... | collective-permute-start | bytes 884744 | tf_op jit(solution)/shard_map/ppermute | solution.py:446
  2.6 8.8 %collective-permute-start.3 = (f32[6,32,128]{2,1,0:T(8,128)S(1)}, f32[6,32,128]{2,1,0:T(8,128)S(1)}, u32[]{:S(2)}, u32[]{:S(2)}) collective-permute-start(f32[6,32,128]{2,1,0:T(8,128)S(1)} %get-tuple-element.31), channel_id=1, source_target_pairs={{2,0},{3,1},{0,2},{1,3},{6,4},{7,5},{4,6},{5,7},{10,8},{11,9},{8,1... | collective-permute-start | bytes 294920 | tf_op jit(solution)/shard_map/ppermute | solution.py:446
  5.1 6.3 %collective-permute-start.4 = (f32[6,32,128]{2,1,0:T(8,128)S(1)}, f32[6,32,128]{2,1,0:T(8,128)S(1)}, u32[]{:S(2)}, u32[]{:S(2)}) collective-permute-start(f32[6,32,128]{2,1,0:T(8,128)S(1)} %get-tuple-element.32), channel_id=1, source_target_pairs={{3,0},{2,1},{1,2},{0,3},{7,4},{6,5},{5,6},{4,7},{11,8},{10,9},{9,1... | collective-permute-start | bytes 294920 | tf_op jit(solution)/shard_map/ppermute | solution.py:446
  5.2 9.9 %collective-permute-start.1 = (f32[12,32,128]{2,1,0:T(8,128)S(1)}, f32[12,32,128]{2,1,0:T(8,128)S(1)}, u32[]{:S(2)}, u32[]{:S(2)}) collective-permute-start(f32[12,32,128]{2,1,0:T(8,128)S(1)} %get-tuple-element.26), channel_id=1, source_target_pairs={{2,0},{3,1},{0,2},{1,3},{6,4},{7,5},{4,6},{5,7},{10,8},{11,9},{8,1... | collective-permute-start | bytes 589832 | tf_op jit(solution)/shard_map/ppermute | solution.py:446
  6.9 11.8 %collective-permute-start.2 = (f32[12,32,128]{2,1,0:T(8,128)S(1)}, f32[12,32,128]{2,1,0:T(8,128)S(1)}, u32[]{:S(2)}, u32[]{:S(2)}) collective-permute-start(f32[12,32,128]{2,1,0:T(8,128)S(1)} %get-tuple-element.27), channel_id=1, source_target_pairs={{3,0},{2,1},{1,2},{0,3},{7,4},{6,5},{5,6},{4,7},{11,8},{10,9},{9,1... | collective-permute-start | bytes 589832 | tf_op jit(solution)/shard_map/ppermute | solution.py:446
  6.9 2.8 %copy-start = (f32[32,3,128,128]{3,2,1,0:T(8,128)S(1)}, f32[32,3,128,128]{3,2,1,0:T(8,128)}, u32[]{:S(2)}) copy-start(f32[32,3,128,128]{3,2,1,0:T(8,128)} %w_ref.1) | copy-start | bytes 18874372
  9.7 0.9 %copy-start.2 = (f32[64,2,64,2]{2,3,1,0:T(2,128)S(1)}, f32[64,2,64,2]{2,3,1,0:T(2,128)}, u32[]{:S(2)}) copy-start(f32[64,2,64,2]{2,3,1,0:T(2,128)} %param.8) | copy-start | bytes 196612
  11.7 0.7 %collective-permute-start.5 = (f32[264,128]{1,0:T(8,128)S(1)}, f32[264,128]{1,0:T(8,128)S(1)}, u32[]{:S(2)}, u32[]{:S(2)}) collective-permute-start(f32[264,128]{1,0:T(8,128)S(1)} %edge.1), channel_id=1, source_target_pairs={{1,4},{4,1},{5,8},{8,5},{9,12},{12,9},{3,6},{6,3},{7,10},{10,7},{1... | collective-permute-start | bytes 405512 | tf_op jit(solution)/shard_map/ppermute | solution.py:454
  22.4 11.4 %collective-permute-start.10 = (f32[23,32,128]{2,1,0:T(8,128)S(1)}, f32[23,32,128]{2,1,0:T(8,128)S(1)}, u32[]{:S(2)}, u32[]{:S(2)}) collective-permute-start(f32[23,32,128]{2,1,0:T(8,128)S(1)} %get-tuple-element.43), channel_id=1, source_target_pairs={{1,0},{0,1},{3,2},{2,3},{5,4},{4,5},{7,6},{6,7},{9,8},{8,9},{11,10... | collective-permute-start | bytes 1130504 | tf_op jit(solution)/shard_map/ppermute | solution.py:446
  24.2 1.3 %collective-permute-start.6 = (f32[1,8,128]{2,1,0:T(8,128)S(1)}, f32[1,8,128]{2,1,0:T(8,128)S(1)}, u32[]{:S(2)}, u32[]{:S(2)}) collective-permute-start(f32[1,8,128]{2,1,0:T(8,128)S(1)} %maximum_bitcast_fusion.refs_0_), channel_id=1, source_target_pairs={{1,0},{0,1},{3,2},{2,3},{5,4},{4,5},{7,6},{6,7},{9,8},{8,9},{11,10... | collective-permute-start | bytes 12296 | tf_op jit(solution)/shard_map/ppermute | solution.py:446
  24.3 9.5 %collective-permute-start.9 = (f32[9,32,128]{2,1,0:T(8,128)S(1)}, f32[9,32,128]{2,1,0:T(8,128)S(1)}, u32[]{:S(2)}, u32[]{:S(2)}) collective-permute-start(f32[9,32,128]{2,1,0:T(8,128)S(1)} %get-tuple-element.42), channel_id=1, source_target_pairs={{1,0},{0,1},{3,2},{2,3},{5,4},{4,5},{7,6},{6,7},{9,8},{8,9},{11,10... | collective-permute-start | bytes 442376 | tf_op jit(solution)/shard_map/ppermute | solution.py:446
  25.5 3.7 %collective-permute-start.7 = (f32[2,8,128]{2,1,0:T(8,128)S(1)}, f32[2,8,128]{2,1,0:T(8,128)S(1)}, u32[]{:S(2)}, u32[]{:S(2)}) collective-permute-start(f32[2,8,128]{2,1,0:T(8,128)S(1)} %pad_maximum_fusion.1), channel_id=1, source_target_pairs={{0,4},{4,0},{8,12},{12,8},{1,5},{5,1},{9,13},{13,9},{2,6},{6,2},{1... | collective-permute-start | bytes 24584 | tf_op jit(solution)/shard_map/ppermute | solution.py:467
  29.2 4.6 %collective-permute-start.8 = (f32[4,8,128]{2,1,0:T(8,128)S(1)}, f32[4,8,128]{2,1,0:T(8,128)S(1)}, u32[]{:S(2)}, u32[]{:S(2)}) collective-permute-start(f32[4,8,128]{2,1,0:T(8,128)S(1)} %pad_maximum_fusion), channel_id=1, source_target_pairs={{0,8},{4,12},{8,0},{12,4},{1,9},{5,13},{9,1},{13,5},{2,10},{6,14},... | collective-permute-start | bytes 49160 | tf_op jit(solution)/shard_map/ppermute | solution.py:467

commit v4 on v3

--- a/solution.py
+++ b/solution.py
@@ -13,9 +13,11 @@
 REACH = 1
 NUGGET = 10.5
 LIMIT = 16 << 20
+GROUP = 16
+ROOMY = 50 << 20
 COST = pl.CostEstimate(flops=1, bytes_accessed=1, transcendentals=0)
-CUTS = (6,)
-STAGES = ((0, -1), (1,))
+CUTS = (3, 14)
+STAGES = ((0, 1), (-1, 2))
 
 F32 = jnp.float32
 BF16 = jnp.bfloat16
@@ -67,23 +69,43 @@
     )(x)
 
 
-def prepare_kernel(blocks, w_ref, r_ref, w2_ref, rh_ref, rl_ref, scale_ref):
+def prepare_kernel(
+    blocks, w_ref, r_ref, w2_ref, rh_ref, rl_ref, scale_ref, held, r_held, sems, r_sem
+):
     me = lax.axis_index("var")
-    count, width = w2_ref.shape[0], w_ref.shape[2]
-    top = jnp.zeros((8, width), F32)
+    count, width = held.shape[0], held.shape[2]
+    r_copy = pltpu.make_async_copy(r_ref, r_held, r_sem)
+    copies = []
     for m in range(count):
         row = block_at(me, m, blocks)
-        for place, slot in enumerate((1 + me, 0, 2 - me)):
-            w = w_ref[row, slot]
+        copies.append(
+            [
+                pltpu.make_async_copy(w_ref.at[row, slot], held.at[m, place], sems.at[m, place])
+                for place, slot in enumerate((1 + me, 0, 2 - me))
+            ]
+        )
+    for m, group in enumerate(copies):
+        for copy in group:
+            copy.start(priority=m % 2)
+    r_copy.start(priority=1)
+    top = jnp.zeros((8, width), F32)
+    for m, group in enumerate(copies):
+        for place, copy in enumerate(group):
+            copy.wait()
+            w = held[m, place]
             high, low = halves(w)
             lanes = slice(place * width, (place + 1) * width)
             w2_ref[m, :width, lanes] = high
             w2_ref[m, width:, lanes] = low
             top = jnp.maximum(top, jnp.max(jnp.abs(w).reshape(-1, 8, width), axis=0))
+    r_copy.wait()
     r = jnp.concatenate(
         [
             jnp.concatenate(
-                [r_ref[pl.ds(VARS * v + w, SEASONS, stride=VARS * VARS), :] for w in range(VARS)],
+                [
+                    r_held[pl.ds(VARS * v + w, SEASONS, stride=VARS * VARS), :]
+                    for w in range(VARS)
+                ],
                 axis=1,
             )
             for v in range(VARS)
@@ -106,7 +128,7 @@
     count = blocks // 2 + 1
     return pl.pallas_call(
         functools.partial(prepare_kernel, blocks),
-        in_specs=[pl.BlockSpec(memory_space=VMEM)] * 2,
+        in_specs=[pl.BlockSpec(memory_space=pl.ANY)] * 2,
         out_specs=[pl.BlockSpec(memory_space=VMEM)] * 4,
         out_shape=[
             jax.ShapeDtypeStruct((count, 2 * width, slots * width), BF16),
@@ -114,7 +136,13 @@
             jax.ShapeDtypeStruct((ORDER, ORDER), BF16),
             jax.ShapeDtypeStruct((8, width), F32),
         ],
-        compiler_params=pltpu.CompilerParams(vmem_limit_bytes=LIMIT),
+        scratch_shapes=[
+            VMEM((count, slots, width, width), F32),
+            VMEM(season.shape, F32),
+            pltpu.SemaphoreType.DMA((count, slots)),
+            pltpu.SemaphoreType.DMA,
+        ],
+        compiler_params=pltpu.CompilerParams(vmem_limit_bytes=ROOMY),
         cost_estimate=COST,
         name="prepare",
     )(spatial, season)
@@ -137,8 +165,8 @@
 
 def space_product(high, low, w2):
     width = w2.shape[0] // 2
-    both = dot(high, w2, NT)
-    return both[:, :width] + both[:, width:] + dot(low, w2[:width], NT)
+    both = dot(jnp.concatenate([high, low], axis=0), w2, NT)
+    return both[:ORDER, :width] + both[:ORDER, width:] + both[ORDER:, :width]
 
 
 def edge_kernel(blocks, parts, w2_ref, count_ref, *refs):
@@ -287,10 +315,19 @@
             total += dot(high[at[0]], w2_ref[0, width:, :width], NN)
             return total + dot(low[at[0]], near, NN)
 
+        rh, rl = rh_ref[...], rl_ref[...]
+        mixer = jnp.concatenate(
+            [
+                jnp.concatenate([rh, rh], axis=1),
+                jnp.concatenate([rl, jnp.zeros_like(rl)], axis=1),
+            ],
+            axis=0,
+        )
+
         def mix(parts_of):
             zh, zl = halves(jnp.concatenate(parts_of, axis=1))
-            lhs = jnp.concatenate([rh_ref[...], rh_ref[...], rl_ref[...]], axis=1)
-            return dot(lhs, jnp.concatenate([zh, zl, zh], axis=0), NN)
+            both = dot(mixer, jnp.concatenate([zh, zl], axis=0), NN)
+            return both[:ORDER] + both[ORDER:]
 
         def hand_out(n, value):
             pick[n] = value
@@ -298,7 +335,7 @@
             theirs[n] = pick[n, pl.ds(starts[1], seasons), :]
 
         total_1, total_2, total_3 = sums_in[1], sums_in[2], sums_in[3]
-        for group in runs(ones, 4):
+        for group in runs(ones, GROUP):
             mixed = mix([space(i, xh, xl, x_at) for i in group])
             for n, i in enumerate(group):
                 one = masked(i, mixed[:, n * width : (n + 1) * width])
@@ -310,7 +347,7 @@
                     hand_out(inner_ones.index(i), one)
         sums_out[1] = total_1
         sums_out[2] = total_2
-        for group in runs(twos, 4):
+        for group in runs(twos, GROUP):
             mixed = mix([space(i, oh, ol, one_at) for i in group])
             for n, i in enumerate(group):
                 two = masked(i, mixed[:, n * width : (n + 1) * width])

time: 35.7 us -> 32.5 us (0.910)
  waiting for transfers between devices: 9.08 us -> 5.02 us
  starting transfers between devices: 12.5 us -> 15.4 us
  local copies, waits for them, and re-layouts: 4.81 us -> 2.03 us
  Pallas kernels: 8.3 us -> 9.02 us
    ppermute x8 -> x10, waiting for transfers between devices: 5.43 us -> 0.99 us  [from_group(): return lax.ppermute(value, ('season', 'var'), pairs)]
    ppermute x8 -> x10, starting transfers between devices: 7.17 us -> 10.5 us  [from_group(): return lax.ppermute(value, ('season', 'var'), pairs)]
    unnamed x8 -> x6, local copies, waits for them, and re-layouts: 4.73 us -> 1.95 us
    pallas_call x1, Pallas kernels: 0.71 us -> 2.9 us  [prepare(): pl.pallas_call(functools.partial(prepare_kernel, blocks), in_specs=[pl.Bl...]
    pallas_call x2, Pallas kernels: 5.34 us -> 3.87 us  [run_stage(): pl.pallas_call(kernel, in_specs=[pl.BlockSpec(memory_space=VMEM)] * len(o...]
    ppermute x2, starting transfers between devices: 4.66 us -> 4.26 us  [gather_tiles(): lax.ppermute(have, 'space', [(i, i ^ hop) for i in range(size)])]
    ppermute x2, waiting for transfers between devices: 3.64 us -> 4.03 us  [gather_tiles(): lax.ppermute(have, 'space', [(i, i ^ hop) for i in range(size)])]
  transfers between devices with their start and end apart: 11 -> 13, of which waited for: 5 -> 4; matrix products, arithmetic and copies ran while one was open for 0% -> 0% of each run, Pallas kernels for 7% -> 22%
where the time goes in v4:
time: 32.5 us; the launch traced here: 32.3 us
  starting transfers between devices  15.4 us (47%)
  Pallas kernels  9.02 us (28%)
  waiting for transfers between devices  5.02 us (15%)
  local copies, waits for them, and re-layouts  2.03 us (6%)
  between operations  0.75 us (2%)
    ppermute x10, starting transfers between devices, from_group(): return lax.ppermute(value, ('season', 'var'), pairs)  10.5 us
    ppermute x2, starting transfers between devices, gather_tiles(): lax.ppermute(have, 'space', [(i, i ^ hop) for i in range(size)])  4.26 us
    ppermute x2, waiting for transfers between devices, gather_tiles(): lax.ppermute(have, 'space', [(i, i ^ hop) for i in range(size)])  4.03 us
    pallas_call x2, Pallas kernels, run_stage(): pl.pallas_call(kernel, in_specs=[pl.BlockSpec(memory_space=VMEM)] * len(o...  3.87 us
    pallas_call x1, Pallas kernels, prepare(): pl.pallas_call(functools.partial(prepare_kernel, blocks), in_specs=[pl.Bl...  2.9 us
    unnamed x6, local copies, waits for them, and re-layouts  1.95 us
    pallas_call x1, Pallas kernels, finish(): pl.pallas_call(functools.partial(finish_kernel, plan, blocks, len(gathere...  1.69 us
    ppermute x10, waiting for transfers between devices, from_group(): return lax.ppermute(value, ('season', 'var'), pairs)  0.99 us
  transfers between devices with their start and end apart: 13, of which 4 were waited for; matrix products, arithmetic and copies ran while one was open for 0% of the time, Pallas kernels for 22%

profile of v4, /device:TPU:0, one launch (start us, length us, event | category | flops | bytes accessed | tf_op | source)
XLA Modules:
  0.0 32.3 jit_solution(3824092083650580021)
XLA Ops:
  0.6 1.0 %copy-done = f32[32,1,4096]{2,1,0:T(1,128)S(1)} copy-done((f32[32,1,4096]{2,1,0:T(1,128)S(1)}, f32[32,1,4096]{2,1,0:T(1,128)}, u32[]{:S(2)}) %copy-start) | copy-done | bytes 524312
  1.7 0.3 %pack.1 = (f32[18,32,128]{2,1,0:T(8,128)S(1)}, f32[18,32,128]{2,1,0:T(8,128)S(1)}, f32[3,32,128]{2,1,0:T(8,128)S(1)}, f32[3,32,128]{2,1,0:T(8,128)S(1)}, f32[11,...) custom-call(f32[1024,128]{1,0:T(8,128)S(1)} %bitcast.8), custom_call_target="tpu_custom_call" | custom-call | flops 1 | bytes 1 | tf_op jit(solution)/shard_map/pack/pallas_call | solution.py:61
  2.0 0.5 %collective-permute-start = (f32[18,32,128]{2,1,0:T(8,128)S(1)}, f32[18,32,128]{2,1,0:T(8,128)S(1)}, u32[]{:S(2)}, u32[]{:S(2)}) collective-permute-start(f32[18,32,128]{2,1,0:T(8,128)S(1)} %get-tuple-element.27.refs_5_), channel_id=1, source_target_pairs={{1,0},{0,1},{3,2},{2,3},{5,4},{4,5},{7,6},{6,7},{9,8},{8,9},{11,10... | collective-permute-start | bytes 884744 | tf_op jit(solution)/shard_map/ppermute | solution.py:483
  2.6 2.6 %collective-permute-start.3 = (f32[3,32,128]{2,1,0:T(8,128)S(1)}, f32[3,32,128]{2,1,0:T(8,128)S(1)}, u32[]{:S(2)}, u32[]{:S(2)}) collective-permute-start(f32[3,32,128]{2,1,0:T(8,128)S(1)} %get-tuple-element.33), channel_id=1, source_target_pairs={{2,0},{3,1},{0,2},{1,3},{6,4},{7,5},{4,6},{5,7},{10,8},{11,9},{8,1... | collective-permute-start | bytes 147464 | tf_op jit(solution)/shard_map/ppermute | solution.py:483
  5.1 0.1 collective-permute-start.4
  5.2 1.7 %collective-permute-start.5 = (f32[11,32,128]{2,1,0:T(8,128)S(1)}, f32[11,32,128]{2,1,0:T(8,128)S(1)}, u32[]{:S(2)}, u32[]{:S(2)}) collective-permute-start(f32[11,32,128]{2,1,0:T(8,128)S(1)} %get-tuple-element.35), channel_id=1, source_target_pairs={{2,0},{3,1},{0,2},{1,3},{6,4},{7,5},{4,6},{5,7},{10,8},{11,9},{8,1... | collective-permute-start | bytes 540680 | tf_op jit(solution)/shard_map/ppermute | solution.py:483
  6.9 0.0 collective-permute-start.6
  6.9 0.9 %copy-done.1 = f32[64,2,64,2]{2,3,1,0:T(2,128)S(1)} copy-done((f32[64,2,64,2]{2,3,1,0:T(2,128)S(1)}, f32[64,2,64,2]{2,3,1,0:T(2,128)}, u32[]{:S(2)}) %copy-start.1) | copy-done | bytes 65560
  7.8 2.9 %prepare.1 = (bf16[17,256,384]{2,1,0:T(8,128)(2,1)S(1)}, bf16[128,128]{1,0:T(8,128)(2,1)S(1)}, bf16[128,128]{1,0:T(8,128)(2,1)S(1)}, f32[8,128]{1,0:T(8,128)S(1)}) custom-call(f32[32,3,128,128]{3,2,1,0:T(8,128)} %w_ref.1, f32[256,64]{1,0:T(8,128)S(1)} %bitcast.9), custom_call_target="tpu_custom_call" | custom-call | flops 1 | bytes 1 | tf_op jit(solution)/shard_map/prepare/pallas_call | solution.py:129
  10.8 0.0 collective-permute-done.3.refs_2_
  10.8 0.0 collective-permute-done.4.refs_3_
  10.8 0.0 collective-permute-done.refs_1_
  10.8 0.1 broadcast_in_dim.12.refs_9_.count_ref.refs_7_
  10.9 0.2 edge.1
  11.1 0.7 %collective-permute-start.7 = (f32[264,128]{1,0:T(8,128)S(1)}, f32[264,128]{1,0:T(8,128)S(1)}, u32[]{:S(2)}, u32[]{:S(2)}) collective-permute-start(f32[264,128]{1,0:T(8,128)S(1)} %edge.1), channel_id=1, source_target_pairs={{1,4},{4,1},{5,8},{8,5},{9,12},{12,9},{3,6},{6,3},{7,10},{10,7},{1... | collective-permute-start | bytes 405512 | tf_op jit(solution)/shard_map/ppermute | solution.py:491
  11.8 1.7 %collective-permute-start.1 = (f32[4,32,128]{2,1,0:T(8,128)S(1)}, f32[4,32,128]{2,1,0:T(8,128)S(1)}, u32[]{:S(2)}, u32[]{:S(2)}) collective-permute-start(f32[4,32,128]{2,1,0:T(8,128)S(1)} %get-tuple-element.28), channel_id=1, source_target_pairs={{2,0},{3,1},{0,2},{1,3},{6,4},{7,5},{4,6},{5,7},{10,8},{11,9},{8,1... | collective-permute-start | bytes 196616 | tf_op jit(solution)/shard_map/ppermute | solution.py:483
  13.5 2.8 %collective-permute-start.2 = (f32[4,32,128]{2,1,0:T(8,128)S(1)}, f32[4,32,128]{2,1,0:T(8,128)S(1)}, u32[]{:S(2)}, u32[]{:S(2)}) collective-permute-start(f32[4,32,128]{2,1,0:T(8,128)S(1)} %get-tuple-element.29), channel_id=1, source_target_pairs={{3,0},{2,1},{1,2},{0,3},{7,4},{6,5},{5,6},{4,7},{11,8},{10,9},{9,1... | collective-permute-start | bytes 196616 | tf_op jit(solution)/shard_map/ppermute | solution.py:483
  16.3 0.2 collective-permute-done.6.refs_5_
  16.5 2.4 %stage.2 = (f32[4,8,128]{2,1,0:T(8,128)S(1)}, f32[22,32,128]{2,1,0:T(8,128)S(1)}, f32[22,32,128]{2,1,0:T(8,128)S(1)}, bf16[4,128,128]{2,1,0:T(8,128)(2,1)S(1)}, ...) custom-call(f32[18,32,128]{2,1,0:T(8,128)S(1)} %get-tuple-element.26.refs_0_.ref, ...), custom_call_target="tpu_custom_call" | custom-call | flops 1 | bytes 1 | tf_op jit(solution)/shard_map/stage/pallas_call | solution.py:380
  18.9 0.2 collective-permute-start.11
  19.2 0.0 collective-permute-done.1.refs_2_
  19.2 1.5 %stage.3 = (f32[4,8,128]{2,1,0:T(8,128)S(1)}, f32[10,32,128]{2,1,0:T(8,128)S(1)}, f32[10,32,128]{2,1,0:T(8,128)S(1)}) custom-call(f32[18,32,128]{2,1,0:T(8,128)S(1)} %get-tuple-element.26.refs_0_.refs_4_, f32[18,32,128]{2,1,0:T(8,128)S(1)} %collective-permute-done.refs_1_, f32[4,32,128]{2,1,0:T(8,128)S(1)} %collective-permute-done.1.refs_2_, ...), custom_call_target="tpu_custom_call" | custom-call | flops 1 | bytes 1 | tf_op jit(solution)/shard_map/stage/pallas_call | solution.py:380
  20.7 0.7 %collective-permute-start.8 = (f32[1,8,128]{2,1,0:T(8,128)S(1)}, f32[1,8,128]{2,1,0:T(8,128)S(1)}, u32[]{:S(2)}, u32[]{:S(2)}) collective-permute-start(f32[1,8,128]{2,1,0:T(8,128)S(1)} %maximum_bitcast_fusion.refs_0_), channel_id=1, source_target_pairs={{1,0},{0,1},{3,2},{2,3},{5,4},{4,5},{7,6},{6,7},{9,8},{8,9},{11,10... | collective-permute-start | bytes 12296 | tf_op jit(solution)/shard_map/ppermute | solution.py:483
  21.4 0.1 collective-permute-start.12
  21.5 0.7 %collective-permute-done.8.refs_1_ = f32[1,8,128]{2,1,0:T(8,128)S(1)} collective-permute-done((f32[1,8,128]{2,1,0:T(8,128)S(1)}, f32[1,8,128]{2,1,0:T(8,128)S(1)}, u32[]{:S(2)}, u32[]{:S(2)}) %collective-permute-start.8) | collective-permute-done | bytes 4128 | tf_op jit(solution)/shard_map/ppermute | solution.py:483
  22.3 1.6 %collective-permute-start.9 = (f32[2,8,128]{2,1,0:T(8,128)S(1)}, f32[2,8,128]{2,1,0:T(8,128)S(1)}, u32[]{:S(2)}, u32[]{:S(2)}) collective-permute-start(f32[2,8,128]{2,1,0:T(8,128)S(1)} %pad_maximum_fusion.1), channel_id=1, source_target_pairs={{0,4},{4,0},{8,12},{12,8},{1,5},{5,1},{9,13},{13,9},{2,6},{6,2},{1... | collective-permute-start | bytes 24584 | tf_op jit(solution)/shard_map/ppermute | solution.py:504
  23.8 2.1 %collective-permute-done.9.refs_2_ = f32[2,8,128]{2,1,0:T(8,128)S(1)} collective-permute-done((f32[2,8,128]{2,1,0:T(8,128)S(1)}, f32[2,8,128]{2,1,0:T(8,128)S(1)}, u32[]{:S(2)}, u32[]{:S(2)}) %collective-permute-start.9) | collective-permute-done | bytes 8224 | tf_op jit(solution)/shard_map/ppermute | solution.py:504
  25.9 2.7 %collective-permute-start.10 = (f32[4,8,128]{2,1,0:T(8,128)S(1)}, f32[4,8,128]{2,1,0:T(8,128)S(1)}, u32[]{:S(2)}, u32[]{:S(2)}) collective-permute-start(f32[4,8,128]{2,1,0:T(8,128)S(1)} %pad_maximum_fusion), channel_id=1, source_target_pairs={{0,8},{4,12},{8,0},{12,4},{1,9},{5,13},{9,1},{13,5},{2,10},{6,14},... | collective-permute-start | bytes 49160 | tf_op jit(solution)/shard_map/ppermute | solution.py:504
  28.6 2.0 %collective-permute-done.10.refs_3_ = f32[4,8,128]{2,1,0:T(8,128)S(1)} collective-permute-done((f32[4,8,128]{2,1,0:T(8,128)S(1)}, f32[4,8,128]{2,1,0:T(8,128)S(1)}, u32[]{:S(2)}, u32[]{:S(2)}) %collective-permute-start.10) | collective-permute-done | bytes 16416 | tf_op jit(solution)/shard_map/ppermute | solution.py:504
  30.6 0.0 collective-permute-done.12.refs_9_
  30.6 0.0 collective-permute-done.11.refs_8_
  30.6 1.7 %finish.1 = (f32[32,32,1,128]{3,2,1,0:T(1,128)}, f32[32,32,1,128]{3,2,1,0:T(1,128)}) custom-call(f32[1,8,128]{2,1,0:T(8,128)S(1)} %maximum_bitcast_fusion.refs_0_, f32[1,8,128]{2,1,0:T(8,128)S(1)} %collective-permute-done.8.refs_1_, f32[2,8,128]{2,1,0:T(8,128)S(1)} %collective-permute-done.9.refs_2_, f32[4,8,128]{2,1,0:T(8,128)S(1)} %collective-permute-done.10.refs_3_, ...), custom_call_target="tpu_custom_call" | custom-call | flops 1 | bytes 1 | tf_op jit(solution)/shard_map/finish/pallas_call | solution.py:463
  (14 shorter events, 0.1 us)
Async XLA Ops:
  0.6 10.1 %copy-start.2 = (s32[32]{0:T(128)S(1)}, s32[32]{0:T(128)}, u32[]{:S(2)}) copy-start(s32[32]{0:T(128)} %param.7) | copy-start | bytes 388
  0.6 1.0 %copy-start = (f32[32,1,4096]{2,1,0:T(1,128)S(1)}, f32[32,1,4096]{2,1,0:T(1,128)}, u32[]{:S(2)}) copy-start(f32[32,1,4096]{2,1,0:T(1,128)} %param.5) | copy-start | bytes 1572868
  2.0 8.8 %collective-permute-start = (f32[18,32,128]{2,1,0:T(8,128)S(1)}, f32[18,32,128]{2,1,0:T(8,128)S(1)}, u32[]{:S(2)}, u32[]{:S(2)}) collective-permute-start(f32[18,32,128]{2,1,0:T(8,128)S(1)} %get-tuple-element.27.refs_5_), channel_id=1, source_target_pairs={{1,0},{0,1},{3,2},{2,3},{5,4},{4,5},{7,6},{6,7},{9,8},{8,9},{11,10... | collective-permute-start | bytes 884744 | tf_op jit(solution)/shard_map/ppermute | solution.py:483
  2.6 8.2 %collective-permute-start.3 = (f32[3,32,128]{2,1,0:T(8,128)S(1)}, f32[3,32,128]{2,1,0:T(8,128)S(1)}, u32[]{:S(2)}, u32[]{:S(2)}) collective-permute-start(f32[3,32,128]{2,1,0:T(8,128)S(1)} %get-tuple-element.33), channel_id=1, source_target_pairs={{2,0},{3,1},{0,2},{1,3},{6,4},{7,5},{4,6},{5,7},{10,8},{11,9},{8,1... | collective-permute-start | bytes 147464 | tf_op jit(solution)/shard_map/ppermute | solution.py:483
  5.1 5.7 %collective-permute-start.4 = (f32[3,32,128]{2,1,0:T(8,128)S(1)}, f32[3,32,128]{2,1,0:T(8,128)S(1)}, u32[]{:S(2)}, u32[]{:S(2)}) collective-permute-start(f32[3,32,128]{2,1,0:T(8,128)S(1)} %get-tuple-element.34), channel_id=1, source_target_pairs={{3,0},{2,1},{1,2},{0,3},{7,4},{6,5},{5,6},{4,7},{11,8},{10,9},{9,1... | collective-permute-start | bytes 147464 | tf_op jit(solution)/shard_map/ppermute | solution.py:483
  5.2 11.1 %collective-permute-start.5 = (f32[11,32,128]{2,1,0:T(8,128)S(1)}, f32[11,32,128]{2,1,0:T(8,128)S(1)}, u32[]{:S(2)}, u32[]{:S(2)}) collective-permute-start(f32[11,32,128]{2,1,0:T(8,128)S(1)} %get-tuple-element.35), channel_id=1, source_target_pairs={{2,0},{3,1},{0,2},{1,3},{6,4},{7,5},{4,6},{5,7},{10,8},{11,9},{8,1... | collective-permute-start | bytes 540680 | tf_op jit(solution)/shard_map/ppermute | solution.py:483
  6.9 9.6 %collective-permute-start.6 = (f32[11,32,128]{2,1,0:T(8,128)S(1)}, f32[11,32,128]{2,1,0:T(8,128)S(1)}, u32[]{:S(2)}, u32[]{:S(2)}) collective-permute-start(f32[11,32,128]{2,1,0:T(8,128)S(1)} %get-tuple-element.36), channel_id=1, source_target_pairs={{3,0},{2,1},{1,2},{0,3},{7,4},{6,5},{5,6},{4,7},{11,8},{10,9},{9,1... | collective-permute-start | bytes 540680 | tf_op jit(solution)/shard_map/ppermute | solution.py:483
  6.9 0.9 %copy-start.1 = (f32[64,2,64,2]{2,3,1,0:T(2,128)S(1)}, f32[64,2,64,2]{2,3,1,0:T(2,128)}, u32[]{:S(2)}) copy-start(f32[64,2,64,2]{2,3,1,0:T(2,128)} %param.8) | copy-start | bytes 196612
  11.1 8.1 %collective-permute-start.7 = (f32[264,128]{1,0:T(8,128)S(1)}, f32[264,128]{1,0:T(8,128)S(1)}, u32[]{:S(2)}, u32[]{:S(2)}) collective-permute-start(f32[264,128]{1,0:T(8,128)S(1)} %edge.1), channel_id=1, source_target_pairs={{1,4},{4,1},{5,8},{8,5},{9,12},{12,9},{3,6},{6,3},{7,10},{10,7},{1... | collective-permute-start | bytes 405512 | tf_op jit(solution)/shard_map/ppermute | solution.py:491
  11.8 7.4 %collective-permute-start.1 = (f32[4,32,128]{2,1,0:T(8,128)S(1)}, f32[4,32,128]{2,1,0:T(8,128)S(1)}, u32[]{:S(2)}, u32[]{:S(2)}) collective-permute-start(f32[4,32,128]{2,1,0:T(8,128)S(1)} %get-tuple-element.28), channel_id=1, source_target_pairs={{2,0},{3,1},{0,2},{1,3},{6,4},{7,5},{4,6},{5,7},{10,8},{11,9},{8,1... | collective-permute-start | bytes 196616 | tf_op jit(solution)/shard_map/ppermute | solution.py:483
  13.5 5.7 %collective-permute-start.2 = (f32[4,32,128]{2,1,0:T(8,128)S(1)}, f32[4,32,128]{2,1,0:T(8,128)S(1)}, u32[]{:S(2)}, u32[]{:S(2)}) collective-permute-start(f32[4,32,128]{2,1,0:T(8,128)S(1)} %get-tuple-element.29), channel_id=1, source_target_pairs={{3,0},{2,1},{1,2},{0,3},{7,4},{6,5},{5,6},{4,7},{11,8},{10,9},{9,1... | collective-permute-start | bytes 196616 | tf_op jit(solution)/shard_map/ppermute | solution.py:483
  18.9 11.6 %collective-permute-start.11 = (f32[22,32,128]{2,1,0:T(8,128)S(1)}, f32[22,32,128]{2,1,0:T(8,128)S(1)}, u32[]{:S(2)}, u32[]{:S(2)}) collective-permute-start(f32[22,32,128]{2,1,0:T(8,128)S(1)} %get-tuple-element.46), channel_id=1, source_target_pairs={{1,0},{0,1},{3,2},{2,3},{5,4},{4,5},{7,6},{6,7},{9,8},{8,9},{11,10... | collective-permute-start | bytes 1081352 | tf_op jit(solution)/shard_map/ppermute | solution.py:483
  20.7 1.6 %collective-permute-start.8 = (f32[1,8,128]{2,1,0:T(8,128)S(1)}, f32[1,8,128]{2,1,0:T(8,128)S(1)}, u32[]{:S(2)}, u32[]{:S(2)}) collective-permute-start(f32[1,8,128]{2,1,0:T(8,128)S(1)} %maximum_bitcast_fusion.refs_0_), channel_id=1, source_target_pairs={{1,0},{0,1},{3,2},{2,3},{5,4},{4,5},{7,6},{6,7},{9,8},{8,9},{11,10... | collective-permute-start | bytes 12296 | tf_op jit(solution)/shard_map/ppermute | solution.py:483
  21.4 9.1 %collective-permute-start.12 = (f32[10,32,128]{2,1,0:T(8,128)S(1)}, f32[10,32,128]{2,1,0:T(8,128)S(1)}, u32[]{:S(2)}, u32[]{:S(2)}) collective-permute-start(f32[10,32,128]{2,1,0:T(8,128)S(1)} %get-tuple-element.47), channel_id=1, source_target_pairs={{1,0},{0,1},{3,2},{2,3},{5,4},{4,5},{7,6},{6,7},{9,8},{8,9},{11,10... | collective-permute-start | bytes 491528 | tf_op jit(solution)/shard_map/ppermute | solution.py:483
  22.3 3.7 %collective-permute-start.9 = (f32[2,8,128]{2,1,0:T(8,128)S(1)}, f32[2,8,128]{2,1,0:T(8,128)S(1)}, u32[]{:S(2)}, u32[]{:S(2)}) collective-permute-start(f32[2,8,128]{2,1,0:T(8,128)S(1)} %pad_maximum_fusion.1), channel_id=1, source_target_pairs={{0,4},{4,0},{8,12},{12,8},{1,5},{5,1},{9,13},{13,9},{2,6},{6,2},{1... | collective-permute-start | bytes 24584 | tf_op jit(solution)/shard_map/ppermute | solution.py:504
  25.9 4.6 %collective-permute-start.10 = (f32[4,8,128]{2,1,0:T(8,128)S(1)}, f32[4,8,128]{2,1,0:T(8,128)S(1)}, u32[]{:S(2)}, u32[]{:S(2)}) collective-permute-start(f32[4,8,128]{2,1,0:T(8,128)S(1)} %pad_maximum_fusion), channel_id=1, source_target_pairs={{0,8},{4,12},{8,0},{12,4},{1,9},{5,13},{9,1},{13,5},{2,10},{6,14},... | collective-permute-start | bytes 49160 | tf_op jit(solution)/shard_map/ppermute | solution.py:504

commit v5 on v4

--- a/solution.py
+++ b/solution.py
@@ -501,7 +501,10 @@
     hop = 1
     while hop < size:
         have = jnp.concatenate(found, axis=0)
-        found.append(lax.ppermute(have, "space", [(i, i ^ hop) for i in range(size)]))
+        pairs = [
+            (i * VARS + v, (i ^ hop) * VARS + 1 - v) for i in range(size) for v in range(VARS)
+        ]
+        found.append(lax.ppermute(have, ("space", "var"), pairs))
         hop *= 2
     return found
 

time: 32.5 us -> 31.3 us (0.963)
  waiting for transfers between devices: 5.02 us -> 3.99 us
    ppermute x2, waiting for transfers between devices: 4.03 us -> 3 us  [gather_tiles(): found.append(lax.ppermute(have, ('space', 'var'), pairs))]
where the time goes in v5:
time: 31.3 us; the launch traced here: 31.1 us
  starting transfers between devices  15.3 us (49%)
  Pallas kernels  9.02 us (29%)
  waiting for transfers between devices  3.99 us (13%)
  local copies, waits for them, and re-layouts  2.03 us (6%)
  between operations  0.75 us (2%)
    ppermute x10, starting transfers between devices, from_group(): return lax.ppermute(value, ('season', 'var'), pairs)  10.5 us
    ppermute x2, starting transfers between devices, gather_tiles(): found.append(lax.ppermute(have, ('space', 'var'), pairs))  4.15 us
    pallas_call x2, Pallas kernels, run_stage(): pl.pallas_call(kernel, in_specs=[pl.BlockSpec(memory_space=VMEM)] * len(o...  3.87 us
    ppermute x2, waiting for transfers between devices, gather_tiles(): found.append(lax.ppermute(have, ('space', 'var'), pairs))  3 us
    pallas_call x1, Pallas kernels, prepare(): pl.pallas_call(functools.partial(prepare_kernel, blocks), in_specs=[pl.Bl...  2.9 us
    unnamed x6, local copies, waits for them, and re-layouts  1.95 us
    pallas_call x1, Pallas kernels, finish(): pl.pallas_call(functools.partial(finish_kernel, plan, blocks, len(gathere...  1.68 us
    ppermute x10, waiting for transfers between devices, from_group(): return lax.ppermute(value, ('season', 'var'), pairs)  0.99 us
  transfers between devices with their start and end apart: 13, of which 4 were waited for; matrix products, arithmetic and copies ran while one was open for 0% of the time, Pallas kernels for 22%

profile of v5, /device:TPU:0, one launch (start us, length us, event | category | flops | bytes accessed | tf_op | source)
XLA Modules:
  0.0 31.1 jit_solution(1465647761391136349)
XLA Ops:
  0.6 1.0 %copy-done = f32[32,1,4096]{2,1,0:T(1,128)S(1)} copy-done((f32[32,1,4096]{2,1,0:T(1,128)S(1)}, f32[32,1,4096]{2,1,0:T(1,128)}, u32[]{:S(2)}) %copy-start) | copy-done | bytes 524312
  1.7 0.3 %pack.1 = (f32[18,32,128]{2,1,0:T(8,128)S(1)}, f32[18,32,128]{2,1,0:T(8,128)S(1)}, f32[3,32,128]{2,1,0:T(8,128)S(1)}, f32[3,32,128]{2,1,0:T(8,128)S(1)}, f32[11,...) custom-call(f32[1024,128]{1,0:T(8,128)S(1)} %bitcast.8), custom_call_target="tpu_custom_call" | custom-call | flops 1 | bytes 1 | tf_op jit(solution)/shard_map/pack/pallas_call | solution.py:61
  2.0 0.5 %collective-permute-start = (f32[18,32,128]{2,1,0:T(8,128)S(1)}, f32[18,32,128]{2,1,0:T(8,128)S(1)}, u32[]{:S(2)}, u32[]{:S(2)}) collective-permute-start(f32[18,32,128]{2,1,0:T(8,128)S(1)} %get-tuple-element.27.refs_5_), channel_id=1, source_target_pairs={{1,0},{0,1},{3,2},{2,3},{5,4},{4,5},{7,6},{6,7},{9,8},{8,9},{11,10... | collective-permute-start | bytes 884744 | tf_op jit(solution)/shard_map/ppermute | solution.py:483
  2.6 2.6 %collective-permute-start.3 = (f32[3,32,128]{2,1,0:T(8,128)S(1)}, f32[3,32,128]{2,1,0:T(8,128)S(1)}, u32[]{:S(2)}, u32[]{:S(2)}) collective-permute-start(f32[3,32,128]{2,1,0:T(8,128)S(1)} %get-tuple-element.33), channel_id=1, source_target_pairs={{2,0},{3,1},{0,2},{1,3},{6,4},{7,5},{4,6},{5,7},{10,8},{11,9},{8,1... | collective-permute-start | bytes 147464 | tf_op jit(solution)/shard_map/ppermute | solution.py:483
  5.1 0.1 collective-permute-start.4
  5.2 1.7 %collective-permute-start.5 = (f32[11,32,128]{2,1,0:T(8,128)S(1)}, f32[11,32,128]{2,1,0:T(8,128)S(1)}, u32[]{:S(2)}, u32[]{:S(2)}) collective-permute-start(f32[11,32,128]{2,1,0:T(8,128)S(1)} %get-tuple-element.35), channel_id=1, source_target_pairs={{2,0},{3,1},{0,2},{1,3},{6,4},{7,5},{4,6},{5,7},{10,8},{11,9},{8,1... | collective-permute-start | bytes 540680 | tf_op jit(solution)/shard_map/ppermute | solution.py:483
  6.9 0.0 collective-permute-start.6
  6.9 0.9 %copy-done.1 = f32[64,2,64,2]{2,3,1,0:T(2,128)S(1)} copy-done((f32[64,2,64,2]{2,3,1,0:T(2,128)S(1)}, f32[64,2,64,2]{2,3,1,0:T(2,128)}, u32[]{:S(2)}) %copy-start.1) | copy-done | bytes 65560
  7.8 2.9 %prepare.1 = (bf16[17,256,384]{2,1,0:T(8,128)(2,1)S(1)}, bf16[128,128]{1,0:T(8,128)(2,1)S(1)}, bf16[128,128]{1,0:T(8,128)(2,1)S(1)}, f32[8,128]{1,0:T(8,128)S(1)}) custom-call(f32[32,3,128,128]{3,2,1,0:T(8,128)} %w_ref.1, f32[256,64]{1,0:T(8,128)S(1)} %bitcast.9), custom_call_target="tpu_custom_call" | custom-call | flops 1 | bytes 1 | tf_op jit(solution)/shard_map/prepare/pallas_call | solution.py:129
  10.8 0.0 collective-permute-done.3.refs_2_
  10.8 0.0 collective-permute-done.4.refs_3_
  10.8 0.0 collective-permute-done.refs_1_
  10.8 0.1 broadcast_in_dim.12.refs_9_.count_ref.refs_7_
  10.9 0.2 edge.1
  11.1 0.7 %collective-permute-start.7 = (f32[264,128]{1,0:T(8,128)S(1)}, f32[264,128]{1,0:T(8,128)S(1)}, u32[]{:S(2)}, u32[]{:S(2)}) collective-permute-start(f32[264,128]{1,0:T(8,128)S(1)} %edge.1), channel_id=1, source_target_pairs={{1,4},{4,1},{5,8},{8,5},{9,12},{12,9},{3,6},{6,3},{7,10},{10,7},{1... | collective-permute-start | bytes 405512 | tf_op jit(solution)/shard_map/ppermute | solution.py:491
  11.8 1.7 %collective-permute-start.1 = (f32[4,32,128]{2,1,0:T(8,128)S(1)}, f32[4,32,128]{2,1,0:T(8,128)S(1)}, u32[]{:S(2)}, u32[]{:S(2)}) collective-permute-start(f32[4,32,128]{2,1,0:T(8,128)S(1)} %get-tuple-element.28), channel_id=1, source_target_pairs={{2,0},{3,1},{0,2},{1,3},{6,4},{7,5},{4,6},{5,7},{10,8},{11,9},{8,1... | collective-permute-start | bytes 196616 | tf_op jit(solution)/shard_map/ppermute | solution.py:483
  13.5 2.8 %collective-permute-start.2 = (f32[4,32,128]{2,1,0:T(8,128)S(1)}, f32[4,32,128]{2,1,0:T(8,128)S(1)}, u32[]{:S(2)}, u32[]{:S(2)}) collective-permute-start(f32[4,32,128]{2,1,0:T(8,128)S(1)} %get-tuple-element.29), channel_id=1, source_target_pairs={{3,0},{2,1},{1,2},{0,3},{7,4},{6,5},{5,6},{4,7},{11,8},{10,9},{9,1... | collective-permute-start | bytes 196616 | tf_op jit(solution)/shard_map/ppermute | solution.py:483
  16.3 0.2 collective-permute-done.6.refs_5_
  16.5 2.4 %stage.2 = (f32[4,8,128]{2,1,0:T(8,128)S(1)}, f32[22,32,128]{2,1,0:T(8,128)S(1)}, f32[22,32,128]{2,1,0:T(8,128)S(1)}, bf16[4,128,128]{2,1,0:T(8,128)(2,1)S(1)}, ...) custom-call(f32[18,32,128]{2,1,0:T(8,128)S(1)} %get-tuple-element.26.refs_0_.ref, ...), custom_call_target="tpu_custom_call" | custom-call | flops 1 | bytes 1 | tf_op jit(solution)/shard_map/stage/pallas_call | solution.py:380
  18.9 0.2 collective-permute-start.11
  19.2 0.0 collective-permute-done.1.refs_2_
  19.2 1.5 %stage.3 = (f32[4,8,128]{2,1,0:T(8,128)S(1)}, f32[10,32,128]{2,1,0:T(8,128)S(1)}, f32[10,32,128]{2,1,0:T(8,128)S(1)}) custom-call(f32[18,32,128]{2,1,0:T(8,128)S(1)} %get-tuple-element.26.refs_0_.refs_4_, f32[18,32,128]{2,1,0:T(8,128)S(1)} %collective-permute-done.refs_1_, f32[4,32,128]{2,1,0:T(8,128)S(1)} %collective-permute-done.1.refs_2_, ...), custom_call_target="tpu_custom_call" | custom-call | flops 1 | bytes 1 | tf_op jit(solution)/shard_map/stage/pallas_call | solution.py:380
  20.7 0.7 %collective-permute-start.8 = (f32[1,8,128]{2,1,0:T(8,128)S(1)}, f32[1,8,128]{2,1,0:T(8,128)S(1)}, u32[]{:S(2)}, u32[]{:S(2)}) collective-permute-start(f32[1,8,128]{2,1,0:T(8,128)S(1)} %maximum_bitcast_fusion.refs_0_), channel_id=1, source_target_pairs={{1,0},{0,1},{3,2},{2,3},{5,4},{4,5},{7,6},{6,7},{9,8},{8,9},{11,10... | collective-permute-start | bytes 12296 | tf_op jit(solution)/shard_map/ppermute | solution.py:483
  21.4 0.1 collective-permute-start.12
  21.5 0.7 %collective-permute-done.8.refs_1_ = f32[1,8,128]{2,1,0:T(8,128)S(1)} collective-permute-done((f32[1,8,128]{2,1,0:T(8,128)S(1)}, f32[1,8,128]{2,1,0:T(8,128)S(1)}, u32[]{:S(2)}, u32[]{:S(2)}) %collective-permute-start.8) | collective-permute-done | bytes 4128 | tf_op jit(solution)/shard_map/ppermute | solution.py:483
  22.3 1.5 %collective-permute-start.9 = (f32[2,8,128]{2,1,0:T(8,128)S(1)}, f32[2,8,128]{2,1,0:T(8,128)S(1)}, u32[]{:S(2)}, u32[]{:S(2)}) collective-permute-start(f32[2,8,128]{2,1,0:T(8,128)S(1)} %pad_maximum_fusion.1), channel_id=1, source_target_pairs={{0,5},{1,4},{4,1},{5,0},{8,13},{9,12},{12,9},{13,8},{2,7},{3,6},{6... | collective-permute-start | bytes 24584 | tf_op jit(solution)/shard_map/ppermute | solution.py:507
  23.8 1.6 %collective-permute-done.9.refs_2_ = f32[2,8,128]{2,1,0:T(8,128)S(1)} collective-permute-done((f32[2,8,128]{2,1,0:T(8,128)S(1)}, f32[2,8,128]{2,1,0:T(8,128)S(1)}, u32[]{:S(2)}, u32[]{:S(2)}) %collective-permute-start.9) | collective-permute-done | bytes 8224 | tf_op jit(solution)/shard_map/ppermute | solution.py:507
  25.4 2.6 %collective-permute-start.10 = (f32[4,8,128]{2,1,0:T(8,128)S(1)}, f32[4,8,128]{2,1,0:T(8,128)S(1)}, u32[]{:S(2)}, u32[]{:S(2)}) collective-permute-start(f32[4,8,128]{2,1,0:T(8,128)S(1)} %pad_maximum_fusion), channel_id=1, source_target_pairs={{0,9},{1,8},{4,13},{5,12},{8,1},{9,0},{12,5},{13,4},{2,11},{3,10},... | collective-permute-start | bytes 49160 | tf_op jit(solution)/shard_map/ppermute | solution.py:507
  28.0 1.4 %collective-permute-done.10.refs_3_ = f32[4,8,128]{2,1,0:T(8,128)S(1)} collective-permute-done((f32[4,8,128]{2,1,0:T(8,128)S(1)}, f32[4,8,128]{2,1,0:T(8,128)S(1)}, u32[]{:S(2)}, u32[]{:S(2)}) %collective-permute-start.10) | collective-permute-done | bytes 16416 | tf_op jit(solution)/shard_map/ppermute | solution.py:507
  29.4 0.0 collective-permute-done.12.refs_9_
  29.4 0.0 collective-permute-done.11.refs_8_
  29.4 1.7 %finish.1 = (f32[32,32,1,128]{3,2,1,0:T(1,128)}, f32[32,32,1,128]{3,2,1,0:T(1,128)}) custom-call(f32[1,8,128]{2,1,0:T(8,128)S(1)} %maximum_bitcast_fusion.refs_0_, f32[1,8,128]{2,1,0:T(8,128)S(1)} %collective-permute-done.8.refs_1_, f32[2,8,128]{2,1,0:T(8,128)S(1)} %collective-permute-done.9.refs_2_, f32[4,8,128]{2,1,0:T(8,128)S(1)} %collective-permute-done.10.refs_3_, ...), custom_call_target="tpu_custom_call" | custom-call | flops 1 | bytes 1 | tf_op jit(solution)/shard_map/finish/pallas_call | solution.py:463
  (14 shorter events, 0.1 us)
Async XLA Ops:
  0.6 10.1 %copy-start.2 = (s32[32]{0:T(128)S(1)}, s32[32]{0:T(128)}, u32[]{:S(2)}) copy-start(s32[32]{0:T(128)} %param.7) | copy-start | bytes 388
  0.6 1.0 %copy-start = (f32[32,1,4096]{2,1,0:T(1,128)S(1)}, f32[32,1,4096]{2,1,0:T(1,128)}, u32[]{:S(2)}) copy-start(f32[32,1,4096]{2,1,0:T(1,128)} %param.5) | copy-start | bytes 1572868
  2.0 8.8 %collective-permute-start = (f32[18,32,128]{2,1,0:T(8,128)S(1)}, f32[18,32,128]{2,1,0:T(8,128)S(1)}, u32[]{:S(2)}, u32[]{:S(2)}) collective-permute-start(f32[18,32,128]{2,1,0:T(8,128)S(1)} %get-tuple-element.27.refs_5_), channel_id=1, source_target_pairs={{1,0},{0,1},{3,2},{2,3},{5,4},{4,5},{7,6},{6,7},{9,8},{8,9},{11,10... | collective-permute-start | bytes 884744 | tf_op jit(solution)/shard_map/ppermute | solution.py:483
  2.6 8.2 %collective-permute-start.3 = (f32[3,32,128]{2,1,0:T(8,128)S(1)}, f32[3,32,128]{2,1,0:T(8,128)S(1)}, u32[]{:S(2)}, u32[]{:S(2)}) collective-permute-start(f32[3,32,128]{2,1,0:T(8,128)S(1)} %get-tuple-element.33), channel_id=1, source_target_pairs={{2,0},{3,1},{0,2},{1,3},{6,4},{7,5},{4,6},{5,7},{10,8},{11,9},{8,1... | collective-permute-start | bytes 147464 | tf_op jit(solution)/shard_map/ppermute | solution.py:483
  5.1 5.7 %collective-permute-start.4 = (f32[3,32,128]{2,1,0:T(8,128)S(1)}, f32[3,32,128]{2,1,0:T(8,128)S(1)}, u32[]{:S(2)}, u32[]{:S(2)}) collective-permute-start(f32[3,32,128]{2,1,0:T(8,128)S(1)} %get-tuple-element.34), channel_id=1, source_target_pairs={{3,0},{2,1},{1,2},{0,3},{7,4},{6,5},{5,6},{4,7},{11,8},{10,9},{9,1... | collective-permute-start | bytes 147464 | tf_op jit(solution)/shard_map/ppermute | solution.py:483
  5.2 11.1 %collective-permute-start.5 = (f32[11,32,128]{2,1,0:T(8,128)S(1)}, f32[11,32,128]{2,1,0:T(8,128)S(1)}, u32[]{:S(2)}, u32[]{:S(2)}) collective-permute-start(f32[11,32,128]{2,1,0:T(8,128)S(1)} %get-tuple-element.35), channel_id=1, source_target_pairs={{2,0},{3,1},{0,2},{1,3},{6,4},{7,5},{4,6},{5,7},{10,8},{11,9},{8,1... | collective-permute-start | bytes 540680 | tf_op jit(solution)/shard_map/ppermute | solution.py:483
  6.9 9.6 %collective-permute-start.6 = (f32[11,32,128]{2,1,0:T(8,128)S(1)}, f32[11,32,128]{2,1,0:T(8,128)S(1)}, u32[]{:S(2)}, u32[]{:S(2)}) collective-permute-start(f32[11,32,128]{2,1,0:T(8,128)S(1)} %get-tuple-element.36), channel_id=1, source_target_pairs={{3,0},{2,1},{1,2},{0,3},{7,4},{6,5},{5,6},{4,7},{11,8},{10,9},{9,1... | collective-permute-start | bytes 540680 | tf_op jit(solution)/shard_map/ppermute | solution.py:483
  6.9 0.9 %copy-start.1 = (f32[64,2,64,2]{2,3,1,0:T(2,128)S(1)}, f32[64,2,64,2]{2,3,1,0:T(2,128)}, u32[]{:S(2)}) copy-start(f32[64,2,64,2]{2,3,1,0:T(2,128)} %param.8) | copy-start | bytes 196612
  11.1 8.1 %collective-permute-start.7 = (f32[264,128]{1,0:T(8,128)S(1)}, f32[264,128]{1,0:T(8,128)S(1)}, u32[]{:S(2)}, u32[]{:S(2)}) collective-permute-start(f32[264,128]{1,0:T(8,128)S(1)} %edge.1), channel_id=1, source_target_pairs={{1,4},{4,1},{5,8},{8,5},{9,12},{12,9},{3,6},{6,3},{7,10},{10,7},{1... | collective-permute-start | bytes 405512 | tf_op jit(solution)/shard_map/ppermute | solution.py:491
  11.8 7.4 %collective-permute-start.1 = (f32[4,32,128]{2,1,0:T(8,128)S(1)}, f32[4,32,128]{2,1,0:T(8,128)S(1)}, u32[]{:S(2)}, u32[]{:S(2)}) collective-permute-start(f32[4,32,128]{2,1,0:T(8,128)S(1)} %get-tuple-element.28), channel_id=1, source_target_pairs={{2,0},{3,1},{0,2},{1,3},{6,4},{7,5},{4,6},{5,7},{10,8},{11,9},{8,1... | collective-permute-start | bytes 196616 | tf_op jit(solution)/shard_map/ppermute | solution.py:483
  13.5 5.7 %collective-permute-start.2 = (f32[4,32,128]{2,1,0:T(8,128)S(1)}, f32[4,32,128]{2,1,0:T(8,128)S(1)}, u32[]{:S(2)}, u32[]{:S(2)}) collective-permute-start(f32[4,32,128]{2,1,0:T(8,128)S(1)} %get-tuple-element.29), channel_id=1, source_target_pairs={{3,0},{2,1},{1,2},{0,3},{7,4},{6,5},{5,6},{4,7},{11,8},{10,9},{9,1... | collective-permute-start | bytes 196616 | tf_op jit(solution)/shard_map/ppermute | solution.py:483
  18.9 10.5 %collective-permute-start.11 = (f32[22,32,128]{2,1,0:T(8,128)S(1)}, f32[22,32,128]{2,1,0:T(8,128)S(1)}, u32[]{:S(2)}, u32[]{:S(2)}) collective-permute-start(f32[22,32,128]{2,1,0:T(8,128)S(1)} %get-tuple-element.46), channel_id=1, source_target_pairs={{1,0},{0,1},{3,2},{2,3},{5,4},{4,5},{7,6},{6,7},{9,8},{8,9},{11,10... | collective-permute-start | bytes 1081352 | tf_op jit(solution)/shard_map/ppermute | solution.py:483
  20.7 1.6 %collective-permute-start.8 = (f32[1,8,128]{2,1,0:T(8,128)S(1)}, f32[1,8,128]{2,1,0:T(8,128)S(1)}, u32[]{:S(2)}, u32[]{:S(2)}) collective-permute-start(f32[1,8,128]{2,1,0:T(8,128)S(1)} %maximum_bitcast_fusion.refs_0_), channel_id=1, source_target_pairs={{1,0},{0,1},{3,2},{2,3},{5,4},{4,5},{7,6},{6,7},{9,8},{8,9},{11,10... | collective-permute-start | bytes 12296 | tf_op jit(solution)/shard_map/ppermute | solution.py:483
  21.4 8.0 %collective-permute-start.12 = (f32[10,32,128]{2,1,0:T(8,128)S(1)}, f32[10,32,128]{2,1,0:T(8,128)S(1)}, u32[]{:S(2)}, u32[]{:S(2)}) collective-permute-start(f32[10,32,128]{2,1,0:T(8,128)S(1)} %get-tuple-element.47), channel_id=1, source_target_pairs={{1,0},{0,1},{3,2},{2,3},{5,4},{4,5},{7,6},{6,7},{9,8},{8,9},{11,10... | collective-permute-start | bytes 491528 | tf_op jit(solution)/shard_map/ppermute | solution.py:483
  22.3 3.1 %collective-permute-start.9 = (f32[2,8,128]{2,1,0:T(8,128)S(1)}, f32[2,8,128]{2,1,0:T(8,128)S(1)}, u32[]{:S(2)}, u32[]{:S(2)}) collective-permute-start(f32[2,8,128]{2,1,0:T(8,128)S(1)} %pad_maximum_fusion.1), channel_id=1, source_target_pairs={{0,5},{1,4},{4,1},{5,0},{8,13},{9,12},{12,9},{13,8},{2,7},{3,6},{6... | collective-permute-start | bytes 24584 | tf_op jit(solution)/shard_map/ppermute | solution.py:507
  25.4 4.1 %collective-permute-start.10 = (f32[4,8,128]{2,1,0:T(8,128)S(1)}, f32[4,8,128]{2,1,0:T(8,128)S(1)}, u32[]{:S(2)}, u32[]{:S(2)}) collective-permute-start(f32[4,8,128]{2,1,0:T(8,128)S(1)} %pad_maximum_fusion), channel_id=1, source_target_pairs={{0,9},{1,8},{4,13},{5,12},{8,1},{9,0},{12,5},{13,4},{2,11},{3,10},... | collective-permute-start | bytes 49160 | tf_op jit(solution)/shard_map/ppermute | solution.py:507

commit v6 on v5

--- a/solution.py
+++ b/solution.py
@@ -16,8 +16,10 @@
 GROUP = 16
 ROOMY = 50 << 20
 COST = pl.CostEstimate(flops=1, bytes_accessed=1, transcendentals=0)
-CUTS = (3, 14)
-STAGES = ((0, 1), (-1, 2))
+ENDS = (2, 2)
+LAST = 3
+OUTER, INNER = -1, -2
+STAGES = ((0, 1, INNER), (OUTER, 2))
 
 F32 = jnp.float32
 BF16 = jnp.bfloat16
@@ -43,23 +45,29 @@
     return m + half_id * (blocks - 1 - 2 * m)
 
 
-def pack_kernel(cuts, blocks, x_ref, same_ref, other_ref, *chunk_refs):
+def make_chunks(half):
+    ends = [i for i in range(half) if i < ENDS[0] or i >= half - ENDS[1]]
+    rest = [i for i in range(half) if i not in ends]
+    return ends, rest[LAST:], rest[:LAST]
+
+
+def pack_kernel(chunks, blocks, x_ref, same_ref, other_ref, *chunk_refs):
     me = lax.axis_index("var")
     seasons = x_ref.shape[0] // blocks
-    for c in range(len(cuts) - 1):
-        for m in range(cuts[c], cuts[c + 1]):
+    for c, places in enumerate(chunks):
+        for at, m in enumerate(places):
             for n, (half_id, ref) in enumerate(((me, same_ref), (1 - me, other_ref))):
                 value = x_ref[pl.ds(block_at(half_id, m, blocks), seasons, stride=blocks), :]
                 ref[m] = value
-                chunk_refs[2 * c + n][m - cuts[c]] = value
-
-
-def pack(x, cuts, blocks):
+                chunk_refs[2 * c + n][at] = value
+
+
+def pack(x, chunks, blocks):
     seasons, width = x.shape[0] // blocks, x.shape[1]
-    counts = [cuts[-1]] + [last - first for first, last in zip(cuts[:-1], cuts[1:])]
+    counts = [blocks // 2] + [len(places) for places in chunks]
     shapes = [(count, seasons, width) for count in counts for _ in range(2)]
     return pl.pallas_call(
-        functools.partial(pack_kernel, cuts, blocks),
+        functools.partial(pack_kernel, chunks, blocks),
         in_specs=[pl.BlockSpec(memory_space=VMEM)],
         out_specs=[pl.BlockSpec(memory_space=VMEM)] * len(shapes),
         out_shape=[jax.ShapeDtypeStruct(shape, F32) for shape in shapes],
@@ -69,41 +77,64 @@
     )(x)
 
 
-def prepare_kernel(
-    blocks, w_ref, r_ref, w2_ref, rh_ref, rl_ref, scale_ref, held, r_held, sems, r_sem
-):
+def prepare_kernel(blocks, w_ref, w2_ref, scale_ref, held, sems):
     me = lax.axis_index("var")
     count, width = held.shape[0], held.shape[2]
-    r_copy = pltpu.make_async_copy(r_ref, r_held, r_sem)
-    copies = []
-    for m in range(count):
-        row = block_at(me, m, blocks)
-        copies.append(
-            [
-                pltpu.make_async_copy(w_ref.at[row, slot], held.at[m, place], sems.at[m, place])
-                for place, slot in enumerate((1 + me, 0, 2 - me))
-            ]
+    base = me * (blocks - count)
+    chunks = sems.shape[0]
+    edges = [count * c // chunks for c in range(chunks + 1)]
+    copies = [
+        pltpu.make_async_copy(
+            w_ref.at[pl.ds(base + first, last - first)], held.at[pl.ds(first, last - first)], sem
         )
-    for m, group in enumerate(copies):
-        for copy in group:
-            copy.start(priority=m % 2)
-    r_copy.start(priority=1)
+        for first, last, sem in zip(edges[:-1], edges[1:], [sems.at[c] for c in range(chunks)])
+    ]
+    for copy in copies:
+        copy.start()
     top = jnp.zeros((8, width), F32)
-    for m, group in enumerate(copies):
-        for place, copy in enumerate(group):
-            copy.wait()
-            w = held[m, place]
-            high, low = halves(w)
-            lanes = slice(place * width, (place + 1) * width)
-            w2_ref[m, :width, lanes] = high
-            w2_ref[m, width:, lanes] = low
-            top = jnp.maximum(top, jnp.max(jnp.abs(w).reshape(-1, 8, width), axis=0))
-    r_copy.wait()
+    for c, copy in enumerate(copies):
+        copy.wait()
+        for row in range(edges[c], edges[c + 1]):
+            m = block_at(me, row, count)
+            for place, slot in enumerate((1 + me, 0, 2 - me)):
+                w = held[row, slot]
+                high, low = halves(w)
+                lanes = slice(place * width, (place + 1) * width)
+                w2_ref[m, :width, lanes] = high
+                w2_ref[m, width:, lanes] = low
+                top = jnp.maximum(top, jnp.max(jnp.abs(w).reshape(-1, 8, width), axis=0))
+    space_top = jnp.max(jnp.max(top, axis=0, keepdims=True), axis=1, keepdims=True)
+    space_top = jnp.where(space_top > 0, space_top, 1.0)
+    scale_ref[...] = jnp.broadcast_to(space_top, scale_ref.shape)
+
+
+def prepare(spatial):
+    blocks, slots, width, _ = spatial.shape
+    count = blocks // 2
+    return pl.pallas_call(
+        functools.partial(prepare_kernel, blocks),
+        in_specs=[pl.BlockSpec(memory_space=pl.ANY)],
+        out_specs=[pl.BlockSpec(memory_space=VMEM)] * 2,
+        out_shape=[
+            jax.ShapeDtypeStruct((count, 2 * width, slots * width), BF16),
+            jax.ShapeDtypeStruct((8, width), F32),
+        ],
+        scratch_shapes=[
+            VMEM((count, slots, width, width), F32),
+            pltpu.SemaphoreType.DMA((4,)),
+        ],
+        compiler_params=pltpu.CompilerParams(vmem_limit_bytes=ROOMY),
+        cost_estimate=COST,
+        name="prepare",
+    )(spatial)
+
+
+def mixer_kernel(season_ref, top_ref, rh_ref, rl_ref, scale_ref):
     r = jnp.concatenate(
         [
             jnp.concatenate(
                 [
-                    r_held[pl.ds(VARS * v + w, SEASONS, stride=VARS * VARS), :]
+                    season_ref[pl.ds(VARS * v + w, SEASONS, stride=VARS * VARS), :]
                     for w in range(VARS)
                 ],
                 axis=1,
@@ -112,40 +143,28 @@
         ],
         axis=0,
     )
-    space_top = jnp.max(jnp.max(top, axis=0, keepdims=True), axis=1, keepdims=True)
+    space_top = top_ref[:1, :1]
     season_top = jnp.max(jnp.max(jnp.abs(r), axis=0, keepdims=True), axis=1, keepdims=True)
-    space_top = jnp.where(space_top > 0, space_top, 1.0)
     season_top = jnp.where(season_top > 0, season_top, 1.0)
-    high, low = halves(r / season_top / space_top)
-    rh_ref[...] = high
-    rl_ref[...] = low
+    rh_ref[...], rl_ref[...] = halves(r / season_top / space_top)
     rows = lax.broadcasted_iota(jnp.int32, scale_ref.shape, 0)
     scale_ref[...] = jnp.where(rows == 4, space_top, jnp.where(rows == 5, season_top, 0.0))
 
 
-def prepare(spatial, season):
-    blocks, slots, width, _ = spatial.shape
-    count = blocks // 2 + 1
+def make_mixer(season, top):
     return pl.pallas_call(
-        functools.partial(prepare_kernel, blocks),
-        in_specs=[pl.BlockSpec(memory_space=pl.ANY)] * 2,
-        out_specs=[pl.BlockSpec(memory_space=VMEM)] * 4,
+        mixer_kernel,
+        in_specs=[pl.BlockSpec(memory_space=VMEM)] * 2,
+        out_specs=[pl.BlockSpec(memory_space=VMEM)] * 3,
         out_shape=[
-            jax.ShapeDtypeStruct((count, 2 * width, slots * width), BF16),
             jax.ShapeDtypeStruct((ORDER, ORDER), BF16),
             jax.ShapeDtypeStruct((ORDER, ORDER), BF16),
-            jax.ShapeDtypeStruct((8, width), F32),
+            jax.ShapeDtypeStruct(top.shape, F32),
         ],
-        scratch_shapes=[
-            VMEM((count, slots, width, width), F32),
-            VMEM(season.shape, F32),
-            pltpu.SemaphoreType.DMA((count, slots)),
-            pltpu.SemaphoreType.DMA,
-        ],
-        compiler_params=pltpu.CompilerParams(vmem_limit_bytes=ROOMY),
+        compiler_params=pltpu.CompilerParams(vmem_limit_bytes=LIMIT),
         cost_estimate=COST,
-        name="prepare",
-    )(spatial, season)
+        name="mixer",
+    )(season, top)
 
 
 def row_starts(seasons, parts):
@@ -169,48 +188,60 @@
     return both[:ORDER, :width] + both[:ORDER, width:] + both[ORDER:, :width]
 
 
-def edge_kernel(blocks, parts, w2_ref, count_ref, *refs):
-    *fields, out_ref, held = refs
+def edge_kernel(blocks, parts, first, w2_ref, count_ref, *refs):
+    *fields, outer_ref, inner_ref, held = refs
     me = lax.axis_index("var")
     seasons, width = fields[0].shape[1:]
-    for start, field in zip(row_starts(seasons, parts), fields):
+    half = blocks // 2
+    ends = (0, 1, half - 2, half - 1)
+    for k, (start, field) in enumerate(zip(row_starts(seasons, parts), fields)):
         season = (iota(seasons, width) + lax.rem(start, SEASONS)).astype(F32)
-        for m in range(2):
+        for n, m in enumerate(ends):
             seen = season >= SEASONS - count_ref[pl.ds(block_at(me, m, blocks), 1), :]
-            held[m, pl.ds(start, seasons), :] = jnp.where(seen, field[m], 0.0)
-    high, low = halves(jnp.concatenate([held[0], held[1]], axis=1))
-    out_ref[:ORDER, :] = held[0]
-    out_ref[ORDER : 2 * ORDER, :] = space_product(high, low, w2_ref[0, :, width:])
-    out_ref[2 * ORDER :, :] = jnp.broadcast_to(
+            piece = field[m if k < VARS else first.index(m)]
+            held[n, pl.ds(start, seasons), :] = jnp.where(seen, piece, 0.0)
+    for ref, n, at, lanes in (
+        (outer_ref, 0, 0, slice(width, 3 * width)),
+        (inner_ref, 2, half - 1, slice(0, 2 * width)),
+    ):
+        high, low = halves(jnp.concatenate([held[n], held[n + 1]], axis=1))
+        ref[:ORDER, :] = held[0 if n == 0 else 3]
+        ref[ORDER : 2 * ORDER, :] = space_product(high, low, w2_ref[at, :, lanes])
+    outer_ref[2 * ORDER :, :] = jnp.broadcast_to(
         count_ref[pl.ds(block_at(me, 0, blocks), 1), :], (8, width)
     )
 
 
-def edge(w2, count_rows, fields, parts):
+def edge(w2, count_rows, fields, parts, first):
     blocks, width = count_rows.shape
     whole = [pl.BlockSpec(memory_space=VMEM)]
     return pl.pallas_call(
-        functools.partial(edge_kernel, blocks, parts),
+        functools.partial(edge_kernel, blocks, parts, first),
         in_specs=whole * (2 + len(fields)),
-        out_specs=pl.BlockSpec(memory_space=VMEM),
-        out_shape=jax.ShapeDtypeStruct((2 * ORDER + 8, width), F32),
-        scratch_shapes=[VMEM((2, ORDER, width), F32)],
+        out_specs=whole * 2,
+        out_shape=[
+            jax.ShapeDtypeStruct((2 * ORDER + 8, width), F32),
+            jax.ShapeDtypeStruct((2 * ORDER, width), F32),
+        ],
+        scratch_shapes=[VMEM((4, ORDER, width), F32)],
         compiler_params=pltpu.CompilerParams(vmem_limit_bytes=LIMIT),
         cost_estimate=COST,
         name="edge",
     )(w2, count_rows, *fields)
 
 
-def make_plan(cuts, half):
+def make_plan(places_of, half):
     plan = []
     have_x, have_1, have_2 = set(), set(), set()
     for chunks in STAGES:
         new = []
         for c in chunks:
-            new += [-1] if c < 0 else list(range(cuts[c], cuts[c + 1]))
+            new += [-1] if c == OUTER else [half] if c == INNER else places_of[c]
         have_x |= set(new)
         ones = [
-            i for i in range(-1, half + 1) if i not in have_1 and {max(i - 1, -1), i, i + 1} <= have_x
+            i
+            for i in range(-1, half + 1)
+            if i not in have_1 and {max(i - 1, -1), i, min(i + 1, half)} <= have_x
         ]
         have_1 |= set(ones)
         twos = [i for i in range(half) if i not in have_2 and {i - 1, i, i + 1} <= have_1]
@@ -237,13 +268,13 @@
     return groups
 
 
-def make_stage(plan, cuts, m, blocks, parts, seasons, width):
+def make_stage(plan, places_of, m, blocks, parts, seasons, width):
     half = blocks // 2
     slots = parts * VARS
     new, ones, twos, keep_x, keep_1 = plan[m]
     first, last = m == 0, m == len(plan) - 1
     chunks = [c for c in STAGES[m] if c >= 0]
-    outer = -1 in STAGES[m]
+    outer, inner = OUTER in STAGES[m], INNER in STAGES[m]
     old_x, old_1 = ([], []) if first else (plan[m - 1][3], plan[m - 1][4])
     x_at = {i: n for n, i in enumerate(list(old_x) + list(new))}
     one_at = {i: n for n, i in enumerate(list(old_1) + list(ones))}
@@ -263,7 +294,9 @@
         if not first:
             old_xh, old_xl, old_1h, old_1l = take(4)
         if outer:
-            (edge_ref,) = take(1)
+            (outer_ref,) = take(1)
+        if inner:
+            (inner_ref,) = take(1)
         sums_out, mine, theirs = take(3)
         if not last:
             keep_xh, keep_xl, keep_1h, keep_1l = take(4)
@@ -272,7 +305,7 @@
 
         def count_row(i):
             if i == -1:
-                return edge_ref[2 * ORDER : 2 * ORDER + 1, :]
+                return outer_ref[2 * ORDER : 2 * ORDER + 1, :]
             return count_ref[pl.ds(block_at(me, i, blocks), 1), :]
 
         season = lax.rem(iota(ORDER, width), SEASONS).astype(F32)
@@ -290,30 +323,33 @@
         starts = row_starts(seasons, parts)
         total_0 = sums_in[0]
         for c, fars in zip(chunks, far_refs):
-            places = [i for i in new if cuts[c] <= i < cuts[c + 1]]
+            places = places_of[c]
             for k, start in enumerate(starts):
                 piece_season = (iota(seasons, width) + lax.rem(start, SEASONS)).astype(F32)
                 for i in places:
-                    piece = near_refs[k][i] if k < VARS else fars[k - VARS][i - cuts[c]]
-                    if 0 <= i < half:
-                        total_0 += fold(piece * piece)
+                    piece = near_refs[k][i] if k < VARS else fars[k - VARS][places.index(i)]
+                    total_0 += fold(piece * piece)
                     seen = piece_season >= SEASONS - count_row(i)
                     high, low = halves(jnp.where(seen, piece, 0.0))
                     xh[x_at[i], pl.ds(start, seasons), :] = high
                     xl[x_at[i], pl.ds(start, seasons), :] = low
         if outer:
-            xh[x_at[-1]], xl[x_at[-1]] = halves(edge_ref[:ORDER, :])
+            xh[x_at[-1]], xl[x_at[-1]] = halves(outer_ref[:ORDER, :])
+        if inner:
+            xh[x_at[half]], xl[x_at[half]] = halves(inner_ref[:ORDER, :])
         sums_out[0] = total_0
 
         def space(i, high, low, at):
-            if i >= 0:
+            if 0 <= i < half:
                 hs = jnp.concatenate([high[at[i + d]] for d in (-1, 0, 1)], axis=1)
                 ls = jnp.concatenate([low[at[i + d]] for d in (-1, 0, 1)], axis=1)
                 return space_product(hs, ls, w2_ref[i])
-            near = w2_ref[0, :width, :width]
-            total = edge_ref[ORDER : 2 * ORDER, :] + dot(high[at[0]], near, NN)
-            total += dot(high[at[0]], w2_ref[0, width:, :width], NN)
-            return total + dot(low[at[0]], near, NN)
+            ref, last_at, lane = (outer_ref, 0, 0) if i < 0 else (inner_ref, half - 1, 2 * width)
+            lanes = slice(lane, lane + width)
+            near = w2_ref[last_at, :width, lanes]
+            total = ref[ORDER : 2 * ORDER, :] + dot(high[at[last_at]], near, NN)
+            total += dot(high[at[last_at]], w2_ref[last_at, width:, lanes], NN)
+            return total + dot(low[at[last_at]], near, NN)
 
         rh, rl = rh_ref[...], rl_ref[...]
         mixer = jnp.concatenate(
@@ -375,8 +411,8 @@
     return kernel, outs, scratch
 
 
-def run_stage(plan, cuts, m, blocks, parts, seasons, width, operands):
-    kernel, outs, scratch = make_stage(plan, cuts, m, blocks, parts, seasons, width)
+def run_stage(plan, chunks, m, blocks, parts, seasons, width, operands):
+    kernel, outs, scratch = make_stage(plan, chunks, m, blocks, parts, seasons, width)
     return pl.pallas_call(
         kernel,
         in_specs=[pl.BlockSpec(memory_space=VMEM)] * len(operands),
@@ -515,29 +551,30 @@
     blocks, _, width, _ = spatial.shape
     parts = lax.axis_size("season")
     half = blocks // 2
-    cuts = (0,) + CUTS + (half + 2,)
-    plan = make_plan(cuts, half)
+    places = make_chunks(half)
+    plan = make_plan(places, half)
 
     x = right_side.reshape(seasons * blocks, width)
     count_rows = jnp.broadcast_to(counts.astype(F32)[:, None], (blocks, width))
 
-    same, other, *packs = pack(x, cuts, blocks)
+    same, other, *packs = pack(x, places, blocks)
     close = [same, from_group(other, 0, 1)]
     chunks = [
         [from_group(pair[w], d, w) for d in range(1, parts) for w in range(VARS)]
         for pair in zip(packs[0::2], packs[1::2])
     ]
-    w2, rh, rl, scale = prepare(
-        spatial, season_cov.transpose(0, 1, 3, 2).reshape(SEASONS * VARS * VARS, SEASONS)
-    )
-    outer = across_edge(edge(w2, count_rows, close + chunks[0], parts))
-
+    w2, top = prepare(spatial)
+    outer, inner = edge(w2, count_rows, close + chunks[0], parts, places[0])
+    outer, inner = across_edge(outer), from_group(inner, 0, 1)
+
+    season = season_cov.transpose(0, 1, 3, 2).reshape(SEASONS * VARS * VARS, SEASONS)
+    rh, rl, scale = make_mixer(season, top)
     sums = jnp.zeros((4, 8, width), F32)
     mine, theirs, kept = [], [], []
     for m, stage in enumerate(STAGES):
         operands = close + [f for c in stage if c >= 0 for f in chunks[c]]
-        operands += [w2, rh, rl, count_rows, sums] + kept + [outer] * (-1 in stage)
-        out = run_stage(plan, cuts, m, blocks, parts, seasons, width, operands)
+        operands += [w2, rh, rl, count_rows, sums] + kept + [outer] * (OUTER in stage) + [inner] * (INNER in stage)
+        out = run_stage(plan, places, m, blocks, parts, seasons, width, operands)
         sums, kept = out[0], list(out[3:])
         mine.append(out[1])
         theirs.append(from_group(out[2], 0, 1))

time: 31.3 us -> 30.6 us (0.978)
  waiting for transfers between devices: 3.99 us -> 5.43 us
  local copies, waits for them, and re-layouts: 2.03 us -> 1.12 us
  Pallas kernels: 9.02 us -> 8.41 us
  starting transfers between devices: 15.3 us -> 14.7 us
    ppermute x10 -> x11, waiting for transfers between devices: 0.99 us -> 2 us  [from_group(): return lax.ppermute(value, ('season', 'var'), pairs)]
    unnamed x6, local copies, waits for them, and re-layouts: 1.95 us -> 1.05 us
    pallas_call x1, Pallas kernels: 2.9 us -> 2.1 us  [prepare(): pl.pallas_call(functools.partial(prepare_kernel, blocks), in_specs=[pl.Bl...]
    ppermute x2, starting transfers between devices: 4.15 us -> 3.71 us  [gather_tiles(): found.append(lax.ppermute(have, ('space', 'var'), pairs))]
    ppermute x2, waiting for transfers between devices: 3 us -> 3.43 us  [gather_tiles(): found.append(lax.ppermute(have, ('space', 'var'), pairs))]
    pallas_call x2 -> x3, Pallas kernels: 0.57 us -> 0.79 us  [the longest x1 0.32 us: pack(): pl.pallas_call(functools.partial(pack_kernel, chunks, blocks), in_specs=[...]
    ppermute x10 -> x11, starting transfers between devices: 10.5 us -> 10.3 us  [from_group(): return lax.ppermute(value, ('season', 'var'), pairs)]
  transfers between devices with their start and end apart: 13 -> 14, of which waited for: 4 -> 6; matrix products, arithmetic and copies ran while one was open for 0% -> 0% of each run, Pallas kernels for 22% -> 21%
where the time goes in v6:
time: 30.6 us; the launch traced here: 30.5 us
  starting transfers between devices  14.7 us (48%)
  Pallas kernels  8.41 us (27%)
  waiting for transfers between devices  5.43 us (18%)
  local copies, waits for them, and re-layouts  1.12 us (4%)
  between operations  0.74 us (2%)
    ppermute x11, starting transfers between devices, from_group(): return lax.ppermute(value, ('season', 'var'), pairs)  10.3 us
    pallas_call x2, Pallas kernels, run_stage(): pl.pallas_call(kernel, in_specs=[pl.BlockSpec(memory_space=VMEM)] * len(o...  3.84 us
    ppermute x2, starting transfers between devices, gather_tiles(): found.append(lax.ppermute(have, ('space', 'var'), pairs))  3.71 us
    ppermute x2, waiting for transfers between devices, gather_tiles(): found.append(lax.ppermute(have, ('space', 'var'), pairs))  3.43 us
    pallas_call x1, Pallas kernels, prepare(): pl.pallas_call(functools.partial(prepare_kernel, blocks), in_specs=[pl.Bl...  2.1 us
    ppermute x11, waiting for transfers between devices, from_group(): return lax.ppermute(value, ('season', 'var'), pairs)  2 us
    pallas_call x1, Pallas kernels, finish(): pl.pallas_call(functools.partial(finish_kernel, plan, blocks, len(gathere...  1.69 us
    unnamed x6, local copies, waits for them, and re-layouts  1.05 us
  transfers between devices with their start and end apart: 14, of which 6 were waited for; matrix products, arithmetic and copies ran while one was open for 0% of the time, Pallas kernels for 21%

profile of v6, /device:TPU:0, one launch (start us, length us, event | category | flops | bytes accessed | tf_op | source)
XLA Modules:
  0.0 30.5 jit_solution(11963176673492245833)
XLA Ops:
  0.6 1.0 %copy-done = f32[32,1,4096]{2,1,0:T(1,128)S(1)} copy-done((f32[32,1,4096]{2,1,0:T(1,128)S(1)}, f32[32,1,4096]{2,1,0:T(1,128)}, u32[]{:S(2)}) %copy-start) | copy-done | bytes 524312
  1.7 0.3 %pack.1 = (f32[16,32,128]{2,1,0:T(8,128)S(1)}, f32[16,32,128]{2,1,0:T(8,128)S(1)}, f32[4,32,128]{2,1,0:T(8,128)S(1)}, f32[4,32,128]{2,1,0:T(8,128)S(1)}, f32[9,3...) custom-call(f32[1024,128]{1,0:T(8,128)S(1)} %bitcast.8), custom_call_target="tpu_custom_call" | custom-call | flops 1 | bytes 1 | tf_op jit(solution)/shard_map/pack/pallas_call | solution.py:69
  2.0 0.5 %collective-permute-start = (f32[16,32,128]{2,1,0:T(8,128)S(1)}, f32[16,32,128]{2,1,0:T(8,128)S(1)}, u32[]{:S(2)}, u32[]{:S(2)}) collective-permute-start(f32[16,32,128]{2,1,0:T(8,128)S(1)} %get-tuple-element.30.refs_5_), channel_id=1, source_target_pairs={{1,0},{0,1},{3,2},{2,3},{5,4},{4,5},{7,6},{6,7},{9,8},{8,9},{11,10... | collective-permute-start | bytes 786440 | tf_op jit(solution)/shard_map/ppermute | solution.py:519
  2.5 2.6 %collective-permute-start.3 = (f32[4,32,128]{2,1,0:T(8,128)S(1)}, f32[4,32,128]{2,1,0:T(8,128)S(1)}, u32[]{:S(2)}, u32[]{:S(2)}) collective-permute-start(f32[4,32,128]{2,1,0:T(8,128)S(1)} %get-tuple-element.37), channel_id=1, source_target_pairs={{2,0},{3,1},{0,2},{1,3},{6,4},{7,5},{4,6},{5,7},{10,8},{11,9},{8,1... | collective-permute-start | bytes 196616 | tf_op jit(solution)/shard_map/ppermute | solution.py:519
  5.1 0.1 collective-permute-start.4
  5.2 1.7 %collective-permute-start.5 = (f32[9,32,128]{2,1,0:T(8,128)S(1)}, f32[9,32,128]{2,1,0:T(8,128)S(1)}, u32[]{:S(2)}, u32[]{:S(2)}) collective-permute-start(f32[9,32,128]{2,1,0:T(8,128)S(1)} %get-tuple-element.39), channel_id=1, source_target_pairs={{2,0},{3,1},{0,2},{1,3},{6,4},{7,5},{4,6},{5,7},{10,8},{11,9},{8,1... | collective-permute-start | bytes 442376 | tf_op jit(solution)/shard_map/ppermute | solution.py:519
  6.9 0.0 collective-permute-start.6
  6.9 2.1 %prepare.1 = (bf16[16,256,384]{2,1,0:T(8,128)(2,1)S(1)}, f32[8,128]{1,0:T(8,128)S(1)}) custom-call(f32[32,3,128,128]{3,2,1,0:T(8,128)} %w_ref.1), custom_call_target="tpu_custom_call" | custom-call | flops 1 | bytes 1 | tf_op jit(solution)/shard_map/prepare/pallas_call | solution.py:114
  9.0 0.0 collective-permute-done.3.refs_2_
  9.1 0.1 collective-permute-done.4.refs_3_
  9.2 0.1 broadcast_in_dim.12.count_ref.refs_9_.refs_7_
  9.2 0.3 edge.1
  9.5 0.7 %collective-permute-start.8 = (f32[264,128]{1,0:T(8,128)S(1)}, f32[264,128]{1,0:T(8,128)S(1)}, u32[]{:S(2)}, u32[]{:S(2)}) collective-permute-start(f32[264,128]{1,0:T(8,128)S(1)} %get-tuple-element.47), channel_id=1, source_target_pairs={{1,4},{4,1},{5,8},{8,5},{9,12},{12,9},{3,6},{6,3},{7,10},{10,7},{1... | collective-permute-start | bytes 405512 | tf_op jit(solution)/shard_map/ppermute | solution.py:527
  10.2 3.1 %collective-permute-start.7 = (f32[256,128]{1,0:T(8,128)S(1)}, f32[256,128]{1,0:T(8,128)S(1)}, u32[]{:S(2)}, u32[]{:S(2)}) collective-permute-start(f32[256,128]{1,0:T(8,128)S(1)} %get-tuple-element.41), channel_id=1, source_target_pairs={{1,0},{0,1},{3,2},{2,3},{5,4},{4,5},{7,6},{6,7},{9,8},{8,9},{11,10... | collective-permute-start | bytes 393224 | tf_op jit(solution)/shard_map/ppermute | solution.py:519
  13.3 1.5 %collective-permute-start.1 = (f32[3,32,128]{2,1,0:T(8,128)S(1)}, f32[3,32,128]{2,1,0:T(8,128)S(1)}, u32[]{:S(2)}, u32[]{:S(2)}) collective-permute-start(f32[3,32,128]{2,1,0:T(8,128)S(1)} %get-tuple-element.31), channel_id=1, source_target_pairs={{2,0},{3,1},{0,2},{1,3},{6,4},{7,5},{4,6},{5,7},{10,8},{11,9},{8,1... | collective-permute-start | bytes 147464 | tf_op jit(solution)/shard_map/ppermute | solution.py:519
  14.8 0.0 collective-permute-done.5.refs_4_
  14.8 0.0 collective-permute-start.2
  14.8 0.2 mixer.1
  15.0 0.5 %collective-permute-done.6.refs_5_ = f32[9,32,128]{2,1,0:T(8,128)S(1)} collective-permute-done((f32[9,32,128]{2,1,0:T(8,128)S(1)}, f32[9,32,128]{2,1,0:T(8,128)S(1)}, u32[]{:S(2)}, u32[]{:S(2)}) %collective-permute-start.6) | collective-permute-done | bytes 147488 | tf_op jit(solution)/shard_map/ppermute | solution.py:519
  15.5 2.3 %stage.2 = (f32[4,8,128]{2,1,0:T(8,128)S(1)}, f32[19,32,128]{2,1,0:T(8,128)S(1)}, f32[19,32,128]{2,1,0:T(8,128)S(1)}, bf16[4,128,128]{2,1,0:T(8,128)(2,1)S(1)}, ...) custom-call(f32[16,32,128]{2,1,0:T(8,128)S(1)} %get-tuple-element.29.refs_0_.ref, ...), custom_call_target="tpu_custom_call" | custom-call | flops 1 | bytes 1 | tf_op jit(solution)/shard_map/stage/pallas_call | solution.py:416
  17.8 0.3 collective-permute-start.12
  18.0 0.8 %collective-permute-done.2.refs_3_ = f32[3,32,128]{2,1,0:T(8,128)S(1)} collective-permute-done((f32[3,32,128]{2,1,0:T(8,128)S(1)}, f32[3,32,128]{2,1,0:T(8,128)S(1)}, u32[]{:S(2)}, u32[]{:S(2)}) %collective-permute-start.2) | collective-permute-done | bytes 49184 | tf_op jit(solution)/shard_map/ppermute | solution.py:519
  18.8 1.6 %stage.3 = (f32[4,8,128]{2,1,0:T(8,128)S(1)}, f32[13,32,128]{2,1,0:T(8,128)S(1)}, f32[13,32,128]{2,1,0:T(8,128)S(1)}) custom-call(f32[16,32,128]{2,1,0:T(8,128)S(1)} %get-tuple-element.29.refs_0_.refs_4_, f32[16,32,128]{2,1,0:T(8,128)S(1)} %collective-permute-done.refs_1_, f32[3,32,128]{2,1,0:T(8,128)S(1)} %collective-permute-done.1.refs_2_, ...), custom_call_target="tpu_custom_call" | custom-call | flops 1 | bytes 1 | tf_op jit(solution)/shard_map/stage/pallas_call | solution.py:416
  20.4 0.2 collective-permute-start.9
  20.6 0.4 %collective-permute-start.13 = (f32[13,32,128]{2,1,0:T(8,128)S(1)}, f32[13,32,128]{2,1,0:T(8,128)S(1)}, u32[]{:S(2)}, u32[]{:S(2)}) collective-permute-start(f32[13,32,128]{2,1,0:T(8,128)S(1)} %get-tuple-element.53), channel_id=1, source_target_pairs={{1,0},{0,1},{3,2},{2,3},{5,4},{4,5},{7,6},{6,7},{9,8},{8,9},{11,10... | collective-permute-start | bytes 638984 | tf_op jit(solution)/shard_map/ppermute | solution.py:519
  21.0 0.7 %collective-permute-done.9.refs_1_ = f32[1,8,128]{2,1,0:T(8,128)S(1)} collective-permute-done((f32[1,8,128]{2,1,0:T(8,128)S(1)}, f32[1,8,128]{2,1,0:T(8,128)S(1)}, u32[]{:S(2)}, u32[]{:S(2)}) %collective-permute-start.9) | collective-permute-done | bytes 4128 | tf_op jit(solution)/shard_map/ppermute | solution.py:519
  21.6 1.3 %collective-permute-start.10 = (f32[2,8,128]{2,1,0:T(8,128)S(1)}, f32[2,8,128]{2,1,0:T(8,128)S(1)}, u32[]{:S(2)}, u32[]{:S(2)}) collective-permute-start(f32[2,8,128]{2,1,0:T(8,128)S(1)} %pad_maximum_fusion.1), channel_id=1, source_target_pairs={{0,5},{1,4},{4,1},{5,0},{8,13},{9,12},{12,9},{13,8},{2,7},{3,6},{6... | collective-permute-start | bytes 24584 | tf_op jit(solution)/shard_map/ppermute | solution.py:543
  23.0 1.7 %collective-permute-done.10.refs_2_ = f32[2,8,128]{2,1,0:T(8,128)S(1)} collective-permute-done((f32[2,8,128]{2,1,0:T(8,128)S(1)}, f32[2,8,128]{2,1,0:T(8,128)S(1)}, u32[]{:S(2)}, u32[]{:S(2)}) %collective-permute-start.10) | collective-permute-done | bytes 8224 | tf_op jit(solution)/shard_map/ppermute | solution.py:543
  24.7 2.4 %collective-permute-start.11 = (f32[4,8,128]{2,1,0:T(8,128)S(1)}, f32[4,8,128]{2,1,0:T(8,128)S(1)}, u32[]{:S(2)}, u32[]{:S(2)}) collective-permute-start(f32[4,8,128]{2,1,0:T(8,128)S(1)} %pad_maximum_fusion), channel_id=1, source_target_pairs={{0,9},{1,8},{4,13},{5,12},{8,1},{9,0},{12,5},{13,4},{2,11},{3,10},... | collective-permute-start | bytes 49160 | tf_op jit(solution)/shard_map/ppermute | solution.py:543
  27.1 1.7 %collective-permute-done.11.refs_3_ = f32[4,8,128]{2,1,0:T(8,128)S(1)} collective-permute-done((f32[4,8,128]{2,1,0:T(8,128)S(1)}, f32[4,8,128]{2,1,0:T(8,128)S(1)}, u32[]{:S(2)}, u32[]{:S(2)}) %collective-permute-start.11) | collective-permute-done | bytes 16416 | tf_op jit(solution)/shard_map/ppermute | solution.py:543
  28.8 0.0 collective-permute-done.13.refs_9_
  28.8 1.7 %finish.1 = (f32[32,32,1,128]{3,2,1,0:T(1,128)}, f32[32,32,1,128]{3,2,1,0:T(1,128)}) custom-call(f32[1,8,128]{2,1,0:T(8,128)S(1)} %maximum_bitcast_fusion.refs_0_, f32[1,8,128]{2,1,0:T(8,128)S(1)} %collective-permute-done.9.refs_1_, f32[2,8,128]{2,1,0:T(8,128)S(1)} %collective-permute-done.10.refs_2_, f32[4,8,128]{2,1,0:T(8,128)S(1)} %collective-permute-done.11.refs_3_, ...), custom_call_target="tpu_custom_call" | custom-call | flops 1 | bytes 1 | tf_op jit(solution)/shard_map/finish/pallas_call | solution.py:499
  (17 shorter events, 0.1 us)
Async XLA Ops:
  0.6 8.4 %copy-start.2 = (s32[32]{0:T(128)S(1)}, s32[32]{0:T(128)}, u32[]{:S(2)}) copy-start(s32[32]{0:T(128)} %param.7) | copy-start | bytes 388
  0.6 1.0 %copy-start = (f32[32,1,4096]{2,1,0:T(1,128)S(1)}, f32[32,1,4096]{2,1,0:T(1,128)}, u32[]{:S(2)}) copy-start(f32[32,1,4096]{2,1,0:T(1,128)} %param.5) | copy-start | bytes 1572868
  1.7 13.1 %copy-start.1 = (f32[64,2,64,2]{2,3,1,0:T(2,128)S(1)}, f32[64,2,64,2]{2,3,1,0:T(2,128)}, u32[]{:S(2)}) copy-start(f32[64,2,64,2]{2,3,1,0:T(2,128)} %param.8) | copy-start | bytes 196612
  2.0 7.1 %collective-permute-start = (f32[16,32,128]{2,1,0:T(8,128)S(1)}, f32[16,32,128]{2,1,0:T(8,128)S(1)}, u32[]{:S(2)}, u32[]{:S(2)}) collective-permute-start(f32[16,32,128]{2,1,0:T(8,128)S(1)} %get-tuple-element.30.refs_5_), channel_id=1, source_target_pairs={{1,0},{0,1},{3,2},{2,3},{5,4},{4,5},{7,6},{6,7},{9,8},{8,9},{11,10... | collective-permute-start | bytes 786440 | tf_op jit(solution)/shard_map/ppermute | solution.py:519
  2.5 6.5 %collective-permute-start.3 = (f32[4,32,128]{2,1,0:T(8,128)S(1)}, f32[4,32,128]{2,1,0:T(8,128)S(1)}, u32[]{:S(2)}, u32[]{:S(2)}) collective-permute-start(f32[4,32,128]{2,1,0:T(8,128)S(1)} %get-tuple-element.37), channel_id=1, source_target_pairs={{2,0},{3,1},{0,2},{1,3},{6,4},{7,5},{4,6},{5,7},{10,8},{11,9},{8,1... | collective-permute-start | bytes 196616 | tf_op jit(solution)/shard_map/ppermute | solution.py:519
  5.1 4.0 %collective-permute-start.4 = (f32[4,32,128]{2,1,0:T(8,128)S(1)}, f32[4,32,128]{2,1,0:T(8,128)S(1)}, u32[]{:S(2)}, u32[]{:S(2)}) collective-permute-start(f32[4,32,128]{2,1,0:T(8,128)S(1)} %get-tuple-element.38), channel_id=1, source_target_pairs={{3,0},{2,1},{1,2},{0,3},{7,4},{6,5},{5,6},{4,7},{11,8},{10,9},{9,1... | collective-permute-start | bytes 196616 | tf_op jit(solution)/shard_map/ppermute | solution.py:519
  5.2 9.6 %collective-permute-start.5 = (f32[9,32,128]{2,1,0:T(8,128)S(1)}, f32[9,32,128]{2,1,0:T(8,128)S(1)}, u32[]{:S(2)}, u32[]{:S(2)}) collective-permute-start(f32[9,32,128]{2,1,0:T(8,128)S(1)} %get-tuple-element.39), channel_id=1, source_target_pairs={{2,0},{3,1},{0,2},{1,3},{6,4},{7,5},{4,6},{5,7},{10,8},{11,9},{8,1... | collective-permute-start | bytes 442376 | tf_op jit(solution)/shard_map/ppermute | solution.py:519
  6.9 8.6 %collective-permute-start.6 = (f32[9,32,128]{2,1,0:T(8,128)S(1)}, f32[9,32,128]{2,1,0:T(8,128)S(1)}, u32[]{:S(2)}, u32[]{:S(2)}) collective-permute-start(f32[9,32,128]{2,1,0:T(8,128)S(1)} %get-tuple-element.40), channel_id=1, source_target_pairs={{3,0},{2,1},{1,2},{0,3},{7,4},{6,5},{5,6},{4,7},{11,8},{10,9},{9,1... | collective-permute-start | bytes 442376 | tf_op jit(solution)/shard_map/ppermute | solution.py:519
  9.5 9.3 %collective-permute-start.8 = (f32[264,128]{1,0:T(8,128)S(1)}, f32[264,128]{1,0:T(8,128)S(1)}, u32[]{:S(2)}, u32[]{:S(2)}) collective-permute-start(f32[264,128]{1,0:T(8,128)S(1)} %get-tuple-element.47), channel_id=1, source_target_pairs={{1,4},{4,1},{5,8},{8,5},{9,12},{12,9},{3,6},{6,3},{7,10},{10,7},{1... | collective-permute-start | bytes 405512 | tf_op jit(solution)/shard_map/ppermute | solution.py:527
  10.2 5.3 %collective-permute-start.7 = (f32[256,128]{1,0:T(8,128)S(1)}, f32[256,128]{1,0:T(8,128)S(1)}, u32[]{:S(2)}, u32[]{:S(2)}) collective-permute-start(f32[256,128]{1,0:T(8,128)S(1)} %get-tuple-element.41), channel_id=1, source_target_pairs={{1,0},{0,1},{3,2},{2,3},{5,4},{4,5},{7,6},{6,7},{9,8},{8,9},{11,10... | collective-permute-start | bytes 393224 | tf_op jit(solution)/shard_map/ppermute | solution.py:519
  13.3 4.7 %collective-permute-start.1 = (f32[3,32,128]{2,1,0:T(8,128)S(1)}, f32[3,32,128]{2,1,0:T(8,128)S(1)}, u32[]{:S(2)}, u32[]{:S(2)}) collective-permute-start(f32[3,32,128]{2,1,0:T(8,128)S(1)} %get-tuple-element.31), channel_id=1, source_target_pairs={{2,0},{3,1},{0,2},{1,3},{6,4},{7,5},{4,6},{5,7},{10,8},{11,9},{8,1... | collective-permute-start | bytes 147464 | tf_op jit(solution)/shard_map/ppermute | solution.py:519
  14.8 4.0 %collective-permute-start.2 = (f32[3,32,128]{2,1,0:T(8,128)S(1)}, f32[3,32,128]{2,1,0:T(8,128)S(1)}, u32[]{:S(2)}, u32[]{:S(2)}) collective-permute-start(f32[3,32,128]{2,1,0:T(8,128)S(1)} %get-tuple-element.32), channel_id=1, source_target_pairs={{3,0},{2,1},{1,2},{0,3},{7,4},{6,5},{5,6},{4,7},{11,8},{10,9},{9,1... | collective-permute-start | bytes 147464 | tf_op jit(solution)/shard_map/ppermute | solution.py:519
  17.8 11.0 %collective-permute-start.12 = (f32[19,32,128]{2,1,0:T(8,128)S(1)}, f32[19,32,128]{2,1,0:T(8,128)S(1)}, u32[]{:S(2)}, u32[]{:S(2)}) collective-permute-start(f32[19,32,128]{2,1,0:T(8,128)S(1)} %get-tuple-element.52), channel_id=1, source_target_pairs={{1,0},{0,1},{3,2},{2,3},{5,4},{4,5},{7,6},{6,7},{9,8},{8,9},{11,10... | collective-permute-start | bytes 933896 | tf_op jit(solution)/shard_map/ppermute | solution.py:519
  20.4 1.2 %collective-permute-start.9 = (f32[1,8,128]{2,1,0:T(8,128)S(1)}, f32[1,8,128]{2,1,0:T(8,128)S(1)}, u32[]{:S(2)}, u32[]{:S(2)}) collective-permute-start(f32[1,8,128]{2,1,0:T(8,128)S(1)} %maximum_bitcast_fusion.refs_0_), channel_id=1, source_target_pairs={{1,0},{0,1},{3,2},{2,3},{5,4},{4,5},{7,6},{6,7},{9,8},{8,9},{11,10... | collective-permute-start | bytes 12296 | tf_op jit(solution)/shard_map/ppermute | solution.py:519
  20.6 8.2 %collective-permute-start.13 = (f32[13,32,128]{2,1,0:T(8,128)S(1)}, f32[13,32,128]{2,1,0:T(8,128)S(1)}, u32[]{:S(2)}, u32[]{:S(2)}) collective-permute-start(f32[13,32,128]{2,1,0:T(8,128)S(1)} %get-tuple-element.53), channel_id=1, source_target_pairs={{1,0},{0,1},{3,2},{2,3},{5,4},{4,5},{7,6},{6,7},{9,8},{8,9},{11,10... | collective-permute-start | bytes 638984 | tf_op jit(solution)/shard_map/ppermute | solution.py:519
  21.6 3.1 %collective-permute-start.10 = (f32[2,8,128]{2,1,0:T(8,128)S(1)}, f32[2,8,128]{2,1,0:T(8,128)S(1)}, u32[]{:S(2)}, u32[]{:S(2)}) collective-permute-start(f32[2,8,128]{2,1,0:T(8,128)S(1)} %pad_maximum_fusion.1), channel_id=1, source_target_pairs={{0,5},{1,4},{4,1},{5,0},{8,13},{9,12},{12,9},{13,8},{2,7},{3,6},{6... | collective-permute-start | bytes 24584 | tf_op jit(solution)/shard_map/ppermute | solution.py:543
  24.7 4.1 %collective-permute-start.11 = (f32[4,8,128]{2,1,0:T(8,128)S(1)}, f32[4,8,128]{2,1,0:T(8,128)S(1)}, u32[]{:S(2)}, u32[]{:S(2)}) collective-permute-start(f32[4,8,128]{2,1,0:T(8,128)S(1)} %pad_maximum_fusion), channel_id=1, source_target_pairs={{0,9},{1,8},{4,13},{5,12},{8,1},{9,0},{12,5},{13,4},{2,11},{3,10},... | collective-permute-start | bytes 49160 | tf_op jit(solution)/shard_map/ppermute | solution.py:543

commit v7 on v6

--- a/solution.py
+++ b/solution.py
@@ -207,6 +207,7 @@
         high, low = halves(jnp.concatenate([held[n], held[n + 1]], axis=1))
         ref[:ORDER, :] = held[0 if n == 0 else 3]
         ref[ORDER : 2 * ORDER, :] = space_product(high, low, w2_ref[at, :, lanes])
+    inner_ref[2 * ORDER :, :] = jnp.zeros((16, width), F32)
     outer_ref[2 * ORDER :, :] = jnp.broadcast_to(
         count_ref[pl.ds(block_at(me, 0, blocks), 1), :], (8, width)
     )
@@ -221,7 +222,7 @@
         out_specs=whole * 2,
         out_shape=[
             jax.ShapeDtypeStruct((2 * ORDER + 8, width), F32),
-            jax.ShapeDtypeStruct((2 * ORDER, width), F32),
+            jax.ShapeDtypeStruct((2 * ORDER + 16, width), F32),
         ],
         scratch_shapes=[VMEM((4, ORDER, width), F32)],
         compiler_params=pltpu.CompilerParams(vmem_limit_bytes=LIMIT),
@@ -470,7 +471,7 @@
         one_at.update({i: (m, n) for n, i in enumerate(inner)})
         two_at.update({i: (m, len(inner) + n) for n, i in enumerate(twos)})
     copies = []
-    for side, (half_id, held, t) in enumerate(((me, mine, tuples[0]), (1 - me, theirs, tuples[1]))):
+    for side, (half_id, held, t) in enumerate(((me, mine, tuples[0]), (1 - me, theirs, tuples[len(tuples) // 2]))):
         ratio = (t[4:5] / top)[:, :1]
         x_1h, r_1h, r_2h = x_1 * ratio, r_1 * ratio, r_2 * ratio * ratio
         for i in range(half):
@@ -528,12 +529,13 @@
 
 
 def gather_tiles(value):
-    found = [value, from_group(value, 0, 1)]
+    found = [value]
     size = lax.axis_size("space")
     if size & (size - 1):
         me = lax.axis_index("space")
-        tiles = lax.all_gather(jnp.concatenate(found, axis=0), "space", axis=0, tiled=True)
-        return [jnp.roll(tiles, -me * VARS, axis=0)]
+        tiles = lax.all_gather(value, "space", axis=0, tiled=True)
+        found = [jnp.roll(tiles, -me, axis=0)]
+        size = 1
     hop = 1
     while hop < size:
         have = jnp.concatenate(found, axis=0)
@@ -542,6 +544,7 @@
         ]
         found.append(lax.ppermute(have, ("space", "var"), pairs))
         hop *= 2
+    found.append(from_group(jnp.concatenate(found, axis=0), 0, 1))
     return found
 
 

time: 30.6 us -> 30.3 us (level)
  waiting for transfers between devices: 5.43 us -> 4.92 us
    ppermute x2, waiting for transfers between devices: 3.43 us -> 3.01 us  [gather_tiles(): found.append(lax.ppermute(have, ('space', 'var'), pairs))]
  transfers between devices with their start and end apart: 14 -> 14, of which waited for: 6 -> 6; matrix products, arithmetic and copies ran while one was open for 0% -> 0% of each run, Pallas kernels for 21% -> 16%
where the time goes in v7:
time: 30.3 us; the launch traced here: 30.1 us
  starting transfers between devices  14.8 us (49%)
  Pallas kernels  8.42 us (28%)
  waiting for transfers between devices  4.92 us (16%)
  local copies, waits for them, and re-layouts  1.12 us (4%)
  between operations  0.76 us (3%)
    ppermute x11, starting transfers between devices, from_group(): return lax.ppermute(value, ('season', 'var'), pairs)  10.6 us
    pallas_call x2, Pallas kernels, run_stage(): pl.pallas_call(kernel, in_specs=[pl.BlockSpec(memory_space=VMEM)] * len(o...  3.85 us
    ppermute x2, starting transfers between devices, gather_tiles(): found.append(lax.ppermute(have, ('space', 'var'), pairs))  3.58 us
    ppermute x2, waiting for transfers between devices, gather_tiles(): found.append(lax.ppermute(have, ('space', 'var'), pairs))  3.01 us
    pallas_call x1, Pallas kernels, prepare(): pl.pallas_call(functools.partial(prepare_kernel, blocks), in_specs=[pl.Bl...  2.1 us
    ppermute x11, waiting for transfers between devices, from_group(): return lax.ppermute(value, ('season', 'var'), pairs)  1.91 us
    pallas_call x1, Pallas kernels, finish(): pl.pallas_call(functools.partial(finish_kernel, plan, blocks, len(gathere...  1.69 us
    unnamed x6, local copies, waits for them, and re-layouts  1.05 us
  transfers between devices with their start and end apart: 14, of which 6 were waited for; matrix products, arithmetic and copies ran while one was open for 0% of the time, Pallas kernels for 16%

profile of v7, /device:TPU:0, one launch (start us, length us, event | category | flops | bytes accessed | tf_op | source)
XLA Modules:
  0.0 30.1 jit_solution(12714299364004847116)
XLA Ops:
  0.6 1.0 %copy-done = f32[32,1,4096]{2,1,0:T(1,128)S(1)} copy-done((f32[32,1,4096]{2,1,0:T(1,128)S(1)}, f32[32,1,4096]{2,1,0:T(1,128)}, u32[]{:S(2)}) %copy-start) | copy-done | bytes 524312
  1.7 0.3 %pack.1 = (f32[16,32,128]{2,1,0:T(8,128)S(1)}, f32[16,32,128]{2,1,0:T(8,128)S(1)}, f32[4,32,128]{2,1,0:T(8,128)S(1)}, f32[4,32,128]{2,1,0:T(8,128)S(1)}, f32[9,3...) custom-call(f32[1024,128]{1,0:T(8,128)S(1)} %bitcast.8), custom_call_target="tpu_custom_call" | custom-call | flops 1 | bytes 1 | tf_op jit(solution)/shard_map/pack/pallas_call | solution.py:69
  2.0 0.5 %collective-permute-start = (f32[16,32,128]{2,1,0:T(8,128)S(1)}, f32[16,32,128]{2,1,0:T(8,128)S(1)}, u32[]{:S(2)}, u32[]{:S(2)}) collective-permute-start(f32[16,32,128]{2,1,0:T(8,128)S(1)} %get-tuple-element.30.refs_5_), channel_id=1, source_target_pairs={{1,0},{0,1},{3,2},{2,3},{5,4},{4,5},{7,6},{6,7},{9,8},{8,9},{11,10... | collective-permute-start | bytes 786440 | tf_op jit(solution)/shard_map/ppermute | solution.py:520
  2.5 2.6 %collective-permute-start.3 = (f32[4,32,128]{2,1,0:T(8,128)S(1)}, f32[4,32,128]{2,1,0:T(8,128)S(1)}, u32[]{:S(2)}, u32[]{:S(2)}) collective-permute-start(f32[4,32,128]{2,1,0:T(8,128)S(1)} %get-tuple-element.37), channel_id=1, source_target_pairs={{2,0},{3,1},{0,2},{1,3},{6,4},{7,5},{4,6},{5,7},{10,8},{11,9},{8,1... | collective-permute-start | bytes 196616 | tf_op jit(solution)/shard_map/ppermute | solution.py:520
  5.1 0.1 collective-permute-start.4
  5.2 1.7 %collective-permute-start.5 = (f32[9,32,128]{2,1,0:T(8,128)S(1)}, f32[9,32,128]{2,1,0:T(8,128)S(1)}, u32[]{:S(2)}, u32[]{:S(2)}) collective-permute-start(f32[9,32,128]{2,1,0:T(8,128)S(1)} %get-tuple-element.39), channel_id=1, source_target_pairs={{2,0},{3,1},{0,2},{1,3},{6,4},{7,5},{4,6},{5,7},{10,8},{11,9},{8,1... | collective-permute-start | bytes 442376 | tf_op jit(solution)/shard_map/ppermute | solution.py:520
  6.9 2.1 %prepare.1 = (bf16[16,256,384]{2,1,0:T(8,128)(2,1)S(1)}, f32[8,128]{1,0:T(8,128)S(1)}) custom-call(f32[32,3,128,128]{3,2,1,0:T(8,128)} %w_ref.1), custom_call_target="tpu_custom_call" | custom-call | flops 1 | bytes 1 | tf_op jit(solution)/shard_map/prepare/pallas_call | solution.py:114
  9.1 0.1 collective-permute-done.4.refs_3_
  9.2 0.1 broadcast_in_dim.12.count_ref.refs_9_.refs_7_
  9.2 0.3 edge.1
  9.5 0.6 %collective-permute-start.7 = (f32[272,128]{1,0:T(8,128)S(1)}, f32[272,128]{1,0:T(8,128)S(1)}, u32[]{:S(2)}, u32[]{:S(2)}) collective-permute-start(f32[272,128]{1,0:T(8,128)S(1)} %get-tuple-element.41), channel_id=1, source_target_pairs={{1,0},{0,1},{3,2},{2,3},{5,4},{4,5},{7,6},{6,7},{9,8},{8,9},{11,10... | collective-permute-start | bytes 417800 | tf_op jit(solution)/shard_map/ppermute | solution.py:520
  10.1 0.7 %collective-permute-start.8 = (f32[264,128]{1,0:T(8,128)S(1)}, f32[264,128]{1,0:T(8,128)S(1)}, u32[]{:S(2)}, u32[]{:S(2)}) collective-permute-start(f32[264,128]{1,0:T(8,128)S(1)} %get-tuple-element.47), channel_id=1, source_target_pairs={{1,4},{4,1},{5,8},{8,5},{9,12},{12,9},{3,6},{6,3},{7,10},{10,7},{1... | collective-permute-start | bytes 405512 | tf_op jit(solution)/shard_map/ppermute | solution.py:528
  10.7 1.6 %collective-permute-start.1 = (f32[3,32,128]{2,1,0:T(8,128)S(1)}, f32[3,32,128]{2,1,0:T(8,128)S(1)}, u32[]{:S(2)}, u32[]{:S(2)}) collective-permute-start(f32[3,32,128]{2,1,0:T(8,128)S(1)} %get-tuple-element.31), channel_id=1, source_target_pairs={{2,0},{3,1},{0,2},{1,3},{6,4},{7,5},{4,6},{5,7},{10,8},{11,9},{8,1... | collective-permute-start | bytes 147464 | tf_op jit(solution)/shard_map/ppermute | solution.py:520
  12.4 0.6 %collective-permute-done.5.refs_4_ = f32[9,32,128]{2,1,0:T(8,128)S(1)} collective-permute-done((f32[9,32,128]{2,1,0:T(8,128)S(1)}, f32[9,32,128]{2,1,0:T(8,128)S(1)}, u32[]{:S(2)}, u32[]{:S(2)}) %collective-permute-start.5) | collective-permute-done | bytes 147488 | tf_op jit(solution)/shard_map/ppermute | solution.py:520
  13.0 2.2 %collective-permute-start.2 = (f32[3,32,128]{2,1,0:T(8,128)S(1)}, f32[3,32,128]{2,1,0:T(8,128)S(1)}, u32[]{:S(2)}, u32[]{:S(2)}) collective-permute-start(f32[3,32,128]{2,1,0:T(8,128)S(1)} %get-tuple-element.32), channel_id=1, source_target_pairs={{3,0},{2,1},{1,2},{0,3},{7,4},{6,5},{5,6},{4,7},{11,8},{10,9},{9,1... | collective-permute-start | bytes 147464 | tf_op jit(solution)/shard_map/ppermute | solution.py:520
  15.2 0.2 mixer.1
  15.4 0.1 collective-permute-done.6.refs_5_
  15.5 2.3 %stage.2 = (f32[4,8,128]{2,1,0:T(8,128)S(1)}, f32[19,32,128]{2,1,0:T(8,128)S(1)}, f32[19,32,128]{2,1,0:T(8,128)S(1)}, bf16[4,128,128]{2,1,0:T(8,128)(2,1)S(1)}, ...) custom-call(f32[16,32,128]{2,1,0:T(8,128)S(1)} %get-tuple-element.29.refs_0_.ref, ...), custom_call_target="tpu_custom_call" | custom-call | flops 1 | bytes 1 | tf_op jit(solution)/shard_map/stage/pallas_call | solution.py:417
  17.8 0.0 collective-permute-done.1.refs_2_
  17.8 0.0 collective-permute-done.2.refs_3_
  17.8 1.6 %stage.3 = (f32[4,8,128]{2,1,0:T(8,128)S(1)}, f32[13,32,128]{2,1,0:T(8,128)S(1)}, f32[13,32,128]{2,1,0:T(8,128)S(1)}) custom-call(f32[16,32,128]{2,1,0:T(8,128)S(1)} %get-tuple-element.29.refs_0_.refs_4_, f32[16,32,128]{2,1,0:T(8,128)S(1)} %collective-permute-done.refs_1_, f32[3,32,128]{2,1,0:T(8,128)S(1)} %collective-permute-done.1.refs_2_, ...), custom_call_target="tpu_custom_call" | custom-call | flops 1 | bytes 1 | tf_op jit(solution)/shard_map/stage/pallas_call | solution.py:417
  19.4 0.8 %collective-permute-start.12 = (f32[19,32,128]{2,1,0:T(8,128)S(1)}, f32[19,32,128]{2,1,0:T(8,128)S(1)}, u32[]{:S(2)}, u32[]{:S(2)}) collective-permute-start(f32[19,32,128]{2,1,0:T(8,128)S(1)} %get-tuple-element.52), channel_id=1, source_target_pairs={{1,0},{0,1},{3,2},{2,3},{5,4},{4,5},{7,6},{6,7},{9,8},{8,9},{11,10... | collective-permute-start | bytes 933896 | tf_op jit(solution)/shard_map/ppermute | solution.py:520
  20.2 1.3 %collective-permute-start.9 = (f32[1,8,128]{2,1,0:T(8,128)S(1)}, f32[1,8,128]{2,1,0:T(8,128)S(1)}, u32[]{:S(2)}, u32[]{:S(2)}) collective-permute-start(f32[1,8,128]{2,1,0:T(8,128)S(1)} %maximum_bitcast_fusion.refs_0_), channel_id=1, source_target_pairs={{0,5},{1,4},{4,1},{5,0},{8,13},{9,12},{12,9},{13,8},{2,7},{3,6},{6... | collective-permute-start | bytes 12296 | tf_op jit(solution)/shard_map/ppermute | solution.py:545
  21.5 0.4 %collective-permute-start.13 = (f32[13,32,128]{2,1,0:T(8,128)S(1)}, f32[13,32,128]{2,1,0:T(8,128)S(1)}, u32[]{:S(2)}, u32[]{:S(2)}) collective-permute-start(f32[13,32,128]{2,1,0:T(8,128)S(1)} %get-tuple-element.53), channel_id=1, source_target_pairs={{1,0},{0,1},{3,2},{2,3},{5,4},{4,5},{7,6},{6,7},{9,8},{8,9},{11,10... | collective-permute-start | bytes 638984 | tf_op jit(solution)/shard_map/ppermute | solution.py:520
  21.9 1.3 %collective-permute-done.9.refs_1_ = f32[1,8,128]{2,1,0:T(8,128)S(1)} collective-permute-done((f32[1,8,128]{2,1,0:T(8,128)S(1)}, f32[1,8,128]{2,1,0:T(8,128)S(1)}, u32[]{:S(2)}, u32[]{:S(2)}) %collective-permute-start.9) | collective-permute-done | bytes 4128 | tf_op jit(solution)/shard_map/ppermute | solution.py:545
  23.2 2.3 %collective-permute-start.10 = (f32[2,8,128]{2,1,0:T(8,128)S(1)}, f32[2,8,128]{2,1,0:T(8,128)S(1)}, u32[]{:S(2)}, u32[]{:S(2)}) collective-permute-start(f32[2,8,128]{2,1,0:T(8,128)S(1)} %pad_maximum_fusion.1), channel_id=1, source_target_pairs={{0,9},{1,8},{4,13},{5,12},{8,1},{9,0},{12,5},{13,4},{2,11},{3,10},... | collective-permute-start | bytes 24584 | tf_op jit(solution)/shard_map/ppermute | solution.py:545
  25.5 1.7 %collective-permute-done.10.refs_2_ = f32[2,8,128]{2,1,0:T(8,128)S(1)} collective-permute-done((f32[2,8,128]{2,1,0:T(8,128)S(1)}, f32[2,8,128]{2,1,0:T(8,128)S(1)}, u32[]{:S(2)}, u32[]{:S(2)}) %collective-permute-start.10) | collective-permute-done | bytes 8224 | tf_op jit(solution)/shard_map/ppermute | solution.py:545
  27.2 0.1 collective-permute-start.11
  27.3 1.1 %collective-permute-done.11.refs_3_ = f32[4,8,128]{2,1,0:T(8,128)S(1)} collective-permute-done((f32[4,8,128]{2,1,0:T(8,128)S(1)}, f32[4,8,128]{2,1,0:T(8,128)S(1)}, u32[]{:S(2)}, u32[]{:S(2)}) %collective-permute-start.11) | collective-permute-done | bytes 16416 | tf_op jit(solution)/shard_map/ppermute | solution.py:520
  28.4 0.0 collective-permute-done.13.refs_9_
  28.4 0.0 collective-permute-done.12.refs_8_
  28.4 1.7 %finish.1 = (f32[32,32,1,128]{3,2,1,0:T(1,128)}, f32[32,32,1,128]{3,2,1,0:T(1,128)}) custom-call(f32[1,8,128]{2,1,0:T(8,128)S(1)} %maximum_bitcast_fusion.refs_0_, f32[1,8,128]{2,1,0:T(8,128)S(1)} %collective-permute-done.9.refs_1_, f32[2,8,128]{2,1,0:T(8,128)S(1)} %collective-permute-done.10.refs_2_, f32[4,8,128]{2,1,0:T(8,128)S(1)} %collective-permute-done.11.refs_3_, ...), custom_call_target="tpu_custom_call" | custom-call | flops 1 | bytes 1 | tf_op jit(solution)/shard_map/finish/pallas_call | solution.py:500
  (17 shorter events, 0.1 us)
Async XLA Ops:
  0.6 8.4 %copy-start.2 = (s32[32]{0:T(128)S(1)}, s32[32]{0:T(128)}, u32[]{:S(2)}) copy-start(s32[32]{0:T(128)} %param.7) | copy-start | bytes 388
  0.6 1.0 %copy-start = (f32[32,1,4096]{2,1,0:T(1,128)S(1)}, f32[32,1,4096]{2,1,0:T(1,128)}, u32[]{:S(2)}) copy-start(f32[32,1,4096]{2,1,0:T(1,128)} %param.5) | copy-start | bytes 1572868
  1.7 13.5 %copy-start.1 = (f32[64,2,64,2]{2,3,1,0:T(2,128)S(1)}, f32[64,2,64,2]{2,3,1,0:T(2,128)}, u32[]{:S(2)}) copy-start(f32[64,2,64,2]{2,3,1,0:T(2,128)} %param.8) | copy-start | bytes 196612
  2.0 7.1 %collective-permute-start = (f32[16,32,128]{2,1,0:T(8,128)S(1)}, f32[16,32,128]{2,1,0:T(8,128)S(1)}, u32[]{:S(2)}, u32[]{:S(2)}) collective-permute-start(f32[16,32,128]{2,1,0:T(8,128)S(1)} %get-tuple-element.30.refs_5_), channel_id=1, source_target_pairs={{1,0},{0,1},{3,2},{2,3},{5,4},{4,5},{7,6},{6,7},{9,8},{8,9},{11,10... | collective-permute-start | bytes 786440 | tf_op jit(solution)/shard_map/ppermute | solution.py:520
  2.5 6.5 %collective-permute-start.3 = (f32[4,32,128]{2,1,0:T(8,128)S(1)}, f32[4,32,128]{2,1,0:T(8,128)S(1)}, u32[]{:S(2)}, u32[]{:S(2)}) collective-permute-start(f32[4,32,128]{2,1,0:T(8,128)S(1)} %get-tuple-element.37), channel_id=1, source_target_pairs={{2,0},{3,1},{0,2},{1,3},{6,4},{7,5},{4,6},{5,7},{10,8},{11,9},{8,1... | collective-permute-start | bytes 196616 | tf_op jit(solution)/shard_map/ppermute | solution.py:520
  5.1 4.0 %collective-permute-start.4 = (f32[4,32,128]{2,1,0:T(8,128)S(1)}, f32[4,32,128]{2,1,0:T(8,128)S(1)}, u32[]{:S(2)}, u32[]{:S(2)}) collective-permute-start(f32[4,32,128]{2,1,0:T(8,128)S(1)} %get-tuple-element.38), channel_id=1, source_target_pairs={{3,0},{2,1},{1,2},{0,3},{7,4},{6,5},{5,6},{4,7},{11,8},{10,9},{9,1... | collective-permute-start | bytes 196616 | tf_op jit(solution)/shard_map/ppermute | solution.py:520
  5.2 7.8 %collective-permute-start.5 = (f32[9,32,128]{2,1,0:T(8,128)S(1)}, f32[9,32,128]{2,1,0:T(8,128)S(1)}, u32[]{:S(2)}, u32[]{:S(2)}) collective-permute-start(f32[9,32,128]{2,1,0:T(8,128)S(1)} %get-tuple-element.39), channel_id=1, source_target_pairs={{2,0},{3,1},{0,2},{1,3},{6,4},{7,5},{4,6},{5,7},{10,8},{11,9},{8,1... | collective-permute-start | bytes 442376 | tf_op jit(solution)/shard_map/ppermute | solution.py:520
  6.9 8.6 %collective-permute-start.6 = (f32[9,32,128]{2,1,0:T(8,128)S(1)}, f32[9,32,128]{2,1,0:T(8,128)S(1)}, u32[]{:S(2)}, u32[]{:S(2)}) collective-permute-start(f32[9,32,128]{2,1,0:T(8,128)S(1)} %get-tuple-element.40), channel_id=1, source_target_pairs={{3,0},{2,1},{1,2},{0,3},{7,4},{6,5},{5,6},{4,7},{11,8},{10,9},{9,1... | collective-permute-start | bytes 442376 | tf_op jit(solution)/shard_map/ppermute | solution.py:520
  9.5 6.0 %collective-permute-start.7 = (f32[272,128]{1,0:T(8,128)S(1)}, f32[272,128]{1,0:T(8,128)S(1)}, u32[]{:S(2)}, u32[]{:S(2)}) collective-permute-start(f32[272,128]{1,0:T(8,128)S(1)} %get-tuple-element.41), channel_id=1, source_target_pairs={{1,0},{0,1},{3,2},{2,3},{5,4},{4,5},{7,6},{6,7},{9,8},{8,9},{11,10... | collective-permute-start | bytes 417800 | tf_op jit(solution)/shard_map/ppermute | solution.py:520
  10.1 7.7 %collective-permute-start.8 = (f32[264,128]{1,0:T(8,128)S(1)}, f32[264,128]{1,0:T(8,128)S(1)}, u32[]{:S(2)}, u32[]{:S(2)}) collective-permute-start(f32[264,128]{1,0:T(8,128)S(1)} %get-tuple-element.47), channel_id=1, source_target_pairs={{1,4},{4,1},{5,8},{8,5},{9,12},{12,9},{3,6},{6,3},{7,10},{10,7},{1... | collective-permute-start | bytes 405512 | tf_op jit(solution)/shard_map/ppermute | solution.py:528
  10.7 7.0 %collective-permute-start.1 = (f32[3,32,128]{2,1,0:T(8,128)S(1)}, f32[3,32,128]{2,1,0:T(8,128)S(1)}, u32[]{:S(2)}, u32[]{:S(2)}) collective-permute-start(f32[3,32,128]{2,1,0:T(8,128)S(1)} %get-tuple-element.31), channel_id=1, source_target_pairs={{2,0},{3,1},{0,2},{1,3},{6,4},{7,5},{4,6},{5,7},{10,8},{11,9},{8,1... | collective-permute-start | bytes 147464 | tf_op jit(solution)/shard_map/ppermute | solution.py:520
  13.0 4.8 %collective-permute-start.2 = (f32[3,32,128]{2,1,0:T(8,128)S(1)}, f32[3,32,128]{2,1,0:T(8,128)S(1)}, u32[]{:S(2)}, u32[]{:S(2)}) collective-permute-start(f32[3,32,128]{2,1,0:T(8,128)S(1)} %get-tuple-element.32), channel_id=1, source_target_pairs={{3,0},{2,1},{1,2},{0,3},{7,4},{6,5},{5,6},{4,7},{11,8},{10,9},{9,1... | collective-permute-start | bytes 147464 | tf_op jit(solution)/shard_map/ppermute | solution.py:520
  19.4 9.0 %collective-permute-start.12 = (f32[19,32,128]{2,1,0:T(8,128)S(1)}, f32[19,32,128]{2,1,0:T(8,128)S(1)}, u32[]{:S(2)}, u32[]{:S(2)}) collective-permute-start(f32[19,32,128]{2,1,0:T(8,128)S(1)} %get-tuple-element.52), channel_id=1, source_target_pairs={{1,0},{0,1},{3,2},{2,3},{5,4},{4,5},{7,6},{6,7},{9,8},{8,9},{11,10... | collective-permute-start | bytes 933896 | tf_op jit(solution)/shard_map/ppermute | solution.py:520
  20.2 3.0 %collective-permute-start.9 = (f32[1,8,128]{2,1,0:T(8,128)S(1)}, f32[1,8,128]{2,1,0:T(8,128)S(1)}, u32[]{:S(2)}, u32[]{:S(2)}) collective-permute-start(f32[1,8,128]{2,1,0:T(8,128)S(1)} %maximum_bitcast_fusion.refs_0_), channel_id=1, source_target_pairs={{0,5},{1,4},{4,1},{5,0},{8,13},{9,12},{12,9},{13,8},{2,7},{3,6},{6... | collective-permute-start | bytes 12296 | tf_op jit(solution)/shard_map/ppermute | solution.py:545
  21.5 6.9 %collective-permute-start.13 = (f32[13,32,128]{2,1,0:T(8,128)S(1)}, f32[13,32,128]{2,1,0:T(8,128)S(1)}, u32[]{:S(2)}, u32[]{:S(2)}) collective-permute-start(f32[13,32,128]{2,1,0:T(8,128)S(1)} %get-tuple-element.53), channel_id=1, source_target_pairs={{1,0},{0,1},{3,2},{2,3},{5,4},{4,5},{7,6},{6,7},{9,8},{8,9},{11,10... | collective-permute-start | bytes 638984 | tf_op jit(solution)/shard_map/ppermute | solution.py:520
  23.2 4.0 %collective-permute-start.10 = (f32[2,8,128]{2,1,0:T(8,128)S(1)}, f32[2,8,128]{2,1,0:T(8,128)S(1)}, u32[]{:S(2)}, u32[]{:S(2)}) collective-permute-start(f32[2,8,128]{2,1,0:T(8,128)S(1)} %pad_maximum_fusion.1), channel_id=1, source_target_pairs={{0,9},{1,8},{4,13},{5,12},{8,1},{9,0},{12,5},{13,4},{2,11},{3,10},... | collective-permute-start | bytes 24584 | tf_op jit(solution)/shard_map/ppermute | solution.py:545
  27.2 1.2 %collective-permute-start.11 = (f32[4,8,128]{2,1,0:T(8,128)S(1)}, f32[4,8,128]{2,1,0:T(8,128)S(1)}, u32[]{:S(2)}, u32[]{:S(2)}) collective-permute-start(f32[4,8,128]{2,1,0:T(8,128)S(1)} %pad_maximum_fusion), channel_id=1, source_target_pairs={{1,0},{0,1},{3,2},{2,3},{5,4},{4,5},{7,6},{6,7},{9,8},{8,9},{11,10... | collective-permute-start | bytes 49160 | tf_op jit(solution)/shard_map/ppermute | solution.py:520

commit v8 on v7

--- a/solution.py
+++ b/solution.py
@@ -454,11 +454,13 @@
     alpha = m0 / first
     lead = alpha * scale
     mean = m1 / m0
-    fresh = lead * lead * (m2 - mean * m1)
-    c = lead * mean + fresh / m0
-    dd = c * c * m0 - 2.0 * c * lead * m1 + lead * lead * m2
+    fresh = lead * lead * jnp.maximum(m2 - mean * m1, 0.0)
+    beta = fresh / m0
+    c = lead * mean + beta
+    dd = fresh + beta * fresh
     dkd = c * c * m1 - 2.0 * c * lead * m2 + lead * lead * m3
-    alpha_2 = fresh / (NUGGET * dd + scale * dkd)
+    below = NUGGET * dd + scale * dkd
+    alpha_2 = jnp.where(below == 0.0, 0.0, fresh / jnp.where(below == 0.0, 1.0, below))
     x_0 = alpha + alpha_2 * c
     r_0 = lead * mean - NUGGET * alpha_2 * c
     x_1 = -alpha_2 * lead

time: 30.3 us -> 30.3 us (level)
  no operation moved by 1% of the time
where the time goes in v8:
time: 30.3 us; the launch traced here: 30.1 us
  starting transfers between devices  14.8 us (49%)
  Pallas kernels  8.42 us (28%)
  waiting for transfers between devices  4.92 us (16%)
  local copies, waits for them, and re-layouts  1.12 us (4%)
  between operations  0.76 us (3%)
    ppermute x11, starting transfers between devices, from_group(): return lax.ppermute(value, ('season', 'var'), pairs)  10.6 us
    pallas_call x2, Pallas kernels, run_stage(): pl.pallas_call(kernel, in_specs=[pl.BlockSpec(memory_space=VMEM)] * len(o...  3.85 us
    ppermute x2, starting transfers between devices, gather_tiles(): found.append(lax.ppermute(have, ('space', 'var'), pairs))  3.58 us
    ppermute x2, waiting for transfers between devices, gather_tiles(): found.append(lax.ppermute(have, ('space', 'var'), pairs))  3.01 us
    pallas_call x1, Pallas kernels, prepare(): pl.pallas_call(functools.partial(prepare_kernel, blocks), in_specs=[pl.Bl...  2.1 us
    ppermute x11, waiting for transfers between devices, from_group(): return lax.ppermute(value, ('season', 'var'), pairs)  1.91 us
    pallas_call x1, Pallas kernels, finish(): pl.pallas_call(functools.partial(finish_kernel, plan, blocks, len(gathere...  1.69 us
    unnamed x6, local copies, waits for them, and re-layouts  1.05 us
  transfers between devices with their start and end apart: 14, of which 6 were waited for; matrix products, arithmetic and copies ran while one was open for 0% of the time, Pallas kernels for 16%

profile of v8, /device:TPU:0, one launch (start us, length us, event | category | flops | bytes accessed | tf_op | source)
XLA Modules:
  0.0 30.1 jit_solution(2076650934959358015)
XLA Ops:
  0.6 1.0 %copy-done = f32[32,1,4096]{2,1,0:T(1,128)S(1)} copy-done((f32[32,1,4096]{2,1,0:T(1,128)S(1)}, f32[32,1,4096]{2,1,0:T(1,128)}, u32[]{:S(2)}) %copy-start) | copy-done | bytes 524312
  1.7 0.3 %pack.1 = (f32[16,32,128]{2,1,0:T(8,128)S(1)}, f32[16,32,128]{2,1,0:T(8,128)S(1)}, f32[4,32,128]{2,1,0:T(8,128)S(1)}, f32[4,32,128]{2,1,0:T(8,128)S(1)}, f32[9,3...) custom-call(f32[1024,128]{1,0:T(8,128)S(1)} %bitcast.8), custom_call_target="tpu_custom_call" | custom-call | flops 1 | bytes 1 | tf_op jit(solution)/shard_map/pack/pallas_call | solution.py:69
  2.0 0.5 %collective-permute-start = (f32[16,32,128]{2,1,0:T(8,128)S(1)}, f32[16,32,128]{2,1,0:T(8,128)S(1)}, u32[]{:S(2)}, u32[]{:S(2)}) collective-permute-start(f32[16,32,128]{2,1,0:T(8,128)S(1)} %get-tuple-element.30.refs_5_), channel_id=1, source_target_pairs={{1,0},{0,1},{3,2},{2,3},{5,4},{4,5},{7,6},{6,7},{9,8},{8,9},{11,10... | collective-permute-start | bytes 786440 | tf_op jit(solution)/shard_map/ppermute | solution.py:522
  2.5 2.6 %collective-permute-start.3 = (f32[4,32,128]{2,1,0:T(8,128)S(1)}, f32[4,32,128]{2,1,0:T(8,128)S(1)}, u32[]{:S(2)}, u32[]{:S(2)}) collective-permute-start(f32[4,32,128]{2,1,0:T(8,128)S(1)} %get-tuple-element.37), channel_id=1, source_target_pairs={{2,0},{3,1},{0,2},{1,3},{6,4},{7,5},{4,6},{5,7},{10,8},{11,9},{8,1... | collective-permute-start | bytes 196616 | tf_op jit(solution)/shard_map/ppermute | solution.py:522
  5.1 0.1 collective-permute-start.4
  5.2 1.7 %collective-permute-start.5 = (f32[9,32,128]{2,1,0:T(8,128)S(1)}, f32[9,32,128]{2,1,0:T(8,128)S(1)}, u32[]{:S(2)}, u32[]{:S(2)}) collective-permute-start(f32[9,32,128]{2,1,0:T(8,128)S(1)} %get-tuple-element.39), channel_id=1, source_target_pairs={{2,0},{3,1},{0,2},{1,3},{6,4},{7,5},{4,6},{5,7},{10,8},{11,9},{8,1... | collective-permute-start | bytes 442376 | tf_op jit(solution)/shard_map/ppermute | solution.py:522
  6.9 2.1 %prepare.1 = (bf16[16,256,384]{2,1,0:T(8,128)(2,1)S(1)}, f32[8,128]{1,0:T(8,128)S(1)}) custom-call(f32[32,3,128,128]{3,2,1,0:T(8,128)} %w_ref.1), custom_call_target="tpu_custom_call" | custom-call | flops 1 | bytes 1 | tf_op jit(solution)/shard_map/prepare/pallas_call | solution.py:114
  9.1 0.1 collective-permute-done.4.refs_3_
  9.2 0.1 broadcast_in_dim.12.count_ref.refs_9_.refs_7_
  9.2 0.3 edge.1
  9.5 0.6 %collective-permute-start.7 = (f32[272,128]{1,0:T(8,128)S(1)}, f32[272,128]{1,0:T(8,128)S(1)}, u32[]{:S(2)}, u32[]{:S(2)}) collective-permute-start(f32[272,128]{1,0:T(8,128)S(1)} %get-tuple-element.41), channel_id=1, source_target_pairs={{1,0},{0,1},{3,2},{2,3},{5,4},{4,5},{7,6},{6,7},{9,8},{8,9},{11,10... | collective-permute-start | bytes 417800 | tf_op jit(solution)/shard_map/ppermute | solution.py:522
  10.1 0.7 %collective-permute-start.8 = (f32[264,128]{1,0:T(8,128)S(1)}, f32[264,128]{1,0:T(8,128)S(1)}, u32[]{:S(2)}, u32[]{:S(2)}) collective-permute-start(f32[264,128]{1,0:T(8,128)S(1)} %get-tuple-element.47), channel_id=1, source_target_pairs={{1,4},{4,1},{5,8},{8,5},{9,12},{12,9},{3,6},{6,3},{7,10},{10,7},{1... | collective-permute-start | bytes 405512 | tf_op jit(solution)/shard_map/ppermute | solution.py:530
  10.7 1.6 %collective-permute-start.1 = (f32[3,32,128]{2,1,0:T(8,128)S(1)}, f32[3,32,128]{2,1,0:T(8,128)S(1)}, u32[]{:S(2)}, u32[]{:S(2)}) collective-permute-start(f32[3,32,128]{2,1,0:T(8,128)S(1)} %get-tuple-element.31), channel_id=1, source_target_pairs={{2,0},{3,1},{0,2},{1,3},{6,4},{7,5},{4,6},{5,7},{10,8},{11,9},{8,1... | collective-permute-start | bytes 147464 | tf_op jit(solution)/shard_map/ppermute | solution.py:522
  12.4 0.6 %collective-permute-done.5.refs_4_ = f32[9,32,128]{2,1,0:T(8,128)S(1)} collective-permute-done((f32[9,32,128]{2,1,0:T(8,128)S(1)}, f32[9,32,128]{2,1,0:T(8,128)S(1)}, u32[]{:S(2)}, u32[]{:S(2)}) %collective-permute-start.5) | collective-permute-done | bytes 147488 | tf_op jit(solution)/shard_map/ppermute | solution.py:522
  13.0 2.2 %collective-permute-start.2 = (f32[3,32,128]{2,1,0:T(8,128)S(1)}, f32[3,32,128]{2,1,0:T(8,128)S(1)}, u32[]{:S(2)}, u32[]{:S(2)}) collective-permute-start(f32[3,32,128]{2,1,0:T(8,128)S(1)} %get-tuple-element.32), channel_id=1, source_target_pairs={{3,0},{2,1},{1,2},{0,3},{7,4},{6,5},{5,6},{4,7},{11,8},{10,9},{9,1... | collective-permute-start | bytes 147464 | tf_op jit(solution)/shard_map/ppermute | solution.py:522
  15.2 0.2 mixer.1
  15.4 0.1 collective-permute-done.6.refs_5_
  15.5 2.3 %stage.2 = (f32[4,8,128]{2,1,0:T(8,128)S(1)}, f32[19,32,128]{2,1,0:T(8,128)S(1)}, f32[19,32,128]{2,1,0:T(8,128)S(1)}, bf16[4,128,128]{2,1,0:T(8,128)(2,1)S(1)}, ...) custom-call(f32[16,32,128]{2,1,0:T(8,128)S(1)} %get-tuple-element.29.refs_0_.ref, ...), custom_call_target="tpu_custom_call" | custom-call | flops 1 | bytes 1 | tf_op jit(solution)/shard_map/stage/pallas_call | solution.py:417
  17.8 0.0 collective-permute-done.1.refs_2_
  17.8 0.0 collective-permute-done.2.refs_3_
  17.8 1.6 %stage.3 = (f32[4,8,128]{2,1,0:T(8,128)S(1)}, f32[13,32,128]{2,1,0:T(8,128)S(1)}, f32[13,32,128]{2,1,0:T(8,128)S(1)}) custom-call(f32[16,32,128]{2,1,0:T(8,128)S(1)} %get-tuple-element.29.refs_0_.refs_4_, f32[16,32,128]{2,1,0:T(8,128)S(1)} %collective-permute-done.refs_1_, f32[3,32,128]{2,1,0:T(8,128)S(1)} %collective-permute-done.1.refs_2_, ...), custom_call_target="tpu_custom_call" | custom-call | flops 1 | bytes 1 | tf_op jit(solution)/shard_map/stage/pallas_call | solution.py:417
  19.4 0.8 %collective-permute-start.12 = (f32[19,32,128]{2,1,0:T(8,128)S(1)}, f32[19,32,128]{2,1,0:T(8,128)S(1)}, u32[]{:S(2)}, u32[]{:S(2)}) collective-permute-start(f32[19,32,128]{2,1,0:T(8,128)S(1)} %get-tuple-element.52), channel_id=1, source_target_pairs={{1,0},{0,1},{3,2},{2,3},{5,4},{4,5},{7,6},{6,7},{9,8},{8,9},{11,10... | collective-permute-start | bytes 933896 | tf_op jit(solution)/shard_map/ppermute | solution.py:522
  20.2 1.3 %collective-permute-start.9 = (f32[1,8,128]{2,1,0:T(8,128)S(1)}, f32[1,8,128]{2,1,0:T(8,128)S(1)}, u32[]{:S(2)}, u32[]{:S(2)}) collective-permute-start(f32[1,8,128]{2,1,0:T(8,128)S(1)} %maximum_bitcast_fusion.refs_0_), channel_id=1, source_target_pairs={{0,5},{1,4},{4,1},{5,0},{8,13},{9,12},{12,9},{13,8},{2,7},{3,6},{6... | collective-permute-start | bytes 12296 | tf_op jit(solution)/shard_map/ppermute | solution.py:547
  21.5 0.4 %collective-permute-start.13 = (f32[13,32,128]{2,1,0:T(8,128)S(1)}, f32[13,32,128]{2,1,0:T(8,128)S(1)}, u32[]{:S(2)}, u32[]{:S(2)}) collective-permute-start(f32[13,32,128]{2,1,0:T(8,128)S(1)} %get-tuple-element.53), channel_id=1, source_target_pairs={{1,0},{0,1},{3,2},{2,3},{5,4},{4,5},{7,6},{6,7},{9,8},{8,9},{11,10... | collective-permute-start | bytes 638984 | tf_op jit(solution)/shard_map/ppermute | solution.py:522
  21.9 1.3 %collective-permute-done.9.refs_1_ = f32[1,8,128]{2,1,0:T(8,128)S(1)} collective-permute-done((f32[1,8,128]{2,1,0:T(8,128)S(1)}, f32[1,8,128]{2,1,0:T(8,128)S(1)}, u32[]{:S(2)}, u32[]{:S(2)}) %collective-permute-start.9) | collective-permute-done | bytes 4128 | tf_op jit(solution)/shard_map/ppermute | solution.py:547
  23.2 2.3 %collective-permute-start.10 = (f32[2,8,128]{2,1,0:T(8,128)S(1)}, f32[2,8,128]{2,1,0:T(8,128)S(1)}, u32[]{:S(2)}, u32[]{:S(2)}) collective-permute-start(f32[2,8,128]{2,1,0:T(8,128)S(1)} %pad_maximum_fusion.1), channel_id=1, source_target_pairs={{0,9},{1,8},{4,13},{5,12},{8,1},{9,0},{12,5},{13,4},{2,11},{3,10},... | collective-permute-start | bytes 24584 | tf_op jit(solution)/shard_map/ppermute | solution.py:547
  25.5 1.7 %collective-permute-done.10.refs_2_ = f32[2,8,128]{2,1,0:T(8,128)S(1)} collective-permute-done((f32[2,8,128]{2,1,0:T(8,128)S(1)}, f32[2,8,128]{2,1,0:T(8,128)S(1)}, u32[]{:S(2)}, u32[]{:S(2)}) %collective-permute-start.10) | collective-permute-done | bytes 8224 | tf_op jit(solution)/shard_map/ppermute | solution.py:547
  27.2 0.1 collective-permute-start.11
  27.3 1.1 %collective-permute-done.11.refs_3_ = f32[4,8,128]{2,1,0:T(8,128)S(1)} collective-permute-done((f32[4,8,128]{2,1,0:T(8,128)S(1)}, f32[4,8,128]{2,1,0:T(8,128)S(1)}, u32[]{:S(2)}, u32[]{:S(2)}) %collective-permute-start.11) | collective-permute-done | bytes 16416 | tf_op jit(solution)/shard_map/ppermute | solution.py:522
  28.4 0.0 collective-permute-done.13.refs_9_
  28.4 0.0 collective-permute-done.12.refs_8_
  28.4 1.7 %finish.1 = (f32[32,32,1,128]{3,2,1,0:T(1,128)}, f32[32,32,1,128]{3,2,1,0:T(1,128)}) custom-call(f32[1,8,128]{2,1,0:T(8,128)S(1)} %maximum_bitcast_fusion.refs_0_, f32[1,8,128]{2,1,0:T(8,128)S(1)} %collective-permute-done.9.refs_1_, f32[2,8,128]{2,1,0:T(8,128)S(1)} %collective-permute-done.10.refs_2_, f32[4,8,128]{2,1,0:T(8,128)S(1)} %collective-permute-done.11.refs_3_, ...), custom_call_target="tpu_custom_call" | custom-call | flops 1 | bytes 1 | tf_op jit(solution)/shard_map/finish/pallas_call | solution.py:502
  (17 shorter events, 0.1 us)
Async XLA Ops:
  0.6 8.4 %copy-start.2 = (s32[32]{0:T(128)S(1)}, s32[32]{0:T(128)}, u32[]{:S(2)}) copy-start(s32[32]{0:T(128)} %param.7) | copy-start | bytes 388
  0.6 1.0 %copy-start = (f32[32,1,4096]{2,1,0:T(1,128)S(1)}, f32[32,1,4096]{2,1,0:T(1,128)}, u32[]{:S(2)}) copy-start(f32[32,1,4096]{2,1,0:T(1,128)} %param.5) | copy-start | bytes 1572868
  1.7 13.5 %copy-start.1 = (f32[64,2,64,2]{2,3,1,0:T(2,128)S(1)}, f32[64,2,64,2]{2,3,1,0:T(2,128)}, u32[]{:S(2)}) copy-start(f32[64,2,64,2]{2,3,1,0:T(2,128)} %param.8) | copy-start | bytes 196612
  2.0 7.1 %collective-permute-start = (f32[16,32,128]{2,1,0:T(8,128)S(1)}, f32[16,32,128]{2,1,0:T(8,128)S(1)}, u32[]{:S(2)}, u32[]{:S(2)}) collective-permute-start(f32[16,32,128]{2,1,0:T(8,128)S(1)} %get-tuple-element.30.refs_5_), channel_id=1, source_target_pairs={{1,0},{0,1},{3,2},{2,3},{5,4},{4,5},{7,6},{6,7},{9,8},{8,9},{11,10... | collective-permute-start | bytes 786440 | tf_op jit(solution)/shard_map/ppermute | solution.py:522
  2.5 6.5 %collective-permute-start.3 = (f32[4,32,128]{2,1,0:T(8,128)S(1)}, f32[4,32,128]{2,1,0:T(8,128)S(1)}, u32[]{:S(2)}, u32[]{:S(2)}) collective-permute-start(f32[4,32,128]{2,1,0:T(8,128)S(1)} %get-tuple-element.37), channel_id=1, source_target_pairs={{2,0},{3,1},{0,2},{1,3},{6,4},{7,5},{4,6},{5,7},{10,8},{11,9},{8,1... | collective-permute-start | bytes 196616 | tf_op jit(solution)/shard_map/ppermute | solution.py:522
  5.1 4.0 %collective-permute-start.4 = (f32[4,32,128]{2,1,0:T(8,128)S(1)}, f32[4,32,128]{2,1,0:T(8,128)S(1)}, u32[]{:S(2)}, u32[]{:S(2)}) collective-permute-start(f32[4,32,128]{2,1,0:T(8,128)S(1)} %get-tuple-element.38), channel_id=1, source_target_pairs={{3,0},{2,1},{1,2},{0,3},{7,4},{6,5},{5,6},{4,7},{11,8},{10,9},{9,1... | collective-permute-start | bytes 196616 | tf_op jit(solution)/shard_map/ppermute | solution.py:522
  5.2 7.8 %collective-permute-start.5 = (f32[9,32,128]{2,1,0:T(8,128)S(1)}, f32[9,32,128]{2,1,0:T(8,128)S(1)}, u32[]{:S(2)}, u32[]{:S(2)}) collective-permute-start(f32[9,32,128]{2,1,0:T(8,128)S(1)} %get-tuple-element.39), channel_id=1, source_target_pairs={{2,0},{3,1},{0,2},{1,3},{6,4},{7,5},{4,6},{5,7},{10,8},{11,9},{8,1... | collective-permute-start | bytes 442376 | tf_op jit(solution)/shard_map/ppermute | solution.py:522
  6.9 8.6 %collective-permute-start.6 = (f32[9,32,128]{2,1,0:T(8,128)S(1)}, f32[9,32,128]{2,1,0:T(8,128)S(1)}, u32[]{:S(2)}, u32[]{:S(2)}) collective-permute-start(f32[9,32,128]{2,1,0:T(8,128)S(1)} %get-tuple-element.40), channel_id=1, source_target_pairs={{3,0},{2,1},{1,2},{0,3},{7,4},{6,5},{5,6},{4,7},{11,8},{10,9},{9,1... | collective-permute-start | bytes 442376 | tf_op jit(solution)/shard_map/ppermute | solution.py:522
  9.5 6.0 %collective-permute-start.7 = (f32[272,128]{1,0:T(8,128)S(1)}, f32[272,128]{1,0:T(8,128)S(1)}, u32[]{:S(2)}, u32[]{:S(2)}) collective-permute-start(f32[272,128]{1,0:T(8,128)S(1)} %get-tuple-element.41), channel_id=1, source_target_pairs={{1,0},{0,1},{3,2},{2,3},{5,4},{4,5},{7,6},{6,7},{9,8},{8,9},{11,10... | collective-permute-start | bytes 417800 | tf_op jit(solution)/shard_map/ppermute | solution.py:522
  10.1 7.7 %collective-permute-start.8 = (f32[264,128]{1,0:T(8,128)S(1)}, f32[264,128]{1,0:T(8,128)S(1)}, u32[]{:S(2)}, u32[]{:S(2)}) collective-permute-start(f32[264,128]{1,0:T(8,128)S(1)} %get-tuple-element.47), channel_id=1, source_target_pairs={{1,4},{4,1},{5,8},{8,5},{9,12},{12,9},{3,6},{6,3},{7,10},{10,7},{1... | collective-permute-start | bytes 405512 | tf_op jit(solution)/shard_map/ppermute | solution.py:530
  10.7 7.0 %collective-permute-start.1 = (f32[3,32,128]{2,1,0:T(8,128)S(1)}, f32[3,32,128]{2,1,0:T(8,128)S(1)}, u32[]{:S(2)}, u32[]{:S(2)}) collective-permute-start(f32[3,32,128]{2,1,0:T(8,128)S(1)} %get-tuple-element.31), channel_id=1, source_target_pairs={{2,0},{3,1},{0,2},{1,3},{6,4},{7,5},{4,6},{5,7},{10,8},{11,9},{8,1... | collective-permute-start | bytes 147464 | tf_op jit(solution)/shard_map/ppermute | solution.py:522
  13.0 4.8 %collective-permute-start.2 = (f32[3,32,128]{2,1,0:T(8,128)S(1)}, f32[3,32,128]{2,1,0:T(8,128)S(1)}, u32[]{:S(2)}, u32[]{:S(2)}) collective-permute-start(f32[3,32,128]{2,1,0:T(8,128)S(1)} %get-tuple-element.32), channel_id=1, source_target_pairs={{3,0},{2,1},{1,2},{0,3},{7,4},{6,5},{5,6},{4,7},{11,8},{10,9},{9,1... | collective-permute-start | bytes 147464 | tf_op jit(solution)/shard_map/ppermute | solution.py:522
  19.4 9.0 %collective-permute-start.12 = (f32[19,32,128]{2,1,0:T(8,128)S(1)}, f32[19,32,128]{2,1,0:T(8,128)S(1)}, u32[]{:S(2)}, u32[]{:S(2)}) collective-permute-start(f32[19,32,128]{2,1,0:T(8,128)S(1)} %get-tuple-element.52), channel_id=1, source_target_pairs={{1,0},{0,1},{3,2},{2,3},{5,4},{4,5},{7,6},{6,7},{9,8},{8,9},{11,10... | collective-permute-start | bytes 933896 | tf_op jit(solution)/shard_map/ppermute | solution.py:522
  20.2 3.0 %collective-permute-start.9 = (f32[1,8,128]{2,1,0:T(8,128)S(1)}, f32[1,8,128]{2,1,0:T(8,128)S(1)}, u32[]{:S(2)}, u32[]{:S(2)}) collective-permute-start(f32[1,8,128]{2,1,0:T(8,128)S(1)} %maximum_bitcast_fusion.refs_0_), channel_id=1, source_target_pairs={{0,5},{1,4},{4,1},{5,0},{8,13},{9,12},{12,9},{13,8},{2,7},{3,6},{6... | collective-permute-start | bytes 12296 | tf_op jit(solution)/shard_map/ppermute | solution.py:547
  21.5 6.9 %collective-permute-start.13 = (f32[13,32,128]{2,1,0:T(8,128)S(1)}, f32[13,32,128]{2,1,0:T(8,128)S(1)}, u32[]{:S(2)}, u32[]{:S(2)}) collective-permute-start(f32[13,32,128]{2,1,0:T(8,128)S(1)} %get-tuple-element.53), channel_id=1, source_target_pairs={{1,0},{0,1},{3,2},{2,3},{5,4},{4,5},{7,6},{6,7},{9,8},{8,9},{11,10... | collective-permute-start | bytes 638984 | tf_op jit(solution)/shard_map/ppermute | solution.py:522
  23.2 4.0 %collective-permute-start.10 = (f32[2,8,128]{2,1,0:T(8,128)S(1)}, f32[2,8,128]{2,1,0:T(8,128)S(1)}, u32[]{:S(2)}, u32[]{:S(2)}) collective-permute-start(f32[2,8,128]{2,1,0:T(8,128)S(1)} %pad_maximum_fusion.1), channel_id=1, source_target_pairs={{0,9},{1,8},{4,13},{5,12},{8,1},{9,0},{12,5},{13,4},{2,11},{3,10},... | collective-permute-start | bytes 24584 | tf_op jit(solution)/shard_map/ppermute | solution.py:547
  27.2 1.2 %collective-permute-start.11 = (f32[4,8,128]{2,1,0:T(8,128)S(1)}, f32[4,8,128]{2,1,0:T(8,128)S(1)}, u32[]{:S(2)}, u32[]{:S(2)}) collective-permute-start(f32[4,8,128]{2,1,0:T(8,128)S(1)} %pad_maximum_fusion), channel_id=1, source_target_pairs={{1,0},{0,1},{3,2},{2,3},{5,4},{4,5},{7,6},{6,7},{9,8},{8,9},{11,10... | collective-permute-start | bytes 49160 | tf_op jit(solution)/shard_map/ppermute | solution.py:522

commit v9 on v8

--- a/solution.py
+++ b/solution.py
@@ -121,7 +121,7 @@
         ],
         scratch_shapes=[
             VMEM((count, slots, width, width), F32),
-            pltpu.SemaphoreType.DMA((4,)),
+            pltpu.SemaphoreType.DMA((8,)),
         ],
         compiler_params=pltpu.CompilerParams(vmem_limit_bytes=ROOMY),
         cost_estimate=COST,

time: 30.3 us -> 30.3 us (level)
  no operation moved by 1% of the time
where the time goes in v9:
time: 30.3 us; the launch traced here: 30.1 us
  starting transfers between devices  14.8 us (49%)
  Pallas kernels  8.37 us (28%)
  waiting for transfers between devices  5.02 us (17%)
  local copies, waits for them, and re-layouts  1.12 us (4%)
  between operations  0.76 us (3%)
    ppermute x11, starting transfers between devices, from_group(): return lax.ppermute(value, ('season', 'var'), pairs)  10.6 us
    pallas_call x2, Pallas kernels, run_stage(): pl.pallas_call(kernel, in_specs=[pl.BlockSpec(memory_space=VMEM)] * len(o...  3.85 us
    ppermute x2, starting transfers between devices, gather_tiles(): found.append(lax.ppermute(have, ('space', 'var'), pairs))  3.58 us
    ppermute x2, waiting for transfers between devices, gather_tiles(): found.append(lax.ppermute(have, ('space', 'var'), pairs))  3.01 us
    pallas_call x1, Pallas kernels, prepare(): pl.pallas_call(functools.partial(prepare_kernel, blocks), in_specs=[pl.Bl...  2.05 us
    ppermute x11, waiting for transfers between devices, from_group(): return lax.ppermute(value, ('season', 'var'), pairs)  2.02 us
    pallas_call x1, Pallas kernels, finish(): pl.pallas_call(functools.partial(finish_kernel, plan, blocks, len(gathere...  1.69 us
    unnamed x6, local copies, waits for them, and re-layouts  1.05 us
  transfers between devices with their start and end apart: 14, of which 6 were waited for; matrix products, arithmetic and copies ran while one was open for 0% of the time, Pallas kernels for 16%

profile of v9, /device:TPU:0, one launch (start us, length us, event | category | flops | bytes accessed | tf_op | source)
XLA Modules:
  0.0 30.1 jit_solution(1812382754876417955)
XLA Ops:
  0.6 1.0 %copy-done = f32[32,1,4096]{2,1,0:T(1,128)S(1)} copy-done((f32[32,1,4096]{2,1,0:T(1,128)S(1)}, f32[32,1,4096]{2,1,0:T(1,128)}, u32[]{:S(2)}) %copy-start) | copy-done | bytes 524312
  1.7 0.3 %pack.1 = (f32[16,32,128]{2,1,0:T(8,128)S(1)}, f32[16,32,128]{2,1,0:T(8,128)S(1)}, f32[4,32,128]{2,1,0:T(8,128)S(1)}, f32[4,32,128]{2,1,0:T(8,128)S(1)}, f32[9,3...) custom-call(f32[1024,128]{1,0:T(8,128)S(1)} %bitcast.8), custom_call_target="tpu_custom_call" | custom-call | flops 1 | bytes 1 | tf_op jit(solution)/shard_map/pack/pallas_call | solution.py:69
  2.0 0.5 %collective-permute-start = (f32[16,32,128]{2,1,0:T(8,128)S(1)}, f32[16,32,128]{2,1,0:T(8,128)S(1)}, u32[]{:S(2)}, u32[]{:S(2)}) collective-permute-start(f32[16,32,128]{2,1,0:T(8,128)S(1)} %get-tuple-element.30.refs_5_), channel_id=1, source_target_pairs={{1,0},{0,1},{3,2},{2,3},{5,4},{4,5},{7,6},{6,7},{9,8},{8,9},{11,10... | collective-permute-start | bytes 786440 | tf_op jit(solution)/shard_map/ppermute | solution.py:522
  2.5 2.6 %collective-permute-start.3 = (f32[4,32,128]{2,1,0:T(8,128)S(1)}, f32[4,32,128]{2,1,0:T(8,128)S(1)}, u32[]{:S(2)}, u32[]{:S(2)}) collective-permute-start(f32[4,32,128]{2,1,0:T(8,128)S(1)} %get-tuple-element.37), channel_id=1, source_target_pairs={{2,0},{3,1},{0,2},{1,3},{6,4},{7,5},{4,6},{5,7},{10,8},{11,9},{8,1... | collective-permute-start | bytes 196616 | tf_op jit(solution)/shard_map/ppermute | solution.py:522
  5.1 0.1 collective-permute-start.4
  5.2 1.7 %collective-permute-start.5 = (f32[9,32,128]{2,1,0:T(8,128)S(1)}, f32[9,32,128]{2,1,0:T(8,128)S(1)}, u32[]{:S(2)}, u32[]{:S(2)}) collective-permute-start(f32[9,32,128]{2,1,0:T(8,128)S(1)} %get-tuple-element.39), channel_id=1, source_target_pairs={{2,0},{3,1},{0,2},{1,3},{6,4},{7,5},{4,6},{5,7},{10,8},{11,9},{8,1... | collective-permute-start | bytes 442376 | tf_op jit(solution)/shard_map/ppermute | solution.py:522
  6.9 2.0 %prepare.1 = (bf16[16,256,384]{2,1,0:T(8,128)(2,1)S(1)}, f32[8,128]{1,0:T(8,128)S(1)}) custom-call(f32[32,3,128,128]{3,2,1,0:T(8,128)} %w_ref.1), custom_call_target="tpu_custom_call" | custom-call | flops 1 | bytes 1 | tf_op jit(solution)/shard_map/prepare/pallas_call | solution.py:114
  9.0 0.0 collective-permute-done.3.refs_2_
  9.0 0.1 collective-permute-done.4.refs_3_
  9.2 0.1 broadcast_in_dim.12.count_ref.refs_9_.refs_7_
  9.2 0.3 edge.1
  9.5 0.6 %collective-permute-start.7 = (f32[272,128]{1,0:T(8,128)S(1)}, f32[272,128]{1,0:T(8,128)S(1)}, u32[]{:S(2)}, u32[]{:S(2)}) collective-permute-start(f32[272,128]{1,0:T(8,128)S(1)} %get-tuple-element.41), channel_id=1, source_target_pairs={{1,0},{0,1},{3,2},{2,3},{5,4},{4,5},{7,6},{6,7},{9,8},{8,9},{11,10... | collective-permute-start | bytes 417800 | tf_op jit(solution)/shard_map/ppermute | solution.py:522
  10.1 0.7 %collective-permute-start.8 = (f32[264,128]{1,0:T(8,128)S(1)}, f32[264,128]{1,0:T(8,128)S(1)}, u32[]{:S(2)}, u32[]{:S(2)}) collective-permute-start(f32[264,128]{1,0:T(8,128)S(1)} %get-tuple-element.47), channel_id=1, source_target_pairs={{1,4},{4,1},{5,8},{8,5},{9,12},{12,9},{3,6},{6,3},{7,10},{10,7},{1... | collective-permute-start | bytes 405512 | tf_op jit(solution)/shard_map/ppermute | solution.py:530
  10.7 1.6 %collective-permute-start.1 = (f32[3,32,128]{2,1,0:T(8,128)S(1)}, f32[3,32,128]{2,1,0:T(8,128)S(1)}, u32[]{:S(2)}, u32[]{:S(2)}) collective-permute-start(f32[3,32,128]{2,1,0:T(8,128)S(1)} %get-tuple-element.31), channel_id=1, source_target_pairs={{2,0},{3,1},{0,2},{1,3},{6,4},{7,5},{4,6},{5,7},{10,8},{11,9},{8,1... | collective-permute-start | bytes 147464 | tf_op jit(solution)/shard_map/ppermute | solution.py:522
  12.4 0.6 %collective-permute-done.5.refs_4_ = f32[9,32,128]{2,1,0:T(8,128)S(1)} collective-permute-done((f32[9,32,128]{2,1,0:T(8,128)S(1)}, f32[9,32,128]{2,1,0:T(8,128)S(1)}, u32[]{:S(2)}, u32[]{:S(2)}) %collective-permute-start.5) | collective-permute-done | bytes 147488 | tf_op jit(solution)/shard_map/ppermute | solution.py:522
  13.0 2.1 %collective-permute-start.2 = (f32[3,32,128]{2,1,0:T(8,128)S(1)}, f32[3,32,128]{2,1,0:T(8,128)S(1)}, u32[]{:S(2)}, u32[]{:S(2)}) collective-permute-start(f32[3,32,128]{2,1,0:T(8,128)S(1)} %get-tuple-element.32), channel_id=1, source_target_pairs={{3,0},{2,1},{1,2},{0,3},{7,4},{6,5},{5,6},{4,7},{11,8},{10,9},{9,1... | collective-permute-start | bytes 147464 | tf_op jit(solution)/shard_map/ppermute | solution.py:522
  15.1 0.2 mixer.1
  15.3 0.2 collective-permute-done.6.refs_5_
  15.5 2.3 %stage.2 = (f32[4,8,128]{2,1,0:T(8,128)S(1)}, f32[19,32,128]{2,1,0:T(8,128)S(1)}, f32[19,32,128]{2,1,0:T(8,128)S(1)}, bf16[4,128,128]{2,1,0:T(8,128)(2,1)S(1)}, ...) custom-call(f32[16,32,128]{2,1,0:T(8,128)S(1)} %get-tuple-element.29.refs_0_.ref, ...), custom_call_target="tpu_custom_call" | custom-call | flops 1 | bytes 1 | tf_op jit(solution)/shard_map/stage/pallas_call | solution.py:417
  17.8 0.0 collective-permute-done.1.refs_2_
  17.8 0.0 collective-permute-done.2.refs_3_
  17.8 1.6 %stage.3 = (f32[4,8,128]{2,1,0:T(8,128)S(1)}, f32[13,32,128]{2,1,0:T(8,128)S(1)}, f32[13,32,128]{2,1,0:T(8,128)S(1)}) custom-call(f32[16,32,128]{2,1,0:T(8,128)S(1)} %get-tuple-element.29.refs_0_.refs_4_, f32[16,32,128]{2,1,0:T(8,128)S(1)} %collective-permute-done.refs_1_, f32[3,32,128]{2,1,0:T(8,128)S(1)} %collective-permute-done.1.refs_2_, ...), custom_call_target="tpu_custom_call" | custom-call | flops 1 | bytes 1 | tf_op jit(solution)/shard_map/stage/pallas_call | solution.py:417
  19.4 0.8 %collective-permute-start.12 = (f32[19,32,128]{2,1,0:T(8,128)S(1)}, f32[19,32,128]{2,1,0:T(8,128)S(1)}, u32[]{:S(2)}, u32[]{:S(2)}) collective-permute-start(f32[19,32,128]{2,1,0:T(8,128)S(1)} %get-tuple-element.52), channel_id=1, source_target_pairs={{1,0},{0,1},{3,2},{2,3},{5,4},{4,5},{7,6},{6,7},{9,8},{8,9},{11,10... | collective-permute-start | bytes 933896 | tf_op jit(solution)/shard_map/ppermute | solution.py:522
  20.2 1.3 %collective-permute-start.9 = (f32[1,8,128]{2,1,0:T(8,128)S(1)}, f32[1,8,128]{2,1,0:T(8,128)S(1)}, u32[]{:S(2)}, u32[]{:S(2)}) collective-permute-start(f32[1,8,128]{2,1,0:T(8,128)S(1)} %maximum_bitcast_fusion.refs_0_), channel_id=1, source_target_pairs={{0,5},{1,4},{4,1},{5,0},{8,13},{9,12},{12,9},{13,8},{2,7},{3,6},{6... | collective-permute-start | bytes 12296 | tf_op jit(solution)/shard_map/ppermute | solution.py:547
  21.5 0.4 %collective-permute-start.13 = (f32[13,32,128]{2,1,0:T(8,128)S(1)}, f32[13,32,128]{2,1,0:T(8,128)S(1)}, u32[]{:S(2)}, u32[]{:S(2)}) collective-permute-start(f32[13,32,128]{2,1,0:T(8,128)S(1)} %get-tuple-element.53), channel_id=1, source_target_pairs={{1,0},{0,1},{3,2},{2,3},{5,4},{4,5},{7,6},{6,7},{9,8},{8,9},{11,10... | collective-permute-start | bytes 638984 | tf_op jit(solution)/shard_map/ppermute | solution.py:522
  21.9 1.3 %collective-permute-done.9.refs_1_ = f32[1,8,128]{2,1,0:T(8,128)S(1)} collective-permute-done((f32[1,8,128]{2,1,0:T(8,128)S(1)}, f32[1,8,128]{2,1,0:T(8,128)S(1)}, u32[]{:S(2)}, u32[]{:S(2)}) %collective-permute-start.9) | collective-permute-done | bytes 4128 | tf_op jit(solution)/shard_map/ppermute | solution.py:547
  23.2 2.3 %collective-permute-start.10 = (f32[2,8,128]{2,1,0:T(8,128)S(1)}, f32[2,8,128]{2,1,0:T(8,128)S(1)}, u32[]{:S(2)}, u32[]{:S(2)}) collective-permute-start(f32[2,8,128]{2,1,0:T(8,128)S(1)} %pad_maximum_fusion.1), channel_id=1, source_target_pairs={{0,9},{1,8},{4,13},{5,12},{8,1},{9,0},{12,5},{13,4},{2,11},{3,10},... | collective-permute-start | bytes 24584 | tf_op jit(solution)/shard_map/ppermute | solution.py:547
  25.5 1.7 %collective-permute-done.10.refs_2_ = f32[2,8,128]{2,1,0:T(8,128)S(1)} collective-permute-done((f32[2,8,128]{2,1,0:T(8,128)S(1)}, f32[2,8,128]{2,1,0:T(8,128)S(1)}, u32[]{:S(2)}, u32[]{:S(2)}) %collective-permute-start.10) | collective-permute-done | bytes 8224 | tf_op jit(solution)/shard_map/ppermute | solution.py:547
  27.2 0.1 collective-permute-start.11
  27.3 1.1 %collective-permute-done.11.refs_3_ = f32[4,8,128]{2,1,0:T(8,128)S(1)} collective-permute-done((f32[4,8,128]{2,1,0:T(8,128)S(1)}, f32[4,8,128]{2,1,0:T(8,128)S(1)}, u32[]{:S(2)}, u32[]{:S(2)}) %collective-permute-start.11) | collective-permute-done | bytes 16416 | tf_op jit(solution)/shard_map/ppermute | solution.py:522
  28.4 0.0 collective-permute-done.13.refs_9_
  28.4 1.7 %finish.1 = (f32[32,32,1,128]{3,2,1,0:T(1,128)}, f32[32,32,1,128]{3,2,1,0:T(1,128)}) custom-call(f32[1,8,128]{2,1,0:T(8,128)S(1)} %maximum_bitcast_fusion.refs_0_, f32[1,8,128]{2,1,0:T(8,128)S(1)} %collective-permute-done.9.refs_1_, f32[2,8,128]{2,1,0:T(8,128)S(1)} %collective-permute-done.10.refs_2_, f32[4,8,128]{2,1,0:T(8,128)S(1)} %collective-permute-done.11.refs_3_, ...), custom_call_target="tpu_custom_call" | custom-call | flops 1 | bytes 1 | tf_op jit(solution)/shard_map/finish/pallas_call | solution.py:502
  (17 shorter events, 0.1 us)
Async XLA Ops:
  0.6 8.3 %copy-start.2 = (s32[32]{0:T(128)S(1)}, s32[32]{0:T(128)}, u32[]{:S(2)}) copy-start(s32[32]{0:T(128)} %param.7) | copy-start | bytes 388
  0.6 1.0 %copy-start = (f32[32,1,4096]{2,1,0:T(1,128)S(1)}, f32[32,1,4096]{2,1,0:T(1,128)}, u32[]{:S(2)}) copy-start(f32[32,1,4096]{2,1,0:T(1,128)} %param.5) | copy-start | bytes 1572868
  1.7 13.4 %copy-start.1 = (f32[64,2,64,2]{2,3,1,0:T(2,128)S(1)}, f32[64,2,64,2]{2,3,1,0:T(2,128)}, u32[]{:S(2)}) copy-start(f32[64,2,64,2]{2,3,1,0:T(2,128)} %param.8) | copy-start | bytes 196612
  2.0 7.1 %collective-permute-start = (f32[16,32,128]{2,1,0:T(8,128)S(1)}, f32[16,32,128]{2,1,0:T(8,128)S(1)}, u32[]{:S(2)}, u32[]{:S(2)}) collective-permute-start(f32[16,32,128]{2,1,0:T(8,128)S(1)} %get-tuple-element.30.refs_5_), channel_id=1, source_target_pairs={{1,0},{0,1},{3,2},{2,3},{5,4},{4,5},{7,6},{6,7},{9,8},{8,9},{11,10... | collective-permute-start | bytes 786440 | tf_op jit(solution)/shard_map/ppermute | solution.py:522
  2.5 6.5 %collective-permute-start.3 = (f32[4,32,128]{2,1,0:T(8,128)S(1)}, f32[4,32,128]{2,1,0:T(8,128)S(1)}, u32[]{:S(2)}, u32[]{:S(2)}) collective-permute-start(f32[4,32,128]{2,1,0:T(8,128)S(1)} %get-tuple-element.37), channel_id=1, source_target_pairs={{2,0},{3,1},{0,2},{1,3},{6,4},{7,5},{4,6},{5,7},{10,8},{11,9},{8,1... | collective-permute-start | bytes 196616 | tf_op jit(solution)/shard_map/ppermute | solution.py:522
  5.1 4.0 %collective-permute-start.4 = (f32[4,32,128]{2,1,0:T(8,128)S(1)}, f32[4,32,128]{2,1,0:T(8,128)S(1)}, u32[]{:S(2)}, u32[]{:S(2)}) collective-permute-start(f32[4,32,128]{2,1,0:T(8,128)S(1)} %get-tuple-element.38), channel_id=1, source_target_pairs={{3,0},{2,1},{1,2},{0,3},{7,4},{6,5},{5,6},{4,7},{11,8},{10,9},{9,1... | collective-permute-start | bytes 196616 | tf_op jit(solution)/shard_map/ppermute | solution.py:522
  5.2 7.8 %collective-permute-start.5 = (f32[9,32,128]{2,1,0:T(8,128)S(1)}, f32[9,32,128]{2,1,0:T(8,128)S(1)}, u32[]{:S(2)}, u32[]{:S(2)}) collective-permute-start(f32[9,32,128]{2,1,0:T(8,128)S(1)} %get-tuple-element.39), channel_id=1, source_target_pairs={{2,0},{3,1},{0,2},{1,3},{6,4},{7,5},{4,6},{5,7},{10,8},{11,9},{8,1... | collective-permute-start | bytes 442376 | tf_op jit(solution)/shard_map/ppermute | solution.py:522
  6.9 8.6 %collective-permute-start.6 = (f32[9,32,128]{2,1,0:T(8,128)S(1)}, f32[9,32,128]{2,1,0:T(8,128)S(1)}, u32[]{:S(2)}, u32[]{:S(2)}) collective-permute-start(f32[9,32,128]{2,1,0:T(8,128)S(1)} %get-tuple-element.40), channel_id=1, source_target_pairs={{3,0},{2,1},{1,2},{0,3},{7,4},{6,5},{5,6},{4,7},{11,8},{10,9},{9,1... | collective-permute-start | bytes 442376 | tf_op jit(solution)/shard_map/ppermute | solution.py:522
  9.5 6.0 %collective-permute-start.7 = (f32[272,128]{1,0:T(8,128)S(1)}, f32[272,128]{1,0:T(8,128)S(1)}, u32[]{:S(2)}, u32[]{:S(2)}) collective-permute-start(f32[272,128]{1,0:T(8,128)S(1)} %get-tuple-element.41), channel_id=1, source_target_pairs={{1,0},{0,1},{3,2},{2,3},{5,4},{4,5},{7,6},{6,7},{9,8},{8,9},{11,10... | collective-permute-start | bytes 417800 | tf_op jit(solution)/shard_map/ppermute | solution.py:522
  10.1 7.7 %collective-permute-start.8 = (f32[264,128]{1,0:T(8,128)S(1)}, f32[264,128]{1,0:T(8,128)S(1)}, u32[]{:S(2)}, u32[]{:S(2)}) collective-permute-start(f32[264,128]{1,0:T(8,128)S(1)} %get-tuple-element.47), channel_id=1, source_target_pairs={{1,4},{4,1},{5,8},{8,5},{9,12},{12,9},{3,6},{6,3},{7,10},{10,7},{1... | collective-permute-start | bytes 405512 | tf_op jit(solution)/shard_map/ppermute | solution.py:530
  10.7 7.0 %collective-permute-start.1 = (f32[3,32,128]{2,1,0:T(8,128)S(1)}, f32[3,32,128]{2,1,0:T(8,128)S(1)}, u32[]{:S(2)}, u32[]{:S(2)}) collective-permute-start(f32[3,32,128]{2,1,0:T(8,128)S(1)} %get-tuple-element.31), channel_id=1, source_target_pairs={{2,0},{3,1},{0,2},{1,3},{6,4},{7,5},{4,6},{5,7},{10,8},{11,9},{8,1... | collective-permute-start | bytes 147464 | tf_op jit(solution)/shard_map/ppermute | solution.py:522
  13.0 4.8 %collective-permute-start.2 = (f32[3,32,128]{2,1,0:T(8,128)S(1)}, f32[3,32,128]{2,1,0:T(8,128)S(1)}, u32[]{:S(2)}, u32[]{:S(2)}) collective-permute-start(f32[3,32,128]{2,1,0:T(8,128)S(1)} %get-tuple-element.32), channel_id=1, source_target_pairs={{3,0},{2,1},{1,2},{0,3},{7,4},{6,5},{5,6},{4,7},{11,8},{10,9},{9,1... | collective-permute-start | bytes 147464 | tf_op jit(solution)/shard_map/ppermute | solution.py:522
  19.4 9.0 %collective-permute-start.12 = (f32[19,32,128]{2,1,0:T(8,128)S(1)}, f32[19,32,128]{2,1,0:T(8,128)S(1)}, u32[]{:S(2)}, u32[]{:S(2)}) collective-permute-start(f32[19,32,128]{2,1,0:T(8,128)S(1)} %get-tuple-element.52), channel_id=1, source_target_pairs={{1,0},{0,1},{3,2},{2,3},{5,4},{4,5},{7,6},{6,7},{9,8},{8,9},{11,10... | collective-permute-start | bytes 933896 | tf_op jit(solution)/shard_map/ppermute | solution.py:522
  20.2 3.0 %collective-permute-start.9 = (f32[1,8,128]{2,1,0:T(8,128)S(1)}, f32[1,8,128]{2,1,0:T(8,128)S(1)}, u32[]{:S(2)}, u32[]{:S(2)}) collective-permute-start(f32[1,8,128]{2,1,0:T(8,128)S(1)} %maximum_bitcast_fusion.refs_0_), channel_id=1, source_target_pairs={{0,5},{1,4},{4,1},{5,0},{8,13},{9,12},{12,9},{13,8},{2,7},{3,6},{6... | collective-permute-start | bytes 12296 | tf_op jit(solution)/shard_map/ppermute | solution.py:547
  21.5 6.9 %collective-permute-start.13 = (f32[13,32,128]{2,1,0:T(8,128)S(1)}, f32[13,32,128]{2,1,0:T(8,128)S(1)}, u32[]{:S(2)}, u32[]{:S(2)}) collective-permute-start(f32[13,32,128]{2,1,0:T(8,128)S(1)} %get-tuple-element.53), channel_id=1, source_target_pairs={{1,0},{0,1},{3,2},{2,3},{5,4},{4,5},{7,6},{6,7},{9,8},{8,9},{11,10... | collective-permute-start | bytes 638984 | tf_op jit(solution)/shard_map/ppermute | solution.py:522
  23.2 4.0 %collective-permute-start.10 = (f32[2,8,128]{2,1,0:T(8,128)S(1)}, f32[2,8,128]{2,1,0:T(8,128)S(1)}, u32[]{:S(2)}, u32[]{:S(2)}) collective-permute-start(f32[2,8,128]{2,1,0:T(8,128)S(1)} %pad_maximum_fusion.1), channel_id=1, source_target_pairs={{0,9},{1,8},{4,13},{5,12},{8,1},{9,0},{12,5},{13,4},{2,11},{3,10},... | collective-permute-start | bytes 24584 | tf_op jit(solution)/shard_map/ppermute | solution.py:547
  27.2 1.2 %collective-permute-start.11 = (f32[4,8,128]{2,1,0:T(8,128)S(1)}, f32[4,8,128]{2,1,0:T(8,128)S(1)}, u32[]{:S(2)}, u32[]{:S(2)}) collective-permute-start(f32[4,8,128]{2,1,0:T(8,128)S(1)} %pad_maximum_fusion), channel_id=1, source_target_pairs={{1,0},{0,1},{3,2},{2,3},{5,4},{4,5},{7,6},{6,7},{9,8},{8,9},{11,10... | collective-permute-start | bytes 49160 | tf_op jit(solution)/shard_map/ppermute | solution.py:522
